TPU v7x, 32 devices: a whole 2x2x4 slice. The times are simulated.
32 devices in a mesh: seq: 2 (over y), fsdp: 16 (over z, x, core).
Axes of the slice: x: 2, y: 2, z: 4, core: 2. Of those that a mesh axis runs over, the one named last changes fastest.
Arguments:
- tokens: bfloat16 [16, 1536, 896], P('fsdp', 'seq'), may hold values from -6 to 6
- seg_ids: int32 [16, 1536], P('fsdp', 'seq'), may hold values from 0 to 2, as said below
- first_gain: bfloat16 [896], P('fsdp'), may hold values from 0.5 to 1.5
- w_qkv: bfloat16 [896, 1152], P('fsdp'), may hold values from -0.1875 to 0.1875
- b_qkv: bfloat16 [1152], P('fsdp'), may hold values from -3 to 3
- w_out: bfloat16 [896, 896], P('fsdp'), may hold values from -1.5 to 1.5
- second_gain: bfloat16 [896], P('fsdp'), may hold values from 0.5 to 1.5
- w_gate: bfloat16 [896, 4864], P('fsdp'), may hold values from -0.1875 to 0.1875
- w_up: bfloat16 [896, 4864], P('fsdp'), may hold values from -0.1875 to 0.1875
- w_down: bfloat16 [4864, 896], P('fsdp'), may hold values from -0.078125 to 0.078125
- cotangent: bfloat16 [16, 1536, 896], P('fsdp', 'seq'), may hold values from -6 to 6
Outputs:
- output: bfloat16 [16, 1536, 896], P('fsdp', 'seq')
- grad_tokens: bfloat16 [16, 1536, 896], P('fsdp', 'seq')
- grad_first_gain: float32 [896], P('fsdp')
- grad_w_qkv: float32 [896, 1152], P('fsdp')
- grad_b_qk: float32 [1024], P('fsdp')
- grad_b_v: float32 [128], P('fsdp')
- grad_w_out: float32 [896, 896], P('fsdp')
- grad_second_gain: float32 [896], P('fsdp')
- grad_w_gate: float32 [896, 4864], P('fsdp')
- grad_w_up: float32 [896, 4864], P('fsdp')
- grad_w_down: float32 [4864, 896], P('fsdp')
Inputs may be any that keep to these rules, and one draw needn't show every extreme that they name: `seg_ids`: along each row the ids never fall; id 0 is a leading document, id 1 a document of at least three quarters of the row's 1536 tokens that covers both halves of the row, id 2 a trailing document; every id appears in every row.
All inputs are finite; a program needn't handle non-finite values.
Results may differ from a plain program's by a relative error of at most 0.017.
Values may be sent and summed in bfloat16 or wider, within the bound.
No kernel may reach another device: no remote copies, remote signals or barrier semaphores. Data moves between devices by JAX's collectives and lax.ppermute only.
A program may use at most 256 MiB of HBM per device.

v0:
```python
import functools

import jax
import jax.numpy as jnp
from jax import lax
from jax.experimental import pallas as pl
from jax.experimental.pallas import tpu as pltpu
from jax.sharding import PartitionSpec as P

HEAD = 64
LANES = 128
TILE = 256
EPSILON = 1e-06
THETA = 1000000.0
FAR = -1e30
MIB = 2**20
EARLY = 10
SHARED = 2

LIGHT = pl.CostEstimate(flops=1, bytes_accessed=1, transcendentals=0)
MIDDLE = pl.CostEstimate(flops=8 * 10**9, bytes_accessed=MIB, transcendentals=0)
SHORT = pl.CostEstimate(flops=28 * 10**8, bytes_accessed=MIB, transcendentals=0)
HEAVY = pl.CostEstimate(flops=6 * 10**10, bytes_accessed=16 * MIB, transcendentals=0)

bf16 = jnp.bfloat16
f32 = jnp.float32


def dot_nn(left, right):
    return lax.dot_general(left, right, (((1,), (0,)), ((), ())), preferred_element_type=f32)


def dot_nt(left, right):
    return lax.dot_general(left, right, (((1,), (1,)), ((), ())), preferred_element_type=f32)


def dot_tn(left, right):
    return lax.dot_general(left, right, (((0,), (0,)), ((), ())), preferred_element_type=f32)


def swap_halves(values_in):
    lane = lax.broadcasted_iota(jnp.int32, values_in.shape, 1)
    ahead = pltpu.roll(values_in, LANES - HEAD // 2, 1)
    behind = pltpu.roll(values_in, HEAD // 2, 1)
    return jnp.where(lane % HEAD < HEAD // 2, ahead, behind)


def turn(values_in, cosines, sines):
    return values_in * cosines + swap_halves(values_in) * sines


def turn_back(grads_in, cosines, sines):
    return grads_in * cosines - swap_halves(grads_in) * sines


def project_kernel(x_ref, gain_ref, w_ref, bias_ref, cos_ref, sin_ref, normed_ref, q_ref, kv_ref):
    x = x_ref[...].astype(f32)
    scale = lax.rsqrt(jnp.mean(x * x, axis=1, keepdims=True) + EPSILON)
    normed = (x * scale * gain_ref[...]).astype(bf16)
    normed_ref[...] = normed
    project = dot_nn(normed, w_ref[...]) + bias_ref[...]
    cosines, sines = cos_ref[...], sin_ref[...]
    width = q_ref.shape[1]
    for start in range(0, width, LANES):
        part = slice(start, start + LANES)
        q_ref[:, part] = turn(project[:, part], cosines, sines).astype(bf16) * (HEAD**-0.5)
    kv_ref[:, :LANES] = turn(project[:, width : width + LANES], cosines, sines).astype(bf16)
    kv_ref[:, LANES:] = project[:, width + LANES :].astype(bf16)


def project_call(x, gain, weight, bias, cosines, sines):
    tokens, width = x.shape
    outs = weight.shape[1]
    rows = tokens // 3
    row = lambda cols: pl.BlockSpec((rows, cols), lambda i: (i, 0))
    whole = lambda *shape: pl.BlockSpec(shape, lambda i: (0, 0))
    return pl.pallas_call(
        project_kernel,
        grid=(3,),
        in_specs=[
            row(width),
            whole(1, width),
            whole(width, outs),
            whole(1, outs),
            row(LANES),
            row(LANES),
        ],
        out_specs=[row(width), row(width), row(2 * LANES)],
        out_shape=[
            jax.ShapeDtypeStruct((tokens, width), bf16),
            jax.ShapeDtypeStruct((tokens, width), bf16),
            jax.ShapeDtypeStruct((tokens, 2 * LANES), bf16),
        ],
        compiler_params=pltpu.CompilerParams(vmem_limit_bytes=62 * MIB),
        cost_estimate=LIGHT,
        name="project",
    )(x, gain, weight, bias, cosines, sines)


def dropping(kernel, start, count):
    def inner(*refs, **settings):
        kernel(*refs[:start], *refs[start + count :], **settings)

    return inner


def spread(ref, columns, out_ref, turned_ref=None):
    both = ref[:, columns].astype(f32)
    shifted = pltpu.roll(both, HEAD, 1)
    low = lax.broadcasted_iota(jnp.int32, both.shape, 1) < HEAD
    for head in range(2):
        for parity in range(2):
            source = both if head == parity else shifted
            alone = jnp.where(low if parity == 0 else ~low, source, 0.0)
            out_ref[head, parity] = alone.astype(bf16)
            if turned_ref is not None:
                turned_ref[head, parity] = alone.T.astype(bf16)


def causal(scores, flipped):
    row_at = lax.broadcasted_iota(jnp.int32, scores.shape, 0)
    col_at = lax.broadcasted_iota(jnp.int32, scores.shape, 1)
    return jnp.where(row_at <= col_at if flipped else col_at <= row_at, scores, FAR)


def near_forward_kernel(q_ref, qx_ref, kv_ref, kx_ref, o_ref, lse_ref, k_s, v_s, *, group):
    step = pl.program_id(0)
    block = q_ref.shape[0] // 2
    lane = lax.broadcasted_iota(jnp.int32, (block, LANES), 1)

    @pl.when(step == 0)
    def _():
        spread(kv_ref, slice(0, LANES), k_s)
        spread(kv_ref, slice(LANES, 2 * LANES), v_s)
        lse_ref[...] = jnp.zeros_like(lse_ref)

    for b in range(2):
        rows = slice(b * block, (b + 1) * block)
        q = jnp.concatenate([q_ref[rows], qx_ref[rows]], axis=1)
        total = None
        stats = lse_ref[rows]
        for parity in range(2):
            kv = (2 * step + parity) // group
            k_at = lambda rows: jnp.concatenate([k_s[kv, parity, rows], kx_ref[rows]], axis=1)
            pieces = [(causal(dot_nt(q, k_at(rows)), False), v_s[kv, parity, rows])]
            if b:
                first = slice(0, block)
                pieces.append((dot_nt(q, k_at(first)), v_s[kv, parity, first]))
            top = functools.reduce(jnp.maximum, [jnp.max(s, axis=1, keepdims=True) for s, _ in pieces])
            weights = [(jnp.exp(s - top), v) for s, v in pieces]
            norm = sum(jnp.sum(p, axis=1, keepdims=True) for p, _ in weights)
            out = sum(dot_nn(p.astype(bf16), v) for p, v in weights) * (1.0 / norm)
            total = out if total is None else total + out
            stats = jnp.where(lane == 2 * step + parity, top + jnp.log(norm), stats)
        o_ref[rows] = total
        lse_ref[rows] = stats


def far_forward_kernel(half_ref, q_ref, qx_ref, kv_ref, kx_ref, near_ref, stats_ref, o_ref, lse_ref, k_s, v_s, lse_s, *, group):
    step = pl.program_id(0)
    tokens = q_ref.shape[0]
    block = tokens // 2

    @pl.when(step == 0)
    def _():
        spread(kv_ref, slice(0, LANES), k_s)
        spread(kv_ref, slice(LANES, 2 * LANES), v_s)
        lse_s[...] = stats_ref[...]

    def run(blocks, keys):
        for b in blocks:
            rows = slice(b * block, (b + 1) * block)
            q = jnp.concatenate([q_ref[rows], qx_ref[rows]], axis=1)
            lane = lax.broadcasted_iota(jnp.int32, (block, LANES), 1)
            stats = lse_s[rows]
            total = None
            scale = None
            for parity in range(2):
                head = 2 * step + parity
                kv = head // group
                k = jnp.concatenate([k_s[kv, parity, keys], kx_ref[keys]], axis=1)
                s = dot_nt(q, k)
                top = jnp.max(s, axis=1, keepdims=True)
                p = jnp.exp(s - top)
                norm = jnp.sum(p, axis=1, keepdims=True)
                far = top + jnp.log(norm)
                near = jnp.sum(jnp.where(lane == head, stats, 0.0), axis=1, keepdims=True)
                both = jnp.maximum(near, far)
                both = both + jnp.log(jnp.exp(near - both) + jnp.exp(far - both))
                out = dot_nn(p.astype(bf16), v_s[kv, parity, keys]) * jnp.exp(top - both)
                total = out if total is None else total + out
                weight = jnp.exp(near - both)
                scale = weight if scale is None else jnp.where(lane < HEAD, scale, weight)
                stats = jnp.where(lane == head, both, stats)
            o_ref[rows] = (near_ref[rows] * scale + total).astype(bf16)
            lse_s[rows] = stats

    @pl.when(half_ref[0] == 0)
    def _():
        first = slice(0, block)
        o_ref[first] = near_ref[first].astype(bf16)
        run((1,), slice(0, tokens))

    @pl.when(half_ref[0] != 0)
    def _():
        run((0, 1), slice(0, block))

    @pl.when(step == pl.num_programs(0) - 1)
    def _():
        lse_ref[...] = lse_s[...].T


def near_forward(q, qx, kv, kx, group):
    tokens, width = q.shape
    column = pl.BlockSpec((tokens, LANES), lambda p: (0, p))
    whole = lambda *shape: pl.BlockSpec(shape, lambda p: (0, 0))
    spare = lambda: pltpu.VMEM((2, 2, tokens, LANES), bf16)
    return pl.pallas_call(
        functools.partial(near_forward_kernel, group=group),
        grid=(width // LANES,),
        in_specs=[column, whole(tokens, LANES), whole(tokens, 2 * LANES), whole(tokens, LANES)],
        out_specs=[column, whole(tokens, LANES)],
        scratch_shapes=[spare(), spare()],
        out_shape=[
            jax.ShapeDtypeStruct((tokens, width), f32),
            jax.ShapeDtypeStruct((tokens, LANES), f32),
        ],
        compiler_params=pltpu.CompilerParams(vmem_limit_bytes=62 * MIB),
        cost_estimate=HEAVY,
        name="attention_near",
    )(q, qx, kv, kx)


def far_forward(half, q, qx, kv, kx, near, stats, group):
    tokens, width = q.shape
    column = pl.BlockSpec((tokens, LANES), lambda p, *_: (0, p))
    whole = lambda *shape: pl.BlockSpec(shape, lambda p, *_: (0, 0))
    spare = lambda: pltpu.VMEM((2, 2, tokens, LANES), bf16)
    return pl.pallas_call(
        functools.partial(far_forward_kernel, group=group),
        grid_spec=pltpu.PrefetchScalarGridSpec(
            num_scalar_prefetch=1,
            grid=(width // LANES,),
            in_specs=[
                column,
                whole(tokens, LANES),
                whole(tokens, 2 * LANES),
                whole(tokens, LANES),
                column,
                whole(tokens, LANES),
            ],
            out_specs=[column, whole(LANES, tokens)],
            scratch_shapes=[spare(), spare(), pltpu.VMEM((tokens, LANES), f32)],
        ),
        out_shape=[
            jax.ShapeDtypeStruct((tokens, width), bf16),
            jax.ShapeDtypeStruct((LANES, tokens), f32),
        ],
        compiler_params=pltpu.CompilerParams(vmem_limit_bytes=62 * MIB),
        cost_estimate=LIGHT,
        name="attention_far",
    )(half, q, qx, kv, kx, near, stats)


def back_block(q, q_wide, g, lse, delta, k, kx, turned, v, masked):
    s = dot_nt(jnp.concatenate([k, kx], axis=1), q_wide)
    if masked:
        s = causal(s, True)
    p = jnp.exp(s - lse)
    ds = (p * (dot_nt(v, g) - delta)).astype(bf16)
    return dot_nn(p.astype(bf16), g), dot_nn(ds, q), dot_nn(turned, ds)


def gather_heads(acc, out_ref, columns):
    low = lax.broadcasted_iota(jnp.int32, acc.shape[2:], 1) < HEAD
    first = acc[0, 0] + pltpu.roll(acc[0, 1], HEAD, 1)
    second = acc[1, 1] + pltpu.roll(acc[1, 0], HEAD, 1)
    out_ref[:, columns] = jnp.where(low, first, second).astype(out_ref.dtype)


def far_backward_kernel(half_ref, q_ref, qx_ref, g_ref, o_ref, lse_ref, kv_ref, kx_ref, dq_ref, dkv_ref, k_s, t_s, v_s, ka, va, *, group):
    step = pl.program_id(0)
    tokens = q_ref.shape[0]
    block = tokens // 2
    keys, values = slice(0, LANES), slice(LANES, 2 * LANES)

    @pl.when(step == 0)
    def _():
        spread(kv_ref, keys, k_s, t_s)
        spread(kv_ref, values, v_s)
        ka[...] = jnp.zeros_like(ka)
        va[...] = jnp.zeros_like(va)

    def run(blocks, key_blocks):
        for b in blocks:
            rows = slice(b * block, (b + 1) * block)
            q = q_ref[rows]
            q_wide = jnp.concatenate([q, qx_ref[rows]], axis=1)
            g = g_ref[rows]
            product = (g.astype(f32) * o_ref[rows].astype(f32)).T
            total = None
            for parity in range(2):
                head = 2 * step + parity
                kv = head // group
                lse = lse_ref[pl.ds(head, 1), rows]
                delta = jnp.sum(product[parity * HEAD : (parity + 1) * HEAD], axis=0, keepdims=True)
                for c in key_blocks:
                    part = slice(c * block, (c + 1) * block)
                    dv, dk, dq = back_block(
                        q, q_wide, g, lse, delta, k_s[kv, parity, part], kx_ref[part],
                        t_s[kv, parity, :, part], v_s[kv, parity, part], False,
                    )
                    va[kv, parity, part] += dv
                    ka[kv, parity, part] += dk
                    total = dq if total is None else total + dq
            dq_ref[:, rows] = total

    @pl.when(half_ref[0] == 0)
    def _():
        dq_ref[:, :block] = jnp.zeros((LANES, block), f32)
        run((1,), (0, 1))

    @pl.when(half_ref[0] != 0)
    def _():
        run((0, 1), (0,))

    @pl.when(step == pl.num_programs(0) - 1)
    def _():
        gather_heads(ka, dkv_ref, keys)
        gather_heads(va, dkv_ref, values)


def near_backward_kernel(q_ref, qx_ref, g_ref, o_ref, lse_ref, cos_ref, sin_ref, kv_ref, kx_ref, far_ref, dq_ref, dkv_ref, k_s, t_s, v_s, ka, va, *, group):
    step = pl.program_id(0)
    tokens = q_ref.shape[0]
    block = tokens // 2
    keys, values = slice(0, LANES), slice(LANES, 2 * LANES)

    @pl.when(step == 0)
    def _():
        spread(kv_ref, keys, k_s, t_s)
        spread(kv_ref, values, v_s)
        ka[...] = jnp.zeros_like(ka)
        va[...] = jnp.zeros_like(va)

    for b in range(2):
        rows = slice(b * block, (b + 1) * block)
        q = q_ref[rows]
        q_wide = jnp.concatenate([q, qx_ref[rows]], axis=1)
        g = g_ref[rows]
        product = (g.astype(f32) * o_ref[rows].astype(f32)).T
        total = far_ref[:, rows]
        for parity in range(2):
            head = 2 * step + parity
            kv = head // group
            lse = lse_ref[pl.ds(head, 1), rows]
            delta = jnp.sum(product[parity * HEAD : (parity + 1) * HEAD], axis=0, keepdims=True)
            for c in range(b + 1):
                part = slice(c * block, (c + 1) * block)
                dv, dk, dq = back_block(
                    q, q_wide, g, lse, delta, k_s[kv, parity, part], kx_ref[part],
                    t_s[kv, parity, :, part], v_s[kv, parity, part], c == b,
                )
                va[kv, parity, part] += dv
                ka[kv, parity, part] += dk
                total = total + dq
        dq_ref[rows] = turn_back(total.T * (HEAD**-0.5), cos_ref[rows], sin_ref[rows]).astype(bf16)

    @pl.when(step == pl.num_programs(0) - 1)
    def _():
        gather_heads(ka, dkv_ref, keys)
        gather_heads(va, dkv_ref, values)


ANYWHERE = pl.BlockSpec(memory_space=pl.ANY)


def alike(arrays):
    return [jax.ShapeDtypeStruct(array.shape, array.dtype) for array in arrays]


def backward_scratch(tokens):
    return [
        pltpu.VMEM((2, 2, tokens, LANES), bf16),
        pltpu.VMEM((2, 2, LANES, tokens), bf16),
        pltpu.VMEM((2, 2, tokens, LANES), bf16),
        pltpu.VMEM((2, 2, tokens, LANES), f32),
        pltpu.VMEM((2, 2, tokens, LANES), f32),
    ]


def far_backward(half, q, qx, g, o, lse, kv, kx, group, through):
    tokens, width = q.shape
    column = pl.BlockSpec((tokens, LANES), lambda p, *_: (0, p))
    across = pl.BlockSpec((LANES, tokens), lambda p, *_: (p, 0))
    whole = lambda *shape: pl.BlockSpec(shape, lambda p, *_: (0, 0))
    return pl.pallas_call(
        functools.partial(dropping(dropping(far_backward_kernel, 10, len(through)), 8, len(through)), group=group),
        grid_spec=pltpu.PrefetchScalarGridSpec(
            num_scalar_prefetch=1,
            grid=(width // LANES,),
            in_specs=[
                column,
                whole(tokens, LANES),
                column,
                column,
                whole(LANES, tokens),
                whole(tokens, 2 * LANES),
                whole(tokens, LANES),
            ]
            + [ANYWHERE] * len(through),
            out_specs=[across, whole(tokens, 2 * LANES)] + [ANYWHERE] * len(through),
            scratch_shapes=backward_scratch(tokens),
        ),
        out_shape=[
            jax.ShapeDtypeStruct((width, tokens), f32),
            jax.ShapeDtypeStruct((tokens, 2 * LANES), bf16),
            *alike(through),
        ],
        input_output_aliases={8 + i: 2 + i for i in range(len(through))},
        compiler_params=pltpu.CompilerParams(vmem_limit_bytes=62 * MIB),
        cost_estimate=LIGHT,
        name="attention_far_back",
    )(half, q, qx, g, o, lse, kv, kx, *through)


def near_backward(q, qx, g, o, lse, cosines, sines, kv, kx, far, group, others):
    tokens, width = q.shape
    column = pl.BlockSpec((tokens, LANES), lambda p: (0, p))
    across = pl.BlockSpec((LANES, tokens), lambda p: (p, 0))
    whole = lambda *shape: pl.BlockSpec(shape, lambda p: (0, 0))
    return pl.pallas_call(
        functools.partial(dropping(near_backward_kernel, 10, len(others)), group=group),
        grid=(width // LANES,),
        in_specs=[
            column,
            whole(tokens, LANES),
            column,
            column,
            whole(LANES, tokens),
            whole(tokens, LANES),
            whole(tokens, LANES),
            whole(tokens, 2 * LANES),
            whole(tokens, LANES),
            across,
        ]
        + [ANYWHERE] * len(others),
        out_specs=[column, whole(tokens, 2 * LANES)],
        scratch_shapes=backward_scratch(tokens),
        out_shape=[
            jax.ShapeDtypeStruct((tokens, width), bf16),
            jax.ShapeDtypeStruct((tokens, 2 * LANES), f32),
        ],
        compiler_params=pltpu.CompilerParams(vmem_limit_bytes=62 * MIB),
        cost_estimate=LIGHT,
        name="attention_near_back",
    )(q, qx, g, o, lse, cosines, sines, kv, kx, far, *others)


def weight_grads_kernel(at_ref, normed_ref, dq_ref, dkv_ref, got_ref, cos_ref, sin_ref, branch_ref, att_ref, project_ref, mine_ref, theirs_ref, bias_ref):
    kv = dkv_ref[...] + got_ref[...].astype(f32)
    keys = turn_back(kv[:, :LANES], cos_ref[...], sin_ref[...])
    project = jnp.concatenate([dq_ref[...], keys.astype(bf16), kv[:, LANES:].astype(bf16)], axis=1)
    project_ref[...] = project
    bias = jnp.sum(project.astype(f32), axis=0, keepdims=True)
    bias_ref[...] = bias
    core, inner, line, seq = (at_ref[i] for i in range(4))
    width = normed_ref.shape[1]
    chips = 8
    piece = width // chips // 2
    normed_t, att_t = normed_ref[...].T, att_ref[...].T
    columns = [(normed_t, project[:, s : s + LANES]) for s in range(0, project.shape[1], LANES)]
    columns += [(att_t, branch_ref[:, s : s + LANES]) for s in range(0, width, LANES)]
    for pair in range(len(columns) // 2):
        (left, one), (other, two) = columns[2 * pair : 2 * pair + 2]
        if left is other:
            value = dot_nn(left, jnp.concatenate([one, two], axis=1))
            one, two = value[:, :LANES], value[:, LANES:]
        else:
            one, two = dot_nn(left, one), dot_nn(other, two)
        quarter = pair // 2
        half = (quarter % 2) ^ seq
        start = quarter // 2 * (4 * piece + 16) + pair % 2 * 2 * piece
        for chip in range(chips):
            rows = slice(chip * 2 * piece, (chip + 1) * 2 * piece)
            here, there = one[rows], two[rows]
            low = jnp.concatenate([here[:piece], there[:piece]], axis=0)
            high = jnp.concatenate([here[piece:], there[piece:]], axis=0)
            away = (chip // 2) ^ line
            place = 2 * (away % 2) + away // 2
            for ref, first in ((mine_ref, core == 0), (theirs_ref, core != 0)):
                value = jnp.where(first, low, high).astype(bf16)
                ref[(chip % 2) ^ inner, half, place, start : start + 2 * piece, :] = value
    row = lax.broadcasted_iota(jnp.int32, (16, LANES), 0)
    last = bias[:, project.shape[1] - LANES :]
    for chip in range(chips):
        away = (chip // 2) ^ line
        place = 2 * (away % 2) + away // 2
        first = bias[:, chip * LANES : (chip + 1) * LANES]
        value = jnp.where(row == 0, first, jnp.where(row == 1, last, 0.0)).astype(bf16)
        for ref in (mine_ref, theirs_ref):
            for half in range(2):
                ref[(chip % 2) ^ inner, half, place, 4 * piece : 4 * piece + 16, :] = value
                ref[(chip % 2) ^ inner, half, place, 8 * piece + 16 :, :] = value


def weight_grads(at, normed, dq, dkv, got, cosines, sines, branch, attended, outs, others):
    tokens, width = normed.shape
    rows = (outs + width) // LANES * (width // 16) // 2 + 32
    packed = jax.ShapeDtypeStruct((2, 2, 4, rows, LANES), bf16)
    out_shape = [
        jax.ShapeDtypeStruct((tokens, outs), bf16),
        packed,
        packed,
        jax.ShapeDtypeStruct((1, outs), f32),
    ]
    args = (normed, dq, dkv, got, cosines, sines, branch, attended)
    whole = lambda array: pl.BlockSpec(array.shape, lambda i, *_: (0,) * len(array.shape))
    return pl.pallas_call(
        dropping(weight_grads_kernel, 9, len(others)),
        grid_spec=pltpu.PrefetchScalarGridSpec(
            num_scalar_prefetch=1,
            grid=(1,),
            in_specs=[whole(array) for array in args] + [ANYWHERE] * len(others),
            out_specs=[whole(array) for array in out_shape],
        ),
        out_shape=out_shape,
        compiler_params=pltpu.CompilerParams(vmem_limit_bytes=62 * MIB),
        cost_estimate=LIGHT,
        name="weight_grads",
    )(at, *args, *others)


def store_half(value, kept_ref, sent_ref):
    for step, ref in enumerate((kept_ref, sent_ref)):

        @pl.when(pl.program_id(0) == step)
        def _(ref=ref):
            ref[...] = value


def input_grad_kernel(at_ref, x_ref, gain_ref, project_ref, w_ref, gm_ref, kept_ref, sent_ref):
    grad = dot_nt(project_ref[...], w_ref[...]) * gain_ref[...]
    x = x_ref[...].astype(f32)
    scale = lax.rsqrt(jnp.mean(x * x, axis=1, keepdims=True) + EPSILON)
    normal = x * scale
    mean = jnp.mean(grad * normal, axis=1, keepdims=True)
    store_half((gm_ref[...] + scale * (grad - normal * mean)).astype(bf16), kept_ref, sent_ref)


def input_grad(half, x, gain, project, weight, grad_middle, others):
    tokens, width = x.shape
    outs = weight.shape[1]
    rows = tokens // 2
    row = lambda cols: pl.BlockSpec((rows, cols), lambda i, half: (i ^ half[0], 0))
    whole = lambda *shape: pl.BlockSpec(shape, lambda i, half: (0, 0))
    return pl.pallas_call(
        dropping(input_grad_kernel, 6, len(others)),
        grid_spec=pltpu.PrefetchScalarGridSpec(
            num_scalar_prefetch=1,
            grid=(2,),
            in_specs=[row(width), whole(1, width), row(outs), whole(width, outs), row(width)]
            + [ANYWHERE] * len(others),
            out_specs=[whole(rows, width)] * 2,
        ),
        out_shape=[jax.ShapeDtypeStruct((rows, width), bf16)] * 2,
        compiler_params=pltpu.CompilerParams(vmem_limit_bytes=62 * MIB),
        cost_estimate=LIGHT,
        name="input_grad",
    )(half, x, gain, project, weight, grad_middle, *others)


def out_project_kernel(x_ref, att_ref, gain_ref, w_ref, middle_ref, normed_ref, out_ref, raw_s, w_s, sem, *, start):
    step = pl.program_id(0)

    @pl.when(step == 0)
    def _():
        if start is None:
            w_s[...] = w_ref[...]
        else:
            copy = pltpu.make_async_copy(w_ref.at[:, pl.ds(start, raw_s.shape[1]), :], raw_s, sem)
            copy.start()
            copy.wait()
            width = w_s.shape[0]
            depth = width // raw_s.shape[0]
            for c in range(width // LANES):
                rows = raw_s[:, c * depth : (c + 1) * depth, :].astype(f32)
                w_s[:, c * LANES : (c + 1) * LANES] = rows.reshape(width, LANES).astype(bf16)
        out_ref[...] = w_s[...]

    middle = x_ref[...].astype(f32) + dot_nn(att_ref[...], w_s[...])
    middle_ref[...] = middle
    scale = lax.rsqrt(jnp.mean(middle * middle, axis=1, keepdims=True) + EPSILON)
    normed_ref[...] = (middle * scale * gain_ref[...]).astype(bf16)


def out_project(x, attended, gain, weight, start, rows):
    tokens, width = x.shape
    part = tokens // 3
    row = pl.BlockSpec((part, width), lambda i: (i, 0))
    whole = lambda *shape: pl.BlockSpec(shape, lambda i: (0, 0))
    raw = start is not None
    return pl.pallas_call(
        functools.partial(out_project_kernel, start=start),
        grid=(3,),
        in_specs=[
            row,
            row,
            whole(1, width),
            pl.BlockSpec(memory_space=pl.ANY) if raw else whole(width, width),
        ],
        out_specs=[row, row, whole(width, width)],
        out_shape=[
            jax.ShapeDtypeStruct((tokens, width), f32),
            jax.ShapeDtypeStruct((tokens, width), bf16),
            jax.ShapeDtypeStruct((width, width), bf16),
        ],
        scratch_shapes=[
            pltpu.VMEM((weight.shape[0], rows, LANES) if raw else (8, LANES), bf16),
            pltpu.VMEM((width, width), bf16),
            pltpu.SemaphoreType.DMA,
        ],
        compiler_params=pltpu.CompilerParams(vmem_limit_bytes=62 * MIB),
        cost_estimate=LIGHT,
        name="out_project",
    )(x, attended, gain, weight)


def middle_back_kernel(at_ref, o1_ref, o2_ref, o3_ref, o4_ref, g1_ref, g2_ref, g3_ref, g4_ref, middle_ref, gout_ref, gain_ref, w_ref, kept_ref, sent_ref, gm_ref, branch_ref, gatt_ref):
    middle = middle_ref[...]
    added = sum(ref[...].astype(f32) for ref in (o1_ref, o2_ref, o3_ref, o4_ref))
    store_half((middle + added).astype(bf16), kept_ref, sent_ref)
    grad = sum(ref[...].astype(f32) for ref in (g1_ref, g2_ref, g3_ref, g4_ref))
    grad = grad * gain_ref[...]
    scale = lax.rsqrt(jnp.mean(middle * middle, axis=1, keepdims=True) + EPSILON)
    normal = middle * scale
    mean = jnp.mean(grad * normal, axis=1, keepdims=True)
    grad = gout_ref[...].astype(f32) + scale * (grad - normal * mean)
    gm_ref[...] = grad
    branch = grad.astype(bf16)
    branch_ref[...] = branch
    gatt_ref[...] = dot_nt(branch, w_ref[...]).astype(bf16)


def middle_back(half, terms, middle, grad_out, gain, weight, others, through):
    tokens, width = middle.shape
    rows = tokens // 2
    row = pl.BlockSpec((rows, width), lambda i, half: (i ^ half[0], 0))
    below = pl.BlockSpec((rows, width), lambda i, half: (2 + (i ^ half[0]), 0))
    whole = lambda *shape: pl.BlockSpec(shape, lambda i, half: (0, 0))
    shape = lambda kind: jax.ShapeDtypeStruct((tokens, width), kind)
    return pl.pallas_call(
        dropping(dropping(middle_back_kernel, 18, len(through)), 13, len(others) + len(through)),
        grid_spec=pltpu.PrefetchScalarGridSpec(
            num_scalar_prefetch=1,
            grid=(2,),
            in_specs=[row] * 4
            + [below] * 4
            + [row, row, whole(1, width), whole(width, width)]
            + [ANYWHERE] * (len(others) + len(through)),
            out_specs=[whole(rows, width)] * 2 + [row] * 3 + [ANYWHERE] * len(through),
        ),
        out_shape=[jax.ShapeDtypeStruct((rows, width), bf16)] * 2 + [shape(f32), shape(bf16), shape(bf16)] + alike(through),
        input_output_aliases={13 + len(others) + i: 5 + i for i in range(len(through))},
        compiler_params=pltpu.CompilerParams(vmem_limit_bytes=62 * MIB),
        cost_estimate=LIGHT,
        name="middle_back",
    )(half, *terms, *terms, middle, grad_out, gain, weight, *others, *through)


LINE = (0, 2, 1, 3)


def mlp_kernel(at_ref, near_ref, far_ref, gnear_ref, gfar_ref, *rest, counts, tiles, first, split):
    w_refs, rest = rest[: len(counts)], rest[len(counts) :]
    own_ref, other_ref, keep_x, send_x, keep_y, send_y = rest[:6]
    n_s, t_s, g_s, p_s, out_s, grad_s, gate_s, up_s, down_s = rest[6:]
    step = pl.program_id(0)
    tile = 2 * (first + step) + at_ref[0]
    tokens, width = near_ref.shape
    shards = w_refs[0].shape[0]
    depth = width // shards
    own = TILE // shards
    chips = shards // 2

    @pl.when(step == 0)
    def _():
        n_s[:tokens] = near_ref[...]
        n_s[tokens:] = far_ref[...]
        g_s[:tokens] = gnear_ref[...]
        g_s[tokens:] = gfar_ref[...]
        t_s[:, :tokens] = near_ref[...].T
        t_s[:, tokens:] = far_ref[...].T
        out_s[...] = jnp.zeros_like(out_s)
        grad_s[...] = jnp.zeros_like(grad_s)

    def load(w_ref):
        for at, square in ((0, gate_s), (2 * depth, up_s)):
            for c in range(TILE // LANES):
                rows = w_ref[:, at + c * depth : at + (c + 1) * depth, :]
                rows = rows.astype(f32).reshape(width, LANES).astype(bf16)
                square[:, c * LANES : (c + 1) * LANES] = rows
        for c in range(width // LANES):
            rows = w_ref[:, 4 * depth + c * own : 4 * depth + (c + 1) * own, :]
            down_s[:, c * LANES : (c + 1) * LANES] = rows.reshape(TILE, LANES)

    begin = 0
    for w_ref, many in zip(w_refs, counts):
        pl.when((step >= begin) & (step < begin + many))(functools.partial(load, w_ref))
        begin += many

    @pl.when(tile >= tiles)
    def _():
        p_s[...] = jnp.zeros_like(p_s)

    @pl.when(tile < tiles)
    def _():
        gate_w, up_w, down_w = gate_s[...], up_s[...], down_s[...]
        n = n_s[...]
        g = g_s[...]
        gate = dot_nn(n, gate_w)
        up = dot_nn(n, up_w)
        grad_hidden = dot_nt(g, down_w)
        sig = 1.0 / (1.0 + jnp.exp(-gate))
        silu = gate * sig
        hidden = (silu * up).astype(bf16)
        grad_gate = (grad_hidden * up * (sig + silu * (1.0 - sig))).astype(bf16)
        grad_up = (grad_hidden * silu).astype(bf16)
        out_s[...] += dot_nn(hidden, down_w)
        grad_s[...] += dot_nt(grad_gate, gate_w) + dot_nt(grad_up, up_w)
        for at, value in ((0, dot_nn(t_s[...], grad_gate)), (1, dot_nn(t_s[...], grad_up))):
            for c in range(TILE // LANES):
                part = value[:, c * LANES : (c + 1) * LANES].astype(bf16)
                start = (2 * at + c) * 2 * depth
                p_s[:, start : start + 2 * depth, :] = part.reshape(chips, 2 * depth, LANES)
        down = dot_tn(hidden, g)
        for c in range(width // LANES):
            part = down[:, c * LANES : (c + 1) * LANES].astype(bf16)
            start = 8 * depth + c * 2 * own
            p_s[:, start : start + 2 * own, :] = part.reshape(chips, 2 * own, LANES)

    half_rows = 6 * depth
    inner, line, seq = at_ref[1], at_ref[2], at_ref[3]

    def piece(line_off, inner_off, half_off):
        chip = 2 * (line ^ line_off) + (inner ^ inner_off)
        start = pl.multiple_of((seq ^ half_off) * half_rows, half_rows)
        return p_s[chip, pl.ds(start, half_rows), :]

    @pl.when(step < split)
    def _():
        for a, off in enumerate(LINE):
            for h in range(2):
                keep_x[h, a] = piece(off, 0, h)
                send_x[h, a] = piece(off, 1, h)

    @pl.when(step >= split)
    def _():
        for a, off in enumerate(LINE):
            for b in range(2):
                keep_y[b, a] = piece(off, b, 0)
                send_y[b, a] = piece(off, b, 1)

    @pl.when(step == pl.num_programs(0) - 1)
    def _():
        for ref, rows in ((own_ref, slice(0, tokens)), (other_ref, slice(tokens, 2 * tokens))):
            ref[:tokens] = out_s[rows].astype(bf16)
            ref[tokens:] = grad_s[rows].astype(bf16)


def mlp_call(at, near, far, gnear, gfar, weights, counts, tiles, first, split):
    tokens, width = near.shape
    shards = weights[0][0].shape[0]
    rows = 6 * width // shards
    count = sum(counts)
    whole = lambda *shape: pl.BlockSpec(shape, lambda j, *_: (0,) * len(shape))
    early = pl.BlockSpec((2, 4, rows, LANES), lambda j, *_: (0, 0, jnp.minimum(j, split - 1), 0))
    late = pl.BlockSpec((2, 4, rows, LANES), lambda j, *_: (0, 0, jnp.maximum(j - split, 0), 0))
    shape_x = jax.ShapeDtypeStruct((2, 4, rows * split, LANES), bf16)
    shape_y = jax.ShapeDtypeStruct((2, 4, rows * (count - split), LANES), bf16)
    wide = jax.ShapeDtypeStruct((2 * tokens, width), bf16)

    def block_of(index):
        return pl.BlockSpec((shards, rows, LANES), lambda j, at: (0, index(j, at), 0))

    return pl.pallas_call(
        functools.partial(mlp_kernel, counts=counts, tiles=tiles, first=first, split=split),
        grid_spec=pltpu.PrefetchScalarGridSpec(
            num_scalar_prefetch=1,
            grid=(count,),
            in_specs=[whole(tokens, width)] * 4 + [block_of(index) for _, index in weights],
            out_specs=[whole(2 * tokens, width)] * 2 + [early, early, late, late],
            scratch_shapes=[
                pltpu.VMEM((2 * tokens, width), bf16),
                pltpu.VMEM((width, 2 * tokens), bf16),
                pltpu.VMEM((2 * tokens, width), bf16),
                pltpu.VMEM((shards // 2, 2 * rows, LANES), bf16),
                pltpu.VMEM((2 * tokens, width), f32),
                pltpu.VMEM((2 * tokens, width), f32),
                pltpu.VMEM((width, TILE), bf16),
                pltpu.VMEM((width, TILE), bf16),
                pltpu.VMEM((TILE, width), bf16),
            ],
        ),
        out_shape=[
            wide,
            wide,
            shape_x,
            shape_x,
            shape_y,
            shape_y,
        ],
        compiler_params=pltpu.CompilerParams(vmem_limit_bytes=62 * MIB),
        cost_estimate=HEAVY,
        name="feed_forward",
    )(at, near, far, gnear, gfar, *(w for w, _ in weights))


def pack_kernel(half_ref, gate_ref, up_ref, down_ref, out_ref, one_ref, two_ref, *, shards, early, shared):
    depth, hidden = gate_ref.shape
    width = down_ref.shape[1]
    tiles = hidden // TILE
    own = TILE // shards
    rows = 6 * depth
    per = LANES // own
    lane = lax.broadcasted_iota(jnp.int32, (depth, LANES), 1) // own

    def write(target, at, blocks, tile):
        target[at : at + 4 * depth, :] = blocks
        for c in range(width // LANES):
            start = at + 4 * depth + c * own
            target[start : start + own, :] = down_ref[tile * own : (tile + 1) * own, c * LANES : (c + 1) * LANES]

    for tile in range(tiles):
        blocks = []
        for ref in (gate_ref, up_ref):
            for c in range(TILE // LANES):
                total = None
                by_shift = {}
                for i in range(per):
                    at = ((c * per + i) * tiles + tile) * own
                    by_shift.setdefault((i - at // own) % per, []).append((i, at // LANES))
                for shift, sources in by_shift.items():
                    value = None
                    for i, block in sources:
                        part = ref[:, block * LANES : (block + 1) * LANES].astype(f32)
                        here = lane == (i - shift) % per
                        value = part if value is None else jnp.where(here, part, value)
                    if shift:
                        value = pltpu.roll(value, shift * own, 1)
                    if total is None:
                        total = value
                    else:
                        for i, _ in sources:
                            total = jnp.where(lane == i, value, total)
                blocks.append(total)
        blocks = jnp.concatenate(blocks, axis=0).astype(bf16)
        if tile < early:
            write(one_ref, tile * rows, blocks, tile)
        elif tile < early + 2 * shared:
            which, at = divmod(tile - early, shared)
            pl.when(half_ref[0] == which)(
                functools.partial(write, one_ref, (early + at) * rows, blocks, tile)
            )
        else:
            write(two_ref, (tile - early - 2 * shared) * rows, blocks, tile)
    pieces = [out_ref[:, c * LANES : (c + 1) * LANES].astype(f32) for c in range(width // LANES)]
    at = (early + shared) * rows
    rest = one_ref.shape[0] - at - len(pieces) * depth
    if rest:
        pieces.append(jnp.zeros((rest, LANES), f32))
    one_ref[at:, :] = jnp.concatenate(pieces, axis=0).astype(bf16)


def out_rows(width, depth):
    return -(-(width // LANES * depth) // 16) * 16


def pack_call(half, w_gate, w_up, w_down, w_out, shards, early, shared):
    depth, hidden = w_gate.shape
    width = w_down.shape[1]
    rows = 6 * depth
    tiles = hidden // TILE
    sizes = (early + shared) * rows + out_rows(width, depth), (tiles - early - 2 * shared) * rows
    whole = lambda shape: pl.BlockSpec(shape, lambda i, *_: (0, 0))
    return pl.pallas_call(
        functools.partial(pack_kernel, shards=shards, early=early, shared=shared),
        grid_spec=pltpu.PrefetchScalarGridSpec(
            num_scalar_prefetch=1,
            grid=(1,),
            in_specs=[whole(w.shape) for w in (w_gate, w_up, w_down, w_out)],
            out_specs=[whole((n, LANES)) for n in sizes],
        ),
        out_shape=[jax.ShapeDtypeStruct((n, LANES), bf16) for n in sizes],
        compiler_params=pltpu.CompilerParams(vmem_limit_bytes=62 * MIB),
        cost_estimate=LIGHT,
        name="pack",
    )(half, w_gate, w_up, w_down, w_out)


def unpack_kernel(at_ref, *refs, shards, cuts):
    chunks = [refs[:4], refs[4:8]]
    wg_ref, wu_ref, gate_ref, up_ref, down_ref, gain_ref, *scratch = refs[8:]
    depth, hidden = gate_ref.shape
    width = down_ref.shape[1]
    tiles = hidden // TILE
    own = TILE // shards
    per = LANES // own
    half_rows = 6 * depth
    core, seq = at_ref[0], at_ref[3]
    for (a, b, c, d), ref in zip(chunks, scratch):
        ref[core, seq] = a[...]
        ref[core, 1 - seq] = b[...]
        ref[1 - core, seq] = c[...]
        ref[1 - core, 1 - seq] = d[...]
    counts = [3 * sum(cut) // half_rows for cut in cuts]

    def rows_of(tile, half, start, size):
        at = tile // 2
        chunk = at >= counts[0]
        at -= counts[0] * chunk
        first, second = cuts[chunk]
        place = at * half_rows + start
        begin, cut = 0, first
        if place >= 3 * first:
            place, begin, cut = place - 3 * first, first, second

        def line_of(place):
            block, place = divmod(place, cut)
            return block * (first + second) + begin + place

        if size == depth:
            row = line_of(place)
            both = scratch[chunk][tile % 2, half, row : row + 2 * size, :].astype(f32)
            low, high = both[:size], both[size:]
        else:
            low, high = (
                scratch[chunk][tile % 2, half, row : row + size, :].astype(f32)
                for row in (line_of(place), line_of(place + size))
            )
        return jnp.where(core == 0, low, high)

    lane = lax.broadcasted_iota(jnp.int32, (depth, LANES), 1) // own
    wide = [[rows_of(tile, at // 3, at % 3 * 2 * depth, depth) for at in range(4)] for tile in range(tiles)]
    gain = jnp.zeros((depth, LANES), f32)
    for number, (ref, weight_ref) in enumerate(((gate_ref, wg_ref), (up_ref, wu_ref))):
        for block in range(hidden // LANES):
            total = None
            for i in range(per):
                shard, tile = divmod(block * per + i, tiles)
                c, at = divmod(shard, per)
                value = wide[tile][2 * number + c]
                if (i - at) % per:
                    value = pltpu.roll(value, (i - at) % per * own, 1)
                total = value if total is None else jnp.where(lane == i, value, total)
            columns = slice(block * LANES, (block + 1) * LANES)
            ref[:, columns] = total
            gain = gain + total * weight_ref[:, columns].astype(f32)
    gain_ref[...] = gain
    for tile in range(tiles):
        for c in range(width // LANES):
            value = rows_of(tile, 1, 2 * depth + c * 2 * own, own)
            down_ref[tile * own : (tile + 1) * own, c * LANES : (c + 1) * LANES] = value


def unpack_call(at, chunks, cuts, w_gate, w_up, shards):
    depth, hidden = w_gate.shape
    tiles = hidden // TILE
    own = TILE // shards
    width = depth * shards
    args = [piece for chunk in chunks for piece in chunk] + [w_gate, w_up]
    out_shape = [
        jax.ShapeDtypeStruct((depth, hidden), f32),
        jax.ShapeDtypeStruct((depth, hidden), f32),
        jax.ShapeDtypeStruct((tiles * own, width), f32),
        jax.ShapeDtypeStruct((depth, LANES), f32),
    ]
    whole = lambda array: pl.BlockSpec(array.shape, lambda i, *_: (0, 0))
    return pl.pallas_call(
        functools.partial(unpack_kernel, shards=shards, cuts=cuts),
        grid_spec=pltpu.PrefetchScalarGridSpec(
            num_scalar_prefetch=1,
            grid=(1,),
            in_specs=[whole(array) for array in args],
            out_specs=[whole(array) for array in out_shape],
            scratch_shapes=[pltpu.VMEM((2, 2, *chunk[0].shape), bf16) for chunk in chunks],
        ),
        out_shape=out_shape,
        compiler_params=pltpu.CompilerParams(vmem_limit_bytes=62 * MIB),
        cost_estimate=LIGHT,
        name="unpack",
    )(at, *args)


def pack_weights(w_gate, w_up, w_down, shards):
    depth, hidden = w_gate.shape
    tiles = hidden // TILE
    own = TILE // shards

    def columns(weight):
        parts = weight.reshape(depth, shards, tiles, own).transpose(0, 2, 1, 3)
        parts = parts.reshape(depth, tiles, TILE // LANES, LANES).transpose(1, 2, 0, 3)
        return parts.reshape(tiles, -1, LANES)

    width = w_down.shape[1]
    down = w_down.reshape(tiles, own, width // LANES, LANES).transpose(0, 2, 1, 3)
    return jnp.concatenate([columns(w_gate), columns(w_up), down.reshape(tiles, -1, LANES)], axis=1)


def unpack_grads(packed, shards, depth):
    tiles = packed.shape[0]
    own = TILE // shards

    def columns(part):
        part = part.reshape(tiles, TILE // LANES, depth, LANES).transpose(2, 0, 1, 3)
        part = part.reshape(depth, tiles, shards, own).transpose(0, 2, 1, 3)
        return part.reshape(depth, tiles * TILE)

    gate, up = columns(packed[:, : 2 * depth]), columns(packed[:, 2 * depth : 4 * depth])
    down = packed[:, 4 * depth :].reshape(tiles, -1, own, LANES).transpose(0, 2, 1, 3)
    return gate, up, down.reshape(tiles * own, -1)


def regroup_weights(gathered, groups, tiles, depth, own):
    shards = gathered.shape[0]
    if shards == groups:
        return gathered
    many = shards // groups
    gathered = gathered.reshape(groups, many, tiles, -1, LANES)
    outs = []
    for start, size in ((0, depth), (2 * depth, depth), (4 * depth, own)):
        stop = start + 2 * depth
        part = gathered[:, :, :, start:stop].reshape(groups, many, tiles, -1, size, LANES)
        outs.append(part.transpose(0, 2, 3, 1, 4, 5).reshape(groups, tiles, -1, LANES))
    return jnp.concatenate(outs, axis=2).reshape(groups, -1, LANES)


class Wires:
    def __init__(self, shards):
        self.shards = shards
        place = lax.axis_index("fsdp")
        self.core = place % 2
        self.inner = (place // 2) % 2
        self.line = place // 4
        self.seq = lax.axis_index("seq")

    def flip(self, values_in, bit):
        return lax.ppermute(values_in, "fsdp", [(i, i ^ bit) for i in range(self.shards)])

    def other_half(self, values_in):
        return lax.ppermute(values_in, "seq", [(0, 1), (1, 0)])


def ordered(bit, own, other):
    return jnp.where(bit == 0, own, other), jnp.where(bit == 0, other, own)


def gather_small(wires, shard, beside):
    if wires.shards != 16:
        return lax.all_gather(shard, "fsdp", axis=0, tiled=False)
    rows = shard.shape[0] // 2
    have = lax.dynamic_slice_in_dim(shard, wires.seq * rows, rows)[None]
    have = jnp.stack(ordered(wires.line // 2, have, wires.flip(have, 8)), axis=0)
    have = jnp.concatenate(ordered(wires.line % 2, have, wires.flip(have, 4)), axis=1)
    have = have.reshape(4, rows, -1)
    beside = beside(have)
    have = jnp.stack(ordered(wires.inner, have, after(wires.flip(have, 2), beside)), axis=1)
    have = jnp.concatenate(ordered(wires.seq, have, wires.other_half(have)), axis=2)
    have = jnp.stack(ordered(wires.core, have, wires.flip(have, 1)), axis=2)
    return have.reshape((16,) + shard.shape)


def pick(values_in, place, axis):
    return lax.dynamic_index_in_dim(values_in, place, axis, keepdims=False)


def plus(*terms):
    return sum(term.astype(f32) for term in terms).astype(bf16)


def after(values_in, others):
    return lax.optimization_barrier((values_in, others))[0]


def sums_kernel(*refs, plan):
    ins = iter(refs)
    for out_ref, parts in zip(refs[sum(map(sum, plan)) :], plan):
        start = 0
        for count in parts:
            total = sum(next(ins)[...].astype(f32) for _ in range(count)).astype(bf16)
            stop = start + total.shape[-2]
            out_ref[..., start:stop, :] = total
            start = stop


def sums(groups, grid=1, others=(), cost=LIGHT, through=()):
    args, in_specs, out_specs, out_shape, plan = [], [], [], [], []
    for parts in groups:
        below = 0
        for terms in parts:
            for array, block, place in terms:
                args.append(array)
                if grid == 1:
                    index = lambda i, place=place: place
                else:
                    index = lambda i, place=place: (*place[:-2], i, 0)
                in_specs.append(pl.BlockSpec(block, index))
            below += block[-2]
        lead = tuple(n for n in block[:-2] if n is not None)
        out_specs.append(pl.BlockSpec((*lead, below, LANES), lambda i, n=len(lead): (0,) * n + (i, 0)))
        out_shape.append(jax.ShapeDtypeStruct((*lead, below * grid, LANES), bf16))
        plan.append([len(terms) for terms in parts])
    return pl.pallas_call(
        dropping(functools.partial(sums_kernel, plan=plan), len(args), len(others) + len(through)),
        grid=(grid,),
        in_specs=in_specs + [ANYWHERE] * (len(others) + len(through)),
        out_specs=out_specs + [ANYWHERE] * len(through),
        out_shape=out_shape + alike(through),
        input_output_aliases={len(args) + len(others) + i: len(plan) + i for i in range(len(through))},
        compiler_params=pltpu.CompilerParams(vmem_limit_bytes=62 * MIB),
        cost_estimate=cost,
        name="sums",
    )(*args, *others, *through)


class ChipSum:
    def __init__(self, wires, keep_x, send_x, keep_y, send_y, grid):
        self.wires, self.grid = wires, grid
        self.kept = keep_x, keep_y
        self.got = wires.flip(send_x, 2), wires.other_half(send_y)

    def rows(self, array):
        return array.shape[-2] // self.grid

    def second(self):
        whole = lambda array: (array, (None, 4, self.rows(array), LANES), (1, 0, 0, 0))
        return [[[whole(k), whole(g)]] for k, g in zip(self.kept, self.got)]

    def second_sent(self, *sent):
        self.sent = sent
        self.next = self.wires.other_half(sent[0]), self.wires.flip(sent[1], 2)

    def third(self):
        groups = []
        for at in (1, 0):
            parts = []
            for k, g, n in zip(self.kept, self.got, self.next):
                old = (None, 2, self.rows(k), LANES), (0, at, 0, 0)
                parts.append([(k, *old), (g, *old), (n, old[0][1:], old[1][1:])])
            groups.append(parts)
        return groups

    def third_sent(self, sent, kept):
        self.sent, self.kept = (sent,), kept
        self.got = self.wires.flip(sent, 4)

    def fourth(self):
        block = (None, self.rows(self.kept), LANES)
        return [[[(self.kept, block, (1, 0, 0)), (self.got, block, (1, 0, 0))]]]

    def fourth_sent(self, sent):
        self.sent = (sent,)
        self.next = self.wires.flip(sent, 8)

    def fifth(self):
        block = (None, self.rows(self.kept), LANES)
        terms = [(self.kept, block, (0, 0, 0)), (self.got, block, (0, 0, 0)), (self.next, block[1:], (0, 0))]
        return [[terms]]

    def fifth_sent(self, sent):
        self.sent = (sent,)
        self.got = self.wires.other_half(sent)

    def total(self):
        return ordered(self.wires.seq, self.sent[0], self.got)


def quarters_in(wires, values_in):
    half = values_in.shape[0] // 2
    got = wires.other_half(values_in[half:])
    return jnp.concatenate(ordered(wires.seq, values_in[:half], got), axis=0)


def per_device(
    shards, tokens, seg_ids, first_gain, w_qkv, b_qkv, w_out, second_gain, w_gate, w_up, w_down, cotangent
):
    wires = Wires(shards)
    tokens = tokens[0]
    count, width = tokens.shape
    depth, qkv_width = w_qkv.shape
    kv_width = (qkv_width - width) // 2
    group = (width // HEAD) // (kv_width // HEAD)
    tiles = w_gate.shape[1] // TILE
    own = TILE // shards
    own_bias = b_qkv.shape[0]
    groups = 16
    chips = groups // 2
    full_depth = width // groups
    full_own = TILE // groups
    small_mesh = shards == groups
    half = wires.seq.astype(jnp.int32).reshape(1)
    if small_mesh:
        at = jnp.stack([wires.core, wires.inner, wires.line, wires.seq]).astype(jnp.int32)
    else:
        at = jnp.stack([wires.core] + [jnp.zeros_like(wires.core)] * 3).astype(jnp.int32)
    steps = -(-tiles // 2)
    early, shared = (EARLY, SHARED) if small_mesh else (2 * (steps // 2), 0)

    pad_rows = -(-(depth + 1) // 8) * 8 - depth
    vector = jnp.concatenate([first_gain, b_qkv, second_gain])
    vector = jnp.pad(vector, (0, qkv_width - vector.shape[0]))
    small = jnp.concatenate([w_qkv, jnp.pad(vector[None], ((0, pad_rows - 1), (0, 0)))], axis=0)
    other_segs = wires.other_half(seg_ids)
    tokens = quarters_in(wires, tokens)
    small, (w_gate, w_up, w_down, w_out) = lax.optimization_barrier((small, (w_gate, w_up, w_down, w_out)))
    out_packed = w_out.reshape(depth, width // LANES, LANES).transpose(1, 0, 2).reshape(-1, LANES)
    out_packed = jnp.pad(out_packed, ((0, out_rows(width, depth) - out_packed.shape[0]), (0, 0)))
    if small_mesh:
        packed_one, packed_two = pack_call(
            half, w_gate, w_up, w_down, w_out, shards, early, shared
        )
    else:
        packed = pack_weights(w_gate, w_up, w_down, shards)
        packed_one = jnp.concatenate([packed[:early].reshape(-1, LANES), out_packed], axis=0)
        packed_two = packed[early:].reshape(-1, LANES)
    all_one = lax.all_gather(packed_one, "fsdp", axis=0, tiled=False)
    packed_two = after(packed_two, packed_one)
    all_two = lax.all_gather(packed_two, "fsdp", axis=0, tiled=False)
    block = count // 2

    def tables(seg_ids, other_segs):
        less = lambda k: jnp.sum((seg_ids < k).astype(jnp.int32)) + jnp.sum((other_segs < k).astype(jnp.int32))
        ones, twos = less(1), less(2)
        own_segs = jnp.concatenate(ordered(wires.seq, seg_ids[0, :block], other_segs[0, block:]))
        far_segs = jnp.concatenate(ordered(wires.seq, seg_ids[0, block:], other_segs[0, :block]))
        index = jnp.arange(count, dtype=jnp.int32)
        index = index + jnp.where(wires.seq == 0, jnp.where(index < block, 0, 2 * block), block)
        local_pos = index - jnp.where(own_segs == 0, 0, jnp.where(own_segs == 1, ones, twos))
        inverse = THETA ** (-(jnp.arange(HEAD // 2, dtype=f32) * 2.0 / HEAD))
        angles = local_pos.astype(f32)[:, None] * inverse[None, :]
        cosines, sines = jnp.cos(angles), jnp.sin(angles)
        cosines = jnp.concatenate([cosines] * 4, axis=1)
        sines = jnp.concatenate([-sines, sines] * 2, axis=1)
        doc = jnp.arange(LANES, dtype=jnp.int32)[None, :]
        kx = (own_segs[:, None] == doc).astype(bf16)
        rkx = (far_segs[:, None] == doc).astype(bf16)
        qx = jnp.where((own_segs[:, None] == doc) | (doc >= 3), 0.0, FAR).astype(bf16)
        return cosines, sines, kx, rkx, qx

    made = []

    def beside(started):
        made.extend(tables(*after((seg_ids, other_segs), started)))
        made.append(after(tokens, started))
        return tuple(made)

    small_all = gather_small(wires, small, beside)
    if not made:
        beside(())
    cosines, sines, kx, rkx, qx, tokens = made
    qkv_full = small_all[:, :depth].reshape(width, qkv_width)
    vectors = small_all[:, depth]
    gain_one = vectors[:, :depth].reshape(1, width).astype(f32)
    bias = vectors[:, depth : depth + own_bias].reshape(1, qkv_width).astype(f32)
    gain_two = vectors[:, depth + own_bias : 2 * depth + own_bias].reshape(1, width).astype(f32)

    normed, queries, kv = project_call(tokens, gain_one, qkv_full, bias, cosines, sines)
    far_kv = wires.other_half(kv)
    cotangent = after(cotangent[0], small_all)
    got = wires.other_half(cotangent[block:])
    near, stats = near_forward(queries, qx, kv, kx, group)
    far_kv, got = after((far_kv, got), stats)
    grad_mlp = jnp.concatenate(ordered(wires.seq, cotangent[:block], got), axis=0)
    far_grad = wires.flip(grad_mlp, 1)
    attended, lse = far_forward(half, queries, qx, far_kv, rkx, near, after(stats, grad_mlp), group)
    far_grad = after(far_grad, lse)
    first_rows = all_one.shape[1] - out_packed.shape[0]
    if small_mesh:
        start, out_weight = first_rows, all_one
    else:
        out_weight = all_one[:, first_rows : first_rows + width // LANES * depth]
        out_weight = out_weight.reshape(shards, width // LANES, depth, LANES).transpose(0, 2, 1, 3)
        start, out_weight = None, out_weight.reshape(width, width)
    middle, normed_two, out_full = out_project(
        tokens, attended, gain_two, out_weight, start, out_packed.shape[0]
    )
    far_normed = wires.flip(normed_two, 1)

    if not small_mesh:
        all_one = regroup_weights(all_one[:, :first_rows], groups, early, depth, own)
        all_two = regroup_weights(all_two, groups, tiles - early, depth, own)
    rows = 6 * full_depth
    tokens_in = at, normed_two, far_normed, grad_mlp, far_grad
    own_tile = lambda start, last: lambda j, at: jnp.clip(2 * (j - start) + at[0], 0, last)
    one_steps = early // 2
    two_weights, two_counts = [(all_two, own_tile(shared, tiles - early - 2 * shared - 1))], [steps - one_steps - shared]
    if shared:
        mine = lax.dynamic_slice_in_dim(all_one, (early + wires.core) * rows, rows, axis=1)
        theirs = wires.other_half(mine)
    own_one, other_one, *grads_one = mlp_call(
        *tokens_in, [(all_one, own_tile(0, early - 1))], [one_steps], tiles, 0, one_steps // 2
    )
    if shared:
        both = jnp.concatenate(ordered(wires.seq, mine, after(theirs, own_one)), axis=1)
        two_weights.insert(0, (both, lambda j, at: jnp.minimum(j, shared - 1)))
        two_counts.insert(0, shared)
    if small_mesh:
        sum_one = ChipSum(wires, *grads_one, 3)
    back_one = wires.flip(other_one, 1)
    own_two, other_two, *grads_two = mlp_call(
        *tokens_in, two_weights, two_counts, tiles, one_steps, (steps - one_steps) // 2
    )
    back_two = wires.flip(other_two, 1)
    if small_mesh:
        sum_one.second_sent(*sums(sum_one.second(), 3, (own_two,), HEAVY))

    others = sum_one.sent if small_mesh else ()
    kept_result, sent_result, grad_middle, branch, grad_attended, *grads_two = middle_back(
        half, (own_one, own_two, back_one, back_two), middle, grad_mlp, gain_two, out_full, others, grads_two
    )
    if small_mesh:
        sum_two = ChipSum(wires, *grads_two, 3)
    far_query, far_kv_grad = far_backward(
        half, queries, qx, grad_attended, attended, lse, far_kv, rkx, group, ()
    )
    got_kv = wires.other_half(far_kv_grad)
    others = ()
    if small_mesh:
        sum_one.third_sent(*sums(sum_one.third(), 3, (far_query,), MIDDLE))
        others = sum_one.sent
    query_grad, kv_grad = near_backward(
        queries, qx, grad_attended, attended, lse, cosines, sines, kv, kx, far_query, group, others
    )
    others = ()
    if small_mesh:
        *sent_two, sent_one, sent_result = sums(
            sum_two.second() + sum_one.fourth(), 3, (query_grad, got_kv), through=(sent_result,)
        )
        sum_two.second_sent(*sent_two)
        sum_one.fourth_sent(sent_one)
        others = (*sum_two.sent, *sum_one.sent)
    got_result = wires.other_half(sent_result)
    project, mine, theirs, bias_grad = weight_grads(
        at, normed, query_grad, kv_grad, got_kv, cosines, sines, branch, attended, qkv_width, others
    )

    qk_own = (width + kv_width) // shards
    blocks = (qkv_width + width) // LANES
    cut = blocks // 4 * full_depth
    if small_mesh:
        theirs = wires.flip(theirs, 1)
        kept_grad, sent_grad = input_grad(half, tokens, gain_one, project, qkv_full, grad_middle, ())
        sent_two, kept_two, sent_one = sums(sum_two.third() + sum_one.fifth(), 3, (kept_grad,), HEAVY)
        sum_two.third_sent(sent_two, kept_two)
        sum_one.fifth_sent(sent_one)
        groups_of = []
        for axis in range(2):
            block = [2, 2, 4, cut + 16, LANES]
            block[axis] = None
            for part in (0, 1):
                place = [0, 0, 0, axis, 0]
                place[axis] = part
                groups_of.append([[(array, tuple(block), tuple(place)) for array in (mine, theirs)]])
        small = ChipSum(wires, *sums(groups_of, 1, sum_two.sent), 1)
        small.second_sent(*sums(small.second(), 1, (got_result,), SHORT))
        sent_two, sent_grad = sums(sum_two.fourth(), 3, small.sent, through=(sent_grad,))
        sum_two.fourth_sent(sent_two)
        small.third_sent(*sums(small.third(), 1, sum_two.sent, MIDDLE))
        got_grad = wires.other_half(sent_grad)
        small.fourth_sent(*sums(small.fourth(), 1))
        sent_two, sum_one.got, got_grad = sums(
            sum_two.fifth(), 3, small.sent, HEAVY, (sum_one.got, got_grad)
        )
        sum_two.fifth_sent(sent_two)
        small.fifth_sent(*sums(small.fifth(), 1, sum_two.sent))
        one, two = small.total()
        bias = one[2 * cut + 16 : 2 * cut + 18].astype(f32)
        bias_qk = lax.dynamic_slice_in_dim(bias[0], wires.core * qk_own, qk_own)
        bias_v = lax.dynamic_slice_in_dim(bias[1], lax.axis_index("fsdp") * (kv_width // shards), kv_width // shards)
        total = jnp.stack([one, two], axis=0).reshape(2, 2, cut + 16, LANES)[:, :, :cut]
        total = total.transpose(1, 0, 2, 3).reshape(blocks, depth, LANES)
    else:
        kept_grad, sent_grad = input_grad(half, tokens, gain_one, project, qkv_full, grad_middle, ())
        got_grad = wires.other_half(sent_grad)
        total = jnp.stack(ordered(wires.core, mine, theirs), axis=0)[:, :, :, jnp.array(LINE)]
        total = total.reshape(*total.shape[:4], 2, cut + 16, LANES)[:, :, :, :, :, :cut]
        total = total.reshape(2, 2, 2, 4, 2, blocks // 4, shards // groups, depth, LANES)
        total = total.transpose(3, 1, 0, 6, 4, 2, 5, 7, 8).reshape(shards, -1, LANES)
        total = lax.psum_scatter(total.astype(f32), "fsdp", scatter_dimension=0, tiled=True)[0]
        total = lax.psum(total.astype(bf16), "seq").reshape(blocks, depth, LANES)
        bias = lax.psum(bias_grad[0], ("seq", "fsdp"))
        place = lax.axis_index("fsdp")
        bias_qk = lax.dynamic_slice_in_dim(bias, place * qk_own, qk_own)
        bias_v = lax.dynamic_slice_in_dim(
            bias, width + kv_width + place * (kv_width // shards), kv_width // shards
        )
    result = jnp.concatenate([kept_result, got_result], axis=0)
    grad_input = jnp.concatenate([kept_grad, got_grad], axis=0)
    total = total.transpose(1, 0, 2).reshape(depth, -1).astype(f32)
    gain_one_grad = jnp.sum(total[:, :qkv_width] * w_qkv.astype(f32), axis=1) / first_gain.astype(f32)

    half_rows = 6 * full_depth
    if small_mesh:
        chunks, cuts = [], []
        for chip_sum, (first, _, second, _) in ((sum_one, grads_one), (sum_two, grads_two)):
            pair = chip_sum.sent[0], chip_sum.got
            chunks.append((*pair, *(wires.flip(piece, 1) for piece in pair)))
            cuts.append((first.shape[2] // 3, second.shape[2] // 3))
        gate_grad, up_grad, down_grad, gain_two_grad = unpack_call(at, chunks, cuts, w_gate, w_up, shards)
        gain_two_grad = jnp.sum(gain_two_grad, axis=1) / second_gain.astype(f32)
    else:
        many = shards // groups
        terms = []
        for keep_x, send_x, keep_y, send_y in (grads_one, grads_two):
            first = jnp.stack([keep_x, send_x], axis=0).reshape(2, 2, 4, -1, half_rows, LANES)
            second = jnp.stack([keep_y, send_y], axis=0).reshape(2, 2, 4, -1, half_rows, LANES)
            places = jnp.array(LINE)
            first = first.transpose(2, 0, 3, 1, 4, 5)[places].reshape(chips, -1, 2, half_rows, LANES)
            second = second.transpose(2, 1, 3, 0, 4, 5)[places].reshape(chips, -1, 2, half_rows, LANES)
            terms += [first, second]
        terms = jnp.concatenate(terms, axis=1).reshape(chips, steps, 2 * half_rows, LANES)
        parts = []
        for start, size in ((0, depth), (4 * full_depth, depth), (8 * full_depth, own)):
            part = terms[:, :, start : start + 4 * full_depth]
            part = part.reshape(chips, steps, -1, 2 * many, size, LANES)
            parts.append(part.transpose(0, 3, 1, 2, 4, 5).reshape(shards, steps, -1, LANES))
        terms = jnp.concatenate(parts, axis=2).astype(f32)
        terms = lax.dynamic_update_index_in_dim(jnp.zeros((2,) + terms.shape, f32), terms, wires.core, 0)
        terms = lax.psum_scatter(terms, "fsdp", scatter_dimension=1, tiled=True)[:, 0]
        terms = lax.psum(terms.astype(bf16), "seq")
        mlp_grads = terms.transpose(1, 0, 2, 3).reshape(2 * steps, -1, LANES)[:tiles]
        gate_grad, up_grad, down_grad = unpack_grads(mlp_grads, shards, depth)
        both = gate_grad.astype(f32) * w_gate.astype(f32) + up_grad.astype(f32) * w_up.astype(f32)
        gain_two_grad = jnp.sum(both, axis=1) / second_gain.astype(f32)
    return (
        result[None],
        grad_input[None],
        gain_one_grad,
        total[:, :qkv_width],
        bias_qk,
        bias_v,
        total[:, qkv_width:],
        gain_two_grad,
        gate_grad.astype(f32),
        up_grad.astype(f32),
        down_grad.astype(f32),
    )


def solution(mesh):
    rows, split, lone = P("fsdp", "seq", None), P("fsdp", None), P("fsdp")
    in_specs = (rows, P("fsdp", "seq"), lone, split, lone, split, lone, split, split, split, rows)
    out_specs = (rows, rows, lone, split, lone, lone, split, lone, split, split, split)
    return jax.shard_map(
        functools.partial(per_device, mesh.shape["fsdp"]),
        mesh=mesh,
        in_specs=in_specs,
        out_specs=out_specs,
        check_vma=False,
    )
```

profile of v0, /device:TPU:0, one launch (start us, length us, event | category | flops | bytes accessed | tf_op | source)
XLA Modules:
  0.0 435.3 jit_solution(7531194567608734832)
XLA Ops:
  9.0 4.4 %pack.1 = (bf16[4432,128]{1,0:T(8,128)(2,1)}, bf16[1680,128]{1,0:T(8,128)(2,1)}) custom-call(s32[1]{0:T(128)} %bitcast.half_ref.refs_0_, bf16[56,4864]{1,0:T(8,128)(2,1)} %refs_8_, bf16[56,4864]{1,0:T(8,128)(2,1)} %refs_9_, bf16[304,896]{1,0:T(8,128)(2,1)} %down_ref, bf16[56,896]{1,0:T(8,128)(2,1)} %out_ref), custom_call_target="tpu_custom_call" | custom-call | flops 1 | bytes 1 | tf_op jit(solution)/shard_map/pack/pallas_call | solution.py:886
  13.5 4.1 collective-permute-start.1
  17.6 1.5 collective-permute-start.4
  22.3 7.4 %collective-permute-done.2 = bf16[2,1,32,1152]{3,2,1,0:T(8,128)(2,1)S(1)} collective-permute-done((bf16[2,1,32,1152]{3,2,1,0:T(8,128)(2,1)S(1)}, bf16[2,1,32,1152]{3,2,1,0:T(8,128)(2,1)S(1)}, u32[]{:S(2)}, u32[]{:S(2)}) %collective-permute-start.2) | collective-permute-done | bytes 147488 | tf_op jit(solution)/shard_map/ppermute | solution.py:1048
  29.8 1.6 collective-permute-start.3
  34.7 1.4 fusion.6
  43.4 1.5 collective-permute-done.3
  45.1 1.4 collective-permute-start.5
  46.4 10.8 %collective-permute-done.5 = bf16[4,2,32,1152]{3,2,0,1:T(8,128)(2,1)S(1)} collective-permute-done((bf16[4,2,32,1152]{3,2,0,1:T(8,128)(2,1)S(1)}, bf16[4,2,32,1152]{3,2,0,1:T(8,128)(2,1)S(1)}, u32[]{:S(2)}, u32[]{:S(2)}) %collective-permute-start.5) | collective-permute-done | bytes 589856 | tf_op jit(solution)/shard_map/ppermute | solution.py:1051
  57.6 2.8 collective-permute-done.6
  61.4 1.5 slice.87
  64.4 6.8 %project.1 = (bf16[768,896]{1,0:T(8,128)(2,1)}, bf16[768,896]{1,0:T(8,128)(2,1)}, bf16[768,256]{1,0:T(8,128)(2,1)}) custom-call(bf16[768,896]{1,0:T(8,128)(2,1)} %pad_maximum_fusion.2.x_ref.refs_1_, f32[1,896]{1,0:T(1,128)} %reshape.163.gain_ref.refs_2_, bf16[896,1152]{1,0:T(8,128)(2,1)} %bitcast.63, f32[1,1152]{1,0:T(1,128)} %reshape.164.bias_ref, ...), custom_call_target="tpu_custom_call" | custom-call | flops 1 | bytes 1 | tf_op jit(solution)/shard_map/project/pallas_call | solution.py:77
  72.6 1.6 collective-permute-start.8
  74.1 16.9 %attention_near.1 = (f32[768,896]{1,0:T(8,128)}, f32[768,128]{1,0:T(8,128)}) custom-call(bf16[768,896]{1,0:T(8,128)(2,1)} %get-tuple-element.102.q_ref.refs_1_.refs_0_, bf16[768,128]{1,0:T(8,128)(2,1)} %select_convert_fusion.qx_ref.refs_2_.refs_1_, bf16[768,256]{1,0:T(8,128)(2,1)} %get-tuple-element.103.kv_ref.refs_7_, bf16[768,128]{1,0:T(8,128)(2,1)} %fusion.1.kx_ref.refs_8_), custom_call_target="tpu_custom_call" | custom-call | flops 60000002048 | bytes 16777216 | tf_op jit(solution)/shard_map/attention_near/pallas_call | solution.py:218
  91.0 6.4 %collective-permute-done.8 = bf16[384,896]{1,0:T(8,128)(2,1)} collective-permute-done((bf16[384,896]{1,0:T(8,128)(2,1)}, bf16[384,896]{1,0:T(8,128)(2,1)}, u32[]{:S(2)}, u32[]{:S(2)}) %collective-permute-start.8) | collective-permute-done | bytes 688160 | tf_op jit(solution)/shard_map/ppermute | solution.py:1051
  99.7 12.9 %attention_far.1 = (bf16[768,896]{1,0:T(8,128)(2,1)}, f32[128,768]{1,0:T(8,128)}) custom-call(s32[1]{0:T(128)} %bitcast.half_ref.refs_0_, bf16[768,896]{1,0:T(8,128)(2,1)} %get-tuple-element.102.q_ref.refs_1_.refs_0_, bf16[768,128]{1,0:T(8,128)(2,1)} %select_convert_fusion.qx_ref.refs_2_.refs_1_, bf16[768,256]{1,0:T(8,128)(2,1)} %copy-done.3, ...), custom_call_target="tpu_custom_call" | custom-call | flops 1 | bytes 1 | tf_op jit(solution)/shard_map/attention_far/pallas_call | solution.py:239
  112.5 5.4 %all-gather.5.cloned.1.call-done = bf16[70912,128]{1,0:T(8,128)(2,1)} async-done(((bf16[4432,128]{1,0:T(8,128)(2,1)}), bf16[70912,128]{1,0:T(8,128)(2,1)}) %all-gather.5.cloned.1.call-update) | async-done | bytes 18153488 | tf_op jit(solution)/shard_map/all_gather | solution.py:1226
  117.9 7.7 %out_project.1 = (f32[768,896]{1,0:T(8,128)}, bf16[768,896]{1,0:T(8,128)(2,1)}, bf16[896,896]{1,0:T(8,128)(2,1)}) custom-call(bf16[768,896]{1,0:T(8,128)(2,1)} %pad_maximum_fusion.2.x_ref.refs_1_, bf16[768,896]{1,0:T(8,128)(2,1)} %get-tuple-element.110.att_ref.refs_4_.refs_3_.refs_8_, f32[1,896]{1,0:T(1,128)} %reshape.165.gain_ref.refs_11_, ...), custom_call_target="tpu_custom_call" | custom-call | flops 1 | bytes 1 | tf_op jit(solution)/shard_map/out_project/pallas_call | solution.py:603
  126.6 2.6 constant_dynamic-slice_fusion.2
  129.2 1.5 collective-permute-start.11
  130.6 50.2 %feed_forward.2 = (bf16[1536,896]{1,0:T(8,128)(2,1)}, bf16[1536,896]{1,0:T(8,128)(2,1)}, bf16[2,4,672,128]{3,2,1,0:T(8,128)(2,1)}, bf16[2,4,672,128]{3,2,1,0:T(8...) custom-call(s32[4]{0:T(128)} %pad_add_fusion.2.at_ref.refs_0_, ...), custom_call_target="tpu_custom_call" | custom-call | flops 60000002048 | bytes 16777216 | tf_op jit(solution)/shard_map/feed_forward/pallas_call | solution.py:786
  181.9 1.9 broadcast_select_fusion.1
  183.8 1.8 pad_maximum_fusion.rest_0_
  186.3 50.4 %feed_forward.3 = (bf16[1536,896]{1,0:T(8,128)(2,1)}, bf16[1536,896]{1,0:T(8,128)(2,1)}, bf16[2,4,672,128]{3,2,1,0:T(8,128)(2,1)}, bf16[2,4,672,128]{3,2,1,0:T(8...) custom-call(s32[4]{0:T(128)} %pad_add_fusion.2.at_ref.refs_0_, ...), custom_call_target="tpu_custom_call" | custom-call | flops 60000002048 | bytes 16777216 | tf_op jit(solution)/shard_map/feed_forward/pallas_call | solution.py:786
  237.2 4.1 sums.11
  242.1 1.5 collective-permute-start.18
  243.6 2.4 collective-permute-done.12.refs_3_.refs_7_
  246.0 10.1 %middle_back.1 = (bf16[384,896]{1,0:T(8,128)(2,1)}, bf16[384,896]{1,0:T(8,128)(2,1)}, f32[768,896]{1,0:T(8,128)}, bf16[768,896]{1,0:T(8,128)(2,1)}, bf16[768,896...) custom-call(s32[1]{0:T(128)} %bitcast.half_ref.refs_0_, ...), custom_call_target="tpu_custom_call", output_to_operand_aliasing={{5}: (15, {}), {6}: (16, {}), {7}: (17, {}), {8}: (18, {})} | custom-call | flops 1 | bytes 1 | tf_op jit(solution)/shard_map/middle_back/pallas_call | solution.py:652
  256.1 1.5 collective-permute-start.17
  257.6 17.2 %attention_far_back.1 = (f32[896,768]{1,0:T(8,128)}, bf16[768,256]{1,0:T(8,128)(2,1)}) custom-call(s32[1]{0:T(128)} %bitcast.half_ref.refs_0_, bf16[768,896]{1,0:T(8,128)(2,1)} %get-tuple-element.102.q_ref.refs_1_.refs_0_, bf16[768,128]{1,0:T(8,128)(2,1)} %select_convert_fusion.qx_ref.refs_2_.refs_1_, bf16[768,896]{1,0:T(8,128)(2,1)} %get-tuple-element.143.refs_3_.refs_2_, ...), custom_call_target="tpu_custom_call" | custom-call | flops 1 | bytes 1 | tf_op jit(solution)/shard_map/attention_far_back/pallas_call | solution.py:397
  275.7 4.7 %sums.12 = (bf16[2,1680,128]{2,1,0:T(8,128)(2,1)}, bf16[2,1680,128]{2,1,0:T(8,128)(2,1)}) custom-call(bf16[2,4,672,128]{3,2,1,0:T(8,128)(2,1)} %get-tuple-element.128.refs_0_.refs_6_, bf16[2,4,672,128]{3,2,1,0:T(8,128)(2,1)} %collective-permute-done.14.refs_1_.refs_7_, bf16[4,672,128]{2,1,0:T(8,128)(2,1)} %collective-permute-done.18.refs_2_.refs_8_, ...), custom_call_target="tpu_custom_call" | custom-call | flops 8000000000 | bytes 1048576 | tf_op jit(solution)/shard_map/sums/pallas_call | solution.py:1113
  282.6 25.3 %attention_near_back.1 = (bf16[768,896]{1,0:T(8,128)(2,1)}, f32[768,256]{1,0:T(8,128)}) custom-call(bf16[768,896]{1,0:T(8,128)(2,1)} %get-tuple-element.102.q_ref.refs_1_.refs_0_, bf16[768,128]{1,0:T(8,128)(2,1)} %select_convert_fusion.qx_ref.refs_2_.refs_1_, bf16[768,896]{1,0:T(8,128)(2,1)} %get-tuple-element.143.refs_3_.refs_2_, ...), custom_call_target="tpu_custom_call" | custom-call | flops 1 | bytes 1 | tf_op jit(solution)/shard_map/attention_near_back/pallas_call | solution.py:432
  307.9 4.2 collective-permute-done.21.refs_7_.refs_4_
  312.8 4.7 %sums.13 = (bf16[4,672,128]{2,1,0:T(8,128)(2,1)}, bf16[4,1008,128]{2,1,0:T(8,128)(2,1)}, bf16[1680,128]{1,0:T(8,128)(2,1)}, bf16[384,896]{1,0:T(8,128)(2,1)}) custom-call(bf16[2,4,672,128]{3,2,1,0:T(8,128)(2,1)} %get-tuple-element.139.refs_0_.refs_6_, ...), custom_call_target="tpu_custom_call", output_to_operand_aliasing={{3}: (8, {})} | custom-call | flops 1 | bytes 1 | tf_op jit(solution)/shard_map/sums/pallas_call | solution.py:1113
  317.6 1.2 collective-permute-start.24
  318.8 1.5 collective-permute-start.23
  320.3 1.8 collective-permute-start.25
  322.1 9.4 %weight_grads.1 = (bf16[768,1152]{1,0:T(8,128)(2,1)}, bf16[2,2,4,480,128]{4,3,2,1,0:T(8,128)(2,1)}, bf16[2,2,4,480,128]{4,3,2,1,0:T(8,128)(2,1)}, f32[1,1152]{1,0:T(1,128)}) custom-call(s32[4]{0:T(128)} %pad_add_fusion.2.at_ref.refs_0_, bf16[768,896]{1,0:T(8,128)(2,1)} %get-tuple-element.151.refs_1_, bf16[768,896]{1,0:T(8,128)(2,1)} %get-tuple-element.147.refs_6_.refs_2_, ...), custom_call_target="tpu_custom_call" | custom-call | flops 1 | bytes 1 | tf_op jit(solution)/shard_map/weight_grads/pallas_call | solution.py:519
  332.1 7.0 %input_grad.1 = (bf16[384,896]{1,0:T(8,128)(2,1)}, bf16[384,896]{1,0:T(8,128)(2,1)}) custom-call(s32[1]{0:T(128)} %bitcast.half_ref.refs_0_, bf16[768,896]{1,0:T(8,128)(2,1)} %pad_maximum_fusion.2.x_ref.refs_1_, f32[1,896]{1,0:T(1,128)} %reshape.163.gain_ref.refs_2_, bf16[768,1152]{1,0:T(8,128)(2,1)} %get-tuple-element.157.refs_3_, ...), custom_call_target="tpu_custom_call" | custom-call | flops 1 | bytes 1 | tf_op jit(solution)/shard_map/input_grad/pallas_call | solution.py:557
  339.1 2.2 collective-permute-done.25.refs_14_
  342.2 5.2 %sums.14 = (bf16[2,1680,128]{2,1,0:T(8,128)(2,1)}, bf16[2,1680,128]{2,1,0:T(8,128)(2,1)}, bf16[1680,128]{1,0:T(8,128)(2,1)}) custom-call(bf16[2,4,672,128]{3,2,1,0:T(8,128)(2,1)} %get-tuple-element.139.refs_0_.refs_6_, bf16[2,4,672,128]{3,2,1,0:T(8,128)(2,1)} %collective-permute-done.16.refs_1_.refs_7_, ...), custom_call_target="tpu_custom_call" | custom-call | flops 60000002048 | bytes 16777216 | tf_op jit(solution)/shard_map/sums/pallas_call | solution.py:1113
  347.4 1.3 copy-done
  348.6 3.4 sums.15
  353.2 1.5 collective-permute-start.29
  355.7 8.4 %collective-permute-done.28.refs_1_.refs_7_ = bf16[2,4,240,128]{3,2,1,0:T(8,128)(2,1)S(1)} collective-permute-done((bf16[2,4,240,128]{3,2,1,0:T(8,128)(2,1)}, bf16[2,4,240,128]{3,2,1,0:T(8,128)(2,1)S(1)}, u32[]{:S(2)}, u32[]{:S(2)}) %collective-permute-start.28) | collective-permute-done | bytes 491552 | tf_op jit(solution)/shard_map/ppermute | solution.py:1048
  365.6 2.2 sums.16
  367.7 1.4 collective-permute-start.31
  369.2 1.5 collective-permute-start.32
  371.0 3.5 collective-permute-done.26.refs_1_
  375.4 2.8 sums.17
  378.5 3.1 collective-permute-start.30
  382.3 2.3 sums.18
  384.7 1.7 collective-permute-start.33
  386.4 2.3 maximum_bitcast_fusion
  388.7 4.7 %collective-permute-done.33.refs_1_ = bf16[2,480,128]{2,1,0:T(8,128)(2,1)S(1)} collective-permute-done((bf16[2,480,128]{2,1,0:T(8,128)(2,1)}, bf16[2,480,128]{2,1,0:T(8,128)(2,1)S(1)}, u32[]{:S(2)}, u32[]{:S(2)}) %collective-permute-start.33) | collective-permute-done | bytes 245792 | tf_op jit(solution)/shard_map/ppermute | solution.py:1048
  394.1 1.6 sums.19.refs_3_
  395.7 3.2 collective-permute-start.36
  399.0 1.5 collective-permute-done.30.refs_2_
  401.3 3.0 sums.20
  404.3 1.7 collective-permute-start.40
  406.5 1.7 sums.21
  408.6 2.3 maximum_bitcast_fusion.1
  410.9 4.4 %collective-permute-done.37 = bf16[480,128]{1,0:T(8,128)(2,1)S(1)} collective-permute-done((bf16[480,128]{1,0:T(8,128)(2,1)}, bf16[480,128]{1,0:T(8,128)(2,1)S(1)}, u32[]{:S(2)}, u32[]{:S(2)}) %collective-permute-start.37) | collective-permute-done | bytes 122912 | tf_op jit(solution)/shard_map/ppermute | solution.py:1051
  420.5 6.1 %unpack.1 = (f32[56,4864]{1,0:T(8,128)}, f32[56,4864]{1,0:T(8,128)}, f32[304,896]{1,0:T(8,128)}, f32[56,128]{1,0:T(8,128)}) custom-call(s32[4]{0:T(128)} %pad_add_fusion.2.at_ref.refs_0_, bf16[1680,128]{1,0:T(8,128)(2,1)} %get-tuple-element.174.refs_0_, bf16[1680,128]{1,0:T(8,128)(2,1)} %get-tuple-element.178.refs_1_, ...), custom_call_target="tpu_custom_call" | custom-call | flops 1 | bytes 1 | tf_op jit(solution)/shard_map/unpack/pallas_call | solution.py:979
  (159 shorter events, 43.6 us)
Async XLA Ops:
  7.2 110.8 %all-gather.5.cloned.1.call-start = ((), (), s32[]{:S(2)}) async-start(), calls=%async_computation | async-start | bytes 19288064 | tf_op jit(solution)/shard_map/all_gather | solution.py:1226
  8.9 8.7 %copy-start.18 = (s32[1,768]{1,0:T(1,128)S(1)}, s32[1,768]{1,0:T(1,128)}, u32[]{:S(2)}) copy-start(s32[1,768]{1,0:T(1,128)} %param.12) | copy-start | bytes 9220
  8.9 10.2 %copy-start.5 = (bf16[1,768,896]{2,1,0:T(8,128)(2,1)S(1)}, bf16[1,768,896]{2,1,0:T(8,128)(2,1)}, u32[]{:S(2)}) copy-start(bf16[1,768,896]{2,1,0:T(8,128)(2,1)} %param.11) | copy-start | bytes 4128772
  13.4 172.9 %all-gather.7.cloned.1.call-start = ((), (), s32[]{:S(2)}) async-start(), calls=%async_computation.1 | async-start | bytes 7311360 | tf_op jit(solution)/shard_map/all_gather | solution.py:1228
  13.5 8.0 %collective-permute-start.1 = (bf16[1,32,1152]{2,1,0:T(8,128)(2,1)S(1)}, bf16[1,32,1152]{2,1,0:T(8,128)(2,1)S(1)}, u32[]{:S(2)}, u32[]{:S(2)}) collective-permute-start(bf16[1,32,1152]{2,1,0:T(8,128)(2,1)S(1)} %dynamic-slice_bitcast_fusion), channel_id=1, source_target_pairs={{0,8},{1,9},{2,10},{3,11},{4,12},{5,13},{6,14},{7,15},{8,0},{9,1},... | collective-permute-start | bytes 221192 | tf_op jit(solution)/shard_map/ppermute | solution.py:1048
  17.6 13.8 %collective-permute-start.4 = (s32[1,768]{1,0:T(1,128)S(1)}, s32[1,768]{1,0:T(1,128)S(1)}, u32[]{:S(2)}, u32[]{:S(2)}) collective-permute-start(s32[1,768]{1,0:T(1,128)S(1)} %copy-done.18), channel_id=1, source_target_pairs={{0,16},{16,0},{1,17},{17,1},{2,18},{18,2},{3,19},{19,3},{4,20},{20... | collective-permute-start | bytes 9224 | tf_op jit(solution)/shard_map/ppermute | solution.py:1051
  20.0 21.0 %collective-permute-start = (bf16[384,896]{1,0:T(8,128)(2,1)}, bf16[384,896]{1,0:T(8,128)(2,1)}, u32[]{:S(2)}, u32[]{:S(2)}) collective-permute-start(bf16[384,896]{1,0:T(8,128)(2,1)} %slice_bitcast_fusion), channel_id=1, source_target_pairs={{0,16},{16,0},{1,17},{17,1},{2,18},{18,2},{3,19},{19,3},{4,20},{20... | collective-permute-start | bytes 2064392 | tf_op jit(solution)/shard_map/ppermute | solution.py:1051
  21.6 8.2 %collective-permute-start.2 = (bf16[2,1,32,1152]{3,2,1,0:T(8,128)(2,1)S(1)}, bf16[2,1,32,1152]{3,2,1,0:T(8,128)(2,1)S(1)}, u32[]{:S(2)}, u32[]{:S(2)}) collective-permute-start(bf16[2,1,32,1152]{3,2,1,0:T(8,128)(2,1)S(1)} %pad_maximum_fusion.10), channel_id=1, source_target_pairs={{0,4},{1,5},{2,6},{3,7},{4,0},{5,1},{6,2},{7,3},{8,12},{9,13},{10,... | collective-permute-start | bytes 442376 | tf_op jit(solution)/shard_map/ppermute | solution.py:1048
  29.8 15.1 %collective-permute-start.3 = (bf16[4,32,1152]{2,1,0:T(8,128)(2,1)S(1)}, bf16[4,32,1152]{2,1,0:T(8,128)(2,1)S(1)}, u32[]{:S(2)}, u32[]{:S(2)}) collective-permute-start(bf16[4,32,1152]{2,1,0:T(8,128)(2,1)S(1)} %bitcast.72), channel_id=1, source_target_pairs={{0,2},{1,3},{2,0},{3,1},{4,6},{5,7},{6,4},{7,5},{8,10},{9,11},{10,... | collective-permute-start | bytes 884744 | tf_op jit(solution)/shard_map/ppermute | solution.py:1048
  45.1 12.1 %collective-permute-start.5 = (bf16[4,2,32,1152]{3,2,0,1:T(8,128)(2,1)S(1)}, bf16[4,2,32,1152]{3,2,0,1:T(8,128)(2,1)S(1)}, u32[]{:S(2)}, u32[]{:S(2)}) collective-permute-start(bf16[4,2,32,1152]{3,2,0,1:T(8,128)(2,1)S(1)} %pad_maximum_fusion.5), channel_id=1, source_target_pairs={{0,16},{16,0},{1,17},{17,1},{2,18},{18,2},{3,19},{19,3},{4,20},{20... | collective-permute-start | bytes 1769480 | tf_op jit(solution)/shard_map/ppermute | solution.py:1051
  57.5 2.9 collective-permute-start.6
  64.4 7.3 %copy-start.6 = (bf16[1,768,896]{2,1,0:T(8,128)(2,1)S(1)}, bf16[1,768,896]{2,1,0:T(8,128)(2,1)}, u32[]{:S(2)}) copy-start(bf16[1,768,896]{2,1,0:T(8,128)(2,1)} %param.21) | copy-start | bytes 4128772
  71.2 19.8 %collective-permute-start.7 = (bf16[768,256]{1,0:T(8,128)(2,1)}, bf16[768,256]{1,0:T(8,128)(2,1)S(1)}, u32[]{:S(2)}, u32[]{:S(2)}) collective-permute-start(bf16[768,256]{1,0:T(8,128)(2,1)} %get-tuple-element.103.kv_ref.refs_7_), channel_id=1, source_target_pairs={{0,16},{16,0},{1,17},{17,1},{2,18},{18,2},{3,19},{19,3},{4,20},{20... | collective-permute-start | bytes 1179656 | tf_op jit(solution)/shard_map/ppermute | solution.py:1051
  72.6 24.8 %collective-permute-start.8 = (bf16[384,896]{1,0:T(8,128)(2,1)}, bf16[384,896]{1,0:T(8,128)(2,1)}, u32[]{:S(2)}, u32[]{:S(2)}) collective-permute-start(bf16[384,896]{1,0:T(8,128)(2,1)} %slice.76), channel_id=1, source_target_pairs={{0,16},{16,0},{1,17},{17,1},{2,18},{18,2},{3,19},{19,3},{4,20},{20... | collective-permute-start | bytes 2064392 | tf_op jit(solution)/shard_map/ppermute | solution.py:1051
  91.0 7.6 %copy-start.3 = (bf16[768,256]{1,0:T(8,128)(2,1)}, bf16[768,256]{1,0:T(8,128)(2,1)S(1)}, u32[]{:S(2)}) copy-start(bf16[768,256]{1,0:T(8,128)(2,1)S(1)} %collective-permute-done.7.kv_ref.refs_6_) | copy-start | bytes 1179652
  98.7 13.8 %copy-start.1 = (bf16[768,896]{1,0:T(8,128)(2,1)}, bf16[768,896]{1,0:T(8,128)(2,1)S(1)}, u32[]{:S(2)}) copy-start(bf16[768,896]{1,0:T(8,128)(2,1)S(1)} %pad_maximum_fusion.3.gnear_ref.refs_10_) | copy-start | bytes 4128772
  98.8 27.8 %collective-permute-start.10 = (bf16[768,896]{1,0:T(8,128)(2,1)S(1)}, bf16[768,896]{1,0:T(8,128)(2,1)}, u32[]{:S(2)}, u32[]{:S(2)}) collective-permute-start(bf16[768,896]{1,0:T(8,128)(2,1)S(1)} %pad_maximum_fusion.3.gnear_ref.refs_10_), channel_id=1, source_target_pairs={{0,1},{1,0},{2,3},{3,2},{4,5},{5,4},{6,7},{7,6},{8,9},{9,8},{10,11... | collective-permute-start | bytes 4128776 | tf_op jit(solution)/shard_map/ppermute | solution.py:1048
  125.7 4.9 %collective-permute-start.9 = (bf16[768,896]{1,0:T(8,128)(2,1)}, bf16[768,896]{1,0:T(8,128)(2,1)}, u32[]{:S(2)}, u32[]{:S(2)}) collective-permute-start(bf16[768,896]{1,0:T(8,128)(2,1)} %get-tuple-element.116.near_ref), channel_id=1, source_target_pairs={{0,1},{1,0},{2,3},{3,2},{4,5},{5,4},{6,7},{7,6},{8,9},{9,8},{10,11... | collective-permute-start | bytes 4128776 | tf_op jit(solution)/shard_map/ppermute | solution.py:1048
  129.2 51.7 %collective-permute-start.11 = (bf16[16,336,128]{2,1,0:T(8,128)(2,1)}, bf16[16,336,128]{2,1,0:T(8,128)(2,1)S(1)}, u32[]{:S(2)}, u32[]{:S(2)}) collective-permute-start(bf16[16,336,128]{2,1,0:T(8,128)(2,1)} %constant_dynamic-slice_fusion.2), channel_id=1, source_target_pairs={{0,16},{16,0},{1,17},{17,1},{2,18},{18,2},{3,19},{19,3},{4,20},{20... | collective-permute-start | bytes 4128776 | tf_op jit(solution)/shard_map/ppermute | solution.py:1051
  180.9 56.3 %collective-permute-start.15 = (bf16[2,4,1008,128]{3,2,1,0:T(8,128)(2,1)}, bf16[2,4,1008,128]{3,2,1,0:T(8,128)(2,1)}, u32[]{:S(2)}, u32[]{:S(2)}) collective-permute-start(bf16[2,4,1008,128]{3,2,1,0:T(8,128)(2,1)} %get-tuple-element.131), channel_id=1, source_target_pairs={{0,16},{16,0},{1,17},{17,1},{2,18},{18,2},{3,19},{19,3},{4,20},{20... | collective-permute-start | bytes 6193160 | tf_op jit(solution)/shard_map/ppermute | solution.py:1051
  181.4 55.8 %collective-permute-start.14 = (bf16[2,4,672,128]{3,2,1,0:T(8,128)(2,1)}, bf16[2,4,672,128]{3,2,1,0:T(8,128)(2,1)}, u32[]{:S(2)}, u32[]{:S(2)}) collective-permute-start(bf16[2,4,672,128]{3,2,1,0:T(8,128)(2,1)} %get-tuple-element.129), channel_id=1, source_target_pairs={{0,2},{1,3},{2,0},{3,1},{4,6},{5,7},{6,4},{7,5},{8,10},{9,11},{10,... | collective-permute-start | bytes 4128776 | tf_op jit(solution)/shard_map/ppermute | solution.py:1048
  236.6 7.0 %collective-permute-start.13 = (bf16[1536,896]{1,0:T(8,128)(2,1)}, bf16[1536,896]{1,0:T(8,128)(2,1)}, u32[]{:S(2)}, u32[]{:S(2)}) collective-permute-start(bf16[1536,896]{1,0:T(8,128)(2,1)} %get-tuple-element.125), channel_id=1, source_target_pairs={{0,1},{1,0},{2,3},{3,2},{4,5},{5,4},{6,7},{7,6},{8,9},{9,8},{10,11... | collective-permute-start | bytes 8257544 | tf_op jit(solution)/shard_map/ppermute | solution.py:1048
  236.7 9.4 %collective-permute-start.12 = (bf16[1536,896]{1,0:T(8,128)(2,1)}, bf16[1536,896]{1,0:T(8,128)(2,1)}, u32[]{:S(2)}, u32[]{:S(2)}) collective-permute-start(bf16[1536,896]{1,0:T(8,128)(2,1)} %get-tuple-element.124), channel_id=1, source_target_pairs={{0,1},{1,0},{2,3},{3,2},{4,5},{5,4},{6,7},{7,6},{8,9},{9,8},{10,11... | collective-permute-start | bytes 8257544 | tf_op jit(solution)/shard_map/ppermute | solution.py:1048
  241.3 34.4 %collective-permute-start.19 = (bf16[4,1008,128]{2,1,0:T(8,128)(2,1)}, bf16[4,1008,128]{2,1,0:T(8,128)(2,1)}, u32[]{:S(2)}, u32[]{:S(2)}) collective-permute-start(bf16[4,1008,128]{2,1,0:T(8,128)(2,1)} %get-tuple-element.133.refs_14_), channel_id=1, source_target_pairs={{0,2},{1,3},{2,0},{3,1},{4,6},{5,7},{6,4},{7,5},{8,10},{9,11},{10,... | collective-permute-start | bytes 3096584 | tf_op jit(solution)/shard_map/ppermute | solution.py:1048
  242.1 33.6 %collective-permute-start.18 = (bf16[4,672,128]{2,1,0:T(8,128)(2,1)}, bf16[4,672,128]{2,1,0:T(8,128)(2,1)}, u32[]{:S(2)}, u32[]{:S(2)}) collective-permute-start(bf16[4,672,128]{2,1,0:T(8,128)(2,1)} %get-tuple-element.132.refs_13_), channel_id=1, source_target_pairs={{0,16},{16,0},{1,17},{17,1},{2,18},{18,2},{3,19},{19,3},{4,20},{20... | collective-permute-start | bytes 2064392 | tf_op jit(solution)/shard_map/ppermute | solution.py:1051
  256.1 56.0 %collective-permute-start.17 = (bf16[2,4,1008,128]{3,2,1,0:T(8,128)(2,1)}, bf16[2,4,1008,128]{3,2,1,0:T(8,128)(2,1)}, u32[]{:S(2)}, u32[]{:S(2)}) collective-permute-start(bf16[2,4,1008,128]{3,2,1,0:T(8,128)(2,1)} %get-tuple-element.142), channel_id=1, source_target_pairs={{0,16},{16,0},{1,17},{17,1},{2,18},{18,2},{3,19},{19,3},{4,20},{20... | collective-permute-start | bytes 6193160 | tf_op jit(solution)/shard_map/ppermute | solution.py:1051
  257.6 17.2 %copy-start.4 = (bf16[2,4,672,128]{3,2,1,0:T(8,128)(2,1)S(1)}, bf16[2,4,672,128]{3,2,1,0:T(8,128)(2,1)}, u32[]{:S(2)}) copy-start(bf16[2,4,672,128]{3,2,1,0:T(8,128)(2,1)} %get-tuple-element.140) | copy-start | bytes 4128772
  274.8 37.3 %collective-permute-start.16 = (bf16[2,4,672,128]{3,2,1,0:T(8,128)(2,1)S(1)}, bf16[2,4,672,128]{3,2,1,0:T(8,128)(2,1)}, u32[]{:S(2)}, u32[]{:S(2)}) collective-permute-start(bf16[2,4,672,128]{3,2,1,0:T(8,128)(2,1)S(1)} %copy-done.4), channel_id=1, source_target_pairs={{0,2},{1,3},{2,0},{3,1},{4,6},{5,7},{6,4},{7,5},{8,10},{9,11},{10,... | collective-permute-start | bytes 4128776 | tf_op jit(solution)/shard_map/ppermute | solution.py:1048
  280.3 31.8 %collective-permute-start.20 = (bf16[2,1680,128]{2,1,0:T(8,128)(2,1)}, bf16[2,1680,128]{2,1,0:T(8,128)(2,1)}, u32[]{:S(2)}, u32[]{:S(2)}) collective-permute-start(bf16[2,1680,128]{2,1,0:T(8,128)(2,1)} %get-tuple-element.146.refs_10_), channel_id=1, source_target_pairs={{0,4},{1,5},{2,6},{3,7},{4,0},{5,1},{6,2},{7,3},{8,12},{9,13},{10,... | collective-permute-start | bytes 2580488 | tf_op jit(solution)/shard_map/ppermute | solution.py:1048
  281.4 30.7 %collective-permute-start.21 = (bf16[768,256]{1,0:T(8,128)(2,1)}, bf16[768,256]{1,0:T(8,128)(2,1)S(1)}, u32[]{:S(2)}, u32[]{:S(2)}) collective-permute-start(bf16[768,256]{1,0:T(8,128)(2,1)} %get-tuple-element.148), channel_id=1, source_target_pairs={{0,16},{16,0},{1,17},{17,1},{2,18},{18,2},{3,19},{19,3},{4,20},{20... | collective-permute-start | bytes 1179656 | tf_op jit(solution)/shard_map/ppermute | solution.py:1051
  317.6 24.6 %collective-permute-start.24 = (bf16[4,1008,128]{2,1,0:T(8,128)(2,1)}, bf16[4,1008,128]{2,1,0:T(8,128)(2,1)}, u32[]{:S(2)}, u32[]{:S(2)}) collective-permute-start(bf16[4,1008,128]{2,1,0:T(8,128)(2,1)} %get-tuple-element.155.refs_10_), channel_id=1, source_target_pairs={{0,2},{1,3},{2,0},{3,1},{4,6},{5,7},{6,4},{7,5},{8,10},{9,11},{10,... | collective-permute-start | bytes 3096584 | tf_op jit(solution)/shard_map/ppermute | solution.py:1048
  318.8 22.6 %collective-permute-start.23 = (bf16[4,672,128]{2,1,0:T(8,128)(2,1)}, bf16[4,672,128]{2,1,0:T(8,128)(2,1)}, u32[]{:S(2)}, u32[]{:S(2)}) collective-permute-start(bf16[4,672,128]{2,1,0:T(8,128)(2,1)} %get-tuple-element.154.refs_9_), channel_id=1, source_target_pairs={{0,16},{16,0},{1,17},{17,1},{2,18},{18,2},{3,19},{19,3},{4,20},{20... | collective-permute-start | bytes 2064392 | tf_op jit(solution)/shard_map/ppermute | solution.py:1051
  320.3 21.1 %collective-permute-start.25 = (bf16[1680,128]{1,0:T(8,128)(2,1)}, bf16[1680,128]{1,0:T(8,128)(2,1)}, u32[]{:S(2)}, u32[]{:S(2)}) collective-permute-start(bf16[1680,128]{1,0:T(8,128)(2,1)} %get-tuple-element.156.refs_11_), channel_id=1, source_target_pairs={{0,8},{1,9},{2,10},{3,11},{4,12},{5,13},{6,14},{7,15},{8,0},{9,1},... | collective-permute-start | bytes 1290248 | tf_op jit(solution)/shard_map/ppermute | solution.py:1048
  331.5 15.9 %collective-permute-start.27 = (bf16[2,2,4,480,128]{4,3,2,1,0:T(8,128)(2,1)}, bf16[2,2,4,480,128]{4,3,2,1,0:T(8,128)(2,1)S(1)}, u32[]{:S(2)}, u32[]{:S(2)}) collective-permute-start(bf16[2,2,4,480,128]{4,3,2,1,0:T(8,128)(2,1)} %get-tuple-element.163), channel_id=1, source_target_pairs={{0,1},{1,0},{2,3},{3,2},{4,5},{5,4},{6,7},{7,6},{8,9},{9,8},{10,11... | collective-permute-start | bytes 5898248 | tf_op jit(solution)/shard_map/ppermute | solution.py:1048
  331.5 24.2 %collective-permute-start.22 = (bf16[384,896]{1,0:T(8,128)(2,1)}, bf16[384,896]{1,0:T(8,128)(2,1)}, u32[]{:S(2)}, u32[]{:S(2)}) collective-permute-start(bf16[384,896]{1,0:T(8,128)(2,1)} %get-tuple-element.150), channel_id=1, source_target_pairs={{0,16},{16,0},{1,17},{17,1},{2,18},{18,2},{3,19},{19,3},{4,20},{20... | collective-permute-start | bytes 2064392 | tf_op jit(solution)/shard_map/ppermute | solution.py:1051
  347.4 1.3 copy-start
  352.1 12.0 %collective-permute-start.28 = (bf16[2,4,240,128]{3,2,1,0:T(8,128)(2,1)}, bf16[2,4,240,128]{3,2,1,0:T(8,128)(2,1)S(1)}, u32[]{:S(2)}, u32[]{:S(2)}) collective-permute-start(bf16[2,4,240,128]{3,2,1,0:T(8,128)(2,1)} %get-tuple-element.165), channel_id=1, source_target_pairs={{0,2},{1,3},{2,0},{3,1},{4,6},{5,7},{6,4},{7,5},{8,10},{9,11},{10,... | collective-permute-start | bytes 1474568 | tf_op jit(solution)/shard_map/ppermute | solution.py:1048
  353.2 11.6 %collective-permute-start.29 = (bf16[2,4,240,128]{3,2,1,0:T(8,128)(2,1)}, bf16[2,4,240,128]{3,2,1,0:T(8,128)(2,1)S(1)}, u32[]{:S(2)}, u32[]{:S(2)}) collective-permute-start(bf16[2,4,240,128]{3,2,1,0:T(8,128)(2,1)} %get-tuple-element.167), channel_id=1, source_target_pairs={{0,16},{16,0},{1,17},{17,1},{2,18},{18,2},{3,19},{19,3},{4,20},{20... | collective-permute-start | bytes 1474568 | tf_op jit(solution)/shard_map/ppermute | solution.py:1051
  354.6 19.8 %collective-permute-start.26 = (bf16[2,1680,128]{2,1,0:T(8,128)(2,1)}, bf16[2,1680,128]{2,1,0:T(8,128)(2,1)S(1)}, u32[]{:S(2)}, u32[]{:S(2)}) collective-permute-start(bf16[2,1680,128]{2,1,0:T(8,128)(2,1)} %get-tuple-element.161.refs_8_), channel_id=1, source_target_pairs={{0,4},{1,5},{2,6},{3,7},{4,0},{5,1},{6,2},{7,3},{8,12},{9,13},{10,... | collective-permute-start | bytes 2580488 | tf_op jit(solution)/shard_map/ppermute | solution.py:1048
  364.1 0.8 copy-start.21
  364.8 0.8 copy-start.22
  367.7 13.9 %collective-permute-start.31 = (bf16[4,240,128]{2,1,0:T(8,128)(2,1)}, bf16[4,240,128]{2,1,0:T(8,128)(2,1)S(1)}, u32[]{:S(2)}, u32[]{:S(2)}) collective-permute-start(bf16[4,240,128]{2,1,0:T(8,128)(2,1)} %get-tuple-element.168.refs_2_), channel_id=1, source_target_pairs={{0,16},{16,0},{1,17},{17,1},{2,18},{18,2},{3,19},{19,3},{4,20},{20... | collective-permute-start | bytes 737288 | tf_op jit(solution)/shard_map/ppermute | solution.py:1051
  369.2 12.5 %collective-permute-start.32 = (bf16[4,240,128]{2,1,0:T(8,128)(2,1)}, bf16[4,240,128]{2,1,0:T(8,128)(2,1)}, u32[]{:S(2)}, u32[]{:S(2)}) collective-permute-start(bf16[4,240,128]{2,1,0:T(8,128)(2,1)} %get-tuple-element.169.refs_3_), channel_id=1, source_target_pairs={{0,2},{1,3},{2,0},{3,1},{4,6},{5,7},{6,4},{7,5},{8,10},{9,11},{10,... | collective-permute-start | bytes 737288 | tf_op jit(solution)/shard_map/ppermute | solution.py:1048
  370.7 28.3 %collective-permute-start.34 = (bf16[1680,128]{1,0:T(8,128)(2,1)}, bf16[1680,128]{1,0:T(8,128)(2,1)}, u32[]{:S(2)}, u32[]{:S(2)}) collective-permute-start(bf16[1680,128]{1,0:T(8,128)(2,1)} %get-tuple-element.174.refs_0_), channel_id=1, source_target_pairs={{0,16},{16,0},{1,17},{17,1},{2,18},{18,2},{3,19},{19,3},{4,20},{20... | collective-permute-start | bytes 1290248 | tf_op jit(solution)/shard_map/ppermute | solution.py:1051
  374.5 0.9 copy-start.8
  378.2 22.3 %collective-permute-start.35 = (bf16[384,896]{1,0:T(8,128)(2,1)}, bf16[384,896]{1,0:T(8,128)(2,1)S(1)}, u32[]{:S(2)}, u32[]{:S(2)}) collective-permute-start(bf16[384,896]{1,0:T(8,128)(2,1)} %get-tuple-element.175), channel_id=1, source_target_pairs={{0,16},{16,0},{1,17},{17,1},{2,18},{18,2},{3,19},{19,3},{4,20},{20... | collective-permute-start | bytes 2064392 | tf_op jit(solution)/shard_map/ppermute | solution.py:1051
  378.5 7.9 %copy-start.9 = (bf16[384,896]{1,0:T(8,128)(2,1)S(1)}, bf16[384,896]{1,0:T(8,128)(2,1)}, u32[]{:S(2)}) copy-start(bf16[384,896]{1,0:T(8,128)(2,1)} %get-tuple-element.138) | copy-start | bytes 2064388
  378.5 22.0 %collective-permute-start.30 = (bf16[1680,128]{1,0:T(8,128)(2,1)}, bf16[1680,128]{1,0:T(8,128)(2,1)}, u32[]{:S(2)}, u32[]{:S(2)}) collective-permute-start(bf16[1680,128]{1,0:T(8,128)(2,1)} %get-tuple-element.171.refs_12_), channel_id=1, source_target_pairs={{0,8},{1,9},{2,10},{3,11},{4,12},{5,13},{6,14},{7,15},{8,0},{9,1},... | collective-permute-start | bytes 1290248 | tf_op jit(solution)/shard_map/ppermute | solution.py:1048
  384.7 8.7 %collective-permute-start.33 = (bf16[2,480,128]{2,1,0:T(8,128)(2,1)}, bf16[2,480,128]{2,1,0:T(8,128)(2,1)S(1)}, u32[]{:S(2)}, u32[]{:S(2)}) collective-permute-start(bf16[2,480,128]{2,1,0:T(8,128)(2,1)} %get-tuple-element.173), channel_id=1, source_target_pairs={{0,4},{1,5},{2,6},{3,7},{4,0},{5,1},{6,2},{7,3},{8,12},{9,13},{10,... | collective-permute-start | bytes 737288 | tf_op jit(solution)/shard_map/ppermute | solution.py:1048
  388.7 30.1 %collective-permute-start.38 = (bf16[1680,128]{1,0:T(8,128)(2,1)}, bf16[1680,128]{1,0:T(8,128)(2,1)}, u32[]{:S(2)}, u32[]{:S(2)}) collective-permute-start(bf16[1680,128]{1,0:T(8,128)(2,1)} %get-tuple-element.174.refs_0_), channel_id=1, source_target_pairs={{0,1},{1,0},{2,3},{3,2},{4,5},{5,4},{6,7},{7,6},{8,9},{9,8},{10,11... | collective-permute-start | bytes 1290248 | tf_op jit(solution)/shard_map/ppermute | solution.py:1048
  395.7 10.8 %collective-permute-start.36 = (bf16[480,128]{1,0:T(8,128)(2,1)}, bf16[480,128]{1,0:T(8,128)(2,1)}, u32[]{:S(2)}, u32[]{:S(2)}) collective-permute-start(bf16[480,128]{1,0:T(8,128)(2,1)} %sums.19.refs_3_), channel_id=1, source_target_pairs={{0,8},{1,9},{2,10},{3,11},{4,12},{5,13},{6,14},{7,15},{8,0},{9,1},... | collective-permute-start | bytes 368648 | tf_op jit(solution)/shard_map/ppermute | solution.py:1048
  400.5 0.8 copy-start.11
  404.3 4.3 copy-start.10
  404.3 13.0 %collective-permute-start.40 = (bf16[1680,128]{1,0:T(8,128)(2,1)}, bf16[1680,128]{1,0:T(8,128)(2,1)S(1)}, u32[]{:S(2)}, u32[]{:S(2)}) collective-permute-start(bf16[1680,128]{1,0:T(8,128)(2,1)} %get-tuple-element.177.refs_3_.refs_4_), channel_id=1, source_target_pairs={{0,16},{16,0},{1,17},{17,1},{2,18},{18,2},{3,19},{19,3},{4,20},{20... | collective-permute-start | bytes 1290248 | tf_op jit(solution)/shard_map/ppermute | solution.py:1051
  406.0 12.8 %collective-permute-start.41 = (bf16[1680,128]{1,0:T(8,128)(2,1)}, bf16[1680,128]{1,0:T(8,128)(2,1)S(1)}, u32[]{:S(2)}, u32[]{:S(2)}) collective-permute-start(bf16[1680,128]{1,0:T(8,128)(2,1)} %get-tuple-element.177.refs_3_.refs_4_), channel_id=1, source_target_pairs={{0,1},{1,0},{2,3},{3,2},{4,5},{5,4},{6,7},{7,6},{8,9},{9,8},{10,11... | collective-permute-start | bytes 1290248 | tf_op jit(solution)/shard_map/ppermute | solution.py:1048
  406.0 12.8 %collective-permute-start.39 = (bf16[1680,128]{1,0:T(8,128)(2,1)}, bf16[1680,128]{1,0:T(8,128)(2,1)S(1)}, u32[]{:S(2)}, u32[]{:S(2)}) collective-permute-start(bf16[1680,128]{1,0:T(8,128)(2,1)} %get-tuple-element.178.refs_1_), channel_id=1, source_target_pairs={{0,1},{1,0},{2,3},{3,2},{4,5},{5,4},{6,7},{7,6},{8,9},{9,8},{10,11... | collective-permute-start | bytes 1290248 | tf_op jit(solution)/shard_map/ppermute | solution.py:1048
  408.2 7.1 %collective-permute-start.37 = (bf16[480,128]{1,0:T(8,128)(2,1)}, bf16[480,128]{1,0:T(8,128)(2,1)S(1)}, u32[]{:S(2)}, u32[]{:S(2)}) collective-permute-start(bf16[480,128]{1,0:T(8,128)(2,1)} %sums.21), channel_id=1, source_target_pairs={{0,16},{16,0},{1,17},{17,1},{2,18},{18,2},{3,19},{19,3},{4,20},{20... | collective-permute-start | bytes 368648 | tf_op jit(solution)/shard_map/ppermute | solution.py:1051
  408.6 6.8 %copy-start.13 = (bf16[480,128]{1,0:T(8,128)(2,1)S(1)}, bf16[480,128]{1,0:T(8,128)(2,1)}, u32[]{:S(2)}) copy-start(bf16[480,128]{1,0:T(8,128)(2,1)} %sums.21) | copy-start | bytes 368644
  410.9 6.4 %copy-start.12 = (bf16[56,1152]{1,0:T(8,128)(2,1)S(1)}, bf16[56,1152]{1,0:T(8,128)(2,1)}, u32[]{:S(2)}) copy-start(bf16[56,1152]{1,0:T(8,128)(2,1)} %param.14) | copy-start | bytes 387076
  415.4 2.9 copy-start.19
  417.4 1.8 copy-start.14
  417.4 1.8 collective-permute-start.42
  418.8 8.6 %copy-start.20 = (bf16[56]{0:T(256)(128)(2,1)S(1)}, bf16[56]{0:T(256)(128)(2,1)}, u32[]{:S(2)}) copy-start(bf16[56]{0:T(256)(128)(2,1)} %param.17) | copy-start | bytes 340
  418.8 0.9 copy-start.15
  (5 other events, 3.7 us)
Sparse Core Ops, SparseCore 0:
  13.5 104.3 all-gather.4
  120.7 65.5 all-gather.6
where the time goes:
time: 444 us; the launch traced here: 435 us
  Pallas kernels  260 us (59%)
  waiting for transfers between devices  69.2 us (16%)
  starting transfers between devices  45.2 us (10%)
  other arithmetic  25.6 us (6%)
  local copies, waits for them, and re-layouts  17.6 us (4%)
  between operations  17.5 us (4%)
    pallas_call x2, Pallas kernels, mlp_call(): pl.pallas_call(functools.partial(mlp_kernel, counts=counts, tiles=tiles,...  101 us
    ppermute x25, waiting for transfers between devices, flip(): lax.ppermute(values_in, 'fsdp', [(i, i ^ bit) for i in range(self.shards)])  36.6 us
    pallas_call x11, Pallas kernels, sums(): pl.pallas_call(dropping(functools.partial(sums_kernel, plan=plan), len(ar...  35.8 us
    ppermute x18, waiting for transfers between devices, other_half(): return lax.ppermute(values_in, 'seq', [(0, 1), (1, 0)])  26.5 us
    ppermute x25, starting transfers between devices, flip(): lax.ppermute(values_in, 'fsdp', [(i, i ^ bit) for i in range(self.shards)])  26 us
    pallas_call x1, Pallas kernels, near_backward(): pl.pallas_call(functools.partial(dropping(near_backward_kernel, 10, len(o...  25.3 us
    ppermute x18, starting transfers between devices, other_half(): return lax.ppermute(values_in, 'seq', [(0, 1), (1, 0)])  19.1 us
    pallas_call x1, Pallas kernels, far_backward(): pl.pallas_call(functools.partial(dropping(dropping(far_backward_kernel, 1...  17.2 us
  transfers between devices with their start and end apart: 45, of which 19 were waited for; matrix products, arithmetic and copies ran while one was open for 8% of the time, Pallas kernels for 56%

commit v1 on v0

--- a/solution.py
+++ b/solution.py
@@ -19,7 +19,6 @@
 
 LIGHT = pl.CostEstimate(flops=1, bytes_accessed=1, transcendentals=0)
 MIDDLE = pl.CostEstimate(flops=8 * 10**9, bytes_accessed=MIB, transcendentals=0)
-SHORT = pl.CostEstimate(flops=28 * 10**8, bytes_accessed=MIB, transcendentals=0)
 HEAVY = pl.CostEstimate(flops=6 * 10**10, bytes_accessed=16 * MIB, transcendentals=0)
 
 bf16 = jnp.bfloat16
@@ -418,7 +417,7 @@
             *alike(through),
         ],
         input_output_aliases={8 + i: 2 + i for i in range(len(through))},
-        compiler_params=pltpu.CompilerParams(vmem_limit_bytes=62 * MIB),
+        compiler_params=pltpu.CompilerParams(vmem_limit_bytes=64 * MIB - 65536),
         cost_estimate=LIGHT,
         name="attention_far_back",
     )(half, q, qx, g, o, lse, kv, kx, *through)
@@ -451,7 +450,7 @@
             jax.ShapeDtypeStruct((tokens, width), bf16),
             jax.ShapeDtypeStruct((tokens, 2 * LANES), f32),
         ],
-        compiler_params=pltpu.CompilerParams(vmem_limit_bytes=62 * MIB),
+        compiler_params=pltpu.CompilerParams(vmem_limit_bytes=64 * MIB - 65536),
         cost_estimate=LIGHT,
         name="attention_near_back",
     )(q, qx, g, o, lse, cosines, sines, kv, kx, far, *others)
@@ -525,7 +524,7 @@
             out_specs=[whole(array) for array in out_shape],
         ),
         out_shape=out_shape,
-        compiler_params=pltpu.CompilerParams(vmem_limit_bytes=62 * MIB),
+        compiler_params=pltpu.CompilerParams(vmem_limit_bytes=64 * MIB - 65536),
         cost_estimate=LIGHT,
         name="weight_grads",
     )(at, *args, *others)
@@ -564,7 +563,7 @@
             out_specs=[whole(rows, width)] * 2,
         ),
         out_shape=[jax.ShapeDtypeStruct((rows, width), bf16)] * 2,
-        compiler_params=pltpu.CompilerParams(vmem_limit_bytes=62 * MIB),
+        compiler_params=pltpu.CompilerParams(vmem_limit_bytes=64 * MIB - 65536),
         cost_estimate=LIGHT,
         name="input_grad",
     )(half, x, gain, project, weight, grad_middle, *others)
@@ -662,7 +661,7 @@
         ),
         out_shape=[jax.ShapeDtypeStruct((rows, width), bf16)] * 2 + [shape(f32), shape(bf16), shape(bf16)] + alike(through),
         input_output_aliases={13 + len(others) + i: 5 + i for i in range(len(through))},
-        compiler_params=pltpu.CompilerParams(vmem_limit_bytes=62 * MIB),
+        compiler_params=pltpu.CompilerParams(vmem_limit_bytes=64 * MIB - 65536),
         cost_estimate=LIGHT,
         name="middle_back",
     )(half, *terms, *terms, middle, grad_out, gain, weight, *others, *through)
@@ -810,7 +809,7 @@
             shape_y,
             shape_y,
         ],
-        compiler_params=pltpu.CompilerParams(vmem_limit_bytes=62 * MIB),
+        compiler_params=pltpu.CompilerParams(vmem_limit_bytes=64 * MIB - 65536),
         cost_estimate=HEAVY,
         name="feed_forward",
     )(at, near, far, gnear, gfar, *(w for w, _ in weights))
@@ -986,7 +985,7 @@
             scratch_shapes=[pltpu.VMEM((2, 2, *chunk[0].shape), bf16) for chunk in chunks],
         ),
         out_shape=out_shape,
-        compiler_params=pltpu.CompilerParams(vmem_limit_bytes=62 * MIB),
+        compiler_params=pltpu.CompilerParams(vmem_limit_bytes=64 * MIB - 65536),
         cost_estimate=LIGHT,
         name="unpack",
     )(at, *args)
@@ -1100,10 +1099,7 @@
         for terms in parts:
             for array, block, place in terms:
                 args.append(array)
-                if grid == 1:
-                    index = lambda i, place=place: place
-                else:
-                    index = lambda i, place=place: (*place[:-2], i, 0)
+                index = lambda i, place=place: (*place[:-2], place[-2] * grid + i, 0)
                 in_specs.append(pl.BlockSpec(block, index))
             below += block[-2]
         lead = tuple(n for n in block[:-2] if n is not None)
@@ -1117,7 +1113,7 @@
         out_specs=out_specs + [ANYWHERE] * len(through),
         out_shape=out_shape + alike(through),
         input_output_aliases={len(args) + len(others) + i: len(plan) + i for i in range(len(through))},
-        compiler_params=pltpu.CompilerParams(vmem_limit_bytes=62 * MIB),
+        compiler_params=pltpu.CompilerParams(vmem_limit_bytes=64 * MIB - 65536),
         cost_estimate=cost,
         name="sums",
     )(*args, *others, *through)
@@ -1132,8 +1128,8 @@
     def rows(self, array):
         return array.shape[-2] // self.grid
 
-    def second(self):
-        whole = lambda array: (array, (None, 4, self.rows(array), LANES), (1, 0, 0, 0))
+    def second(self, grid=1):
+        whole = lambda array: (array, (None, 4, array.shape[-2] // grid, LANES), (1, 0, 0, 0))
         return [[[whole(k), whole(g)]] for k, g in zip(self.kept, self.got)]
 
     def second_sent(self, *sent):
@@ -1154,16 +1150,16 @@
         self.sent, self.kept = (sent,), kept
         self.got = self.wires.flip(sent, 4)
 
-    def fourth(self):
-        block = (None, self.rows(self.kept), LANES)
+    def fourth(self, grid=1):
+        block = (None, self.kept.shape[-2] // grid, LANES)
         return [[[(self.kept, block, (1, 0, 0)), (self.got, block, (1, 0, 0))]]]
 
     def fourth_sent(self, sent):
         self.sent = (sent,)
         self.next = self.wires.flip(sent, 8)
 
-    def fifth(self):
-        block = (None, self.rows(self.kept), LANES)
+    def fifth(self, grid=1):
+        block = (None, self.kept.shape[-2] // grid, LANES)
         terms = [(self.kept, block, (0, 0, 0)), (self.got, block, (0, 0, 0)), (self.next, block[1:], (0, 0))]
         return [[terms]]
 
@@ -1312,7 +1308,7 @@
     )
     back_two = wires.flip(other_two, 1)
     if small_mesh:
-        sum_one.second_sent(*sums(sum_one.second(), 3, (own_two,), HEAVY))
+        sum_one.second_sent(*sums(sum_one.second(1), 1, (own_two,), HEAVY))
 
     others = sum_one.sent if small_mesh else ()
     kept_result, sent_result, grad_middle, branch, grad_attended, *grads_two = middle_back(
@@ -1334,7 +1330,7 @@
     others = ()
     if small_mesh:
         *sent_two, sent_one, sent_result = sums(
-            sum_two.second() + sum_one.fourth(), 3, (query_grad, got_kv), through=(sent_result,)
+            sum_two.second(1) + sum_one.fourth(1), 1, (query_grad, got_kv), through=(sent_result,)
         )
         sum_two.second_sent(*sent_two)
         sum_one.fourth_sent(sent_one)
@@ -1350,7 +1346,7 @@
     if small_mesh:
         theirs = wires.flip(theirs, 1)
         kept_grad, sent_grad = input_grad(half, tokens, gain_one, project, qkv_full, grad_middle, ())
-        sent_two, kept_two, sent_one = sums(sum_two.third() + sum_one.fifth(), 3, (kept_grad,), HEAVY)
+        sent_two, kept_two, sent_one = sums(sum_two.third() + sum_one.fifth(3), 3, (kept_grad,), HEAVY)
         sum_two.third_sent(sent_two, kept_two)
         sum_one.fifth_sent(sent_one)
         groups_of = []
@@ -1361,18 +1357,19 @@
                 place = [0, 0, 0, axis, 0]
                 place[axis] = part
                 groups_of.append([[(array, tuple(block), tuple(place)) for array in (mine, theirs)]])
-        small = ChipSum(wires, *sums(groups_of, 1, sum_two.sent), 1)
-        small.second_sent(*sums(small.second(), 1, (got_result,), SHORT))
-        sent_two, sent_grad = sums(sum_two.fourth(), 3, small.sent, through=(sent_grad,))
+        small = ChipSum(wires, *sums(groups_of, 1, (*sum_two.sent, got_result)), 1)
+        *sent, sent_two, sent_grad = sums(small.second() + sum_two.fourth(), 1, (), LIGHT, (sent_grad,))
+        small.second_sent(*sent)
         sum_two.fourth_sent(sent_two)
+        got_grad = wires.other_half(sent_grad)
         small.third_sent(*sums(small.third(), 1, sum_two.sent, MIDDLE))
-        got_grad = wires.other_half(sent_grad)
-        small.fourth_sent(*sums(small.fourth(), 1))
-        sent_two, sum_one.got, got_grad = sums(
-            sum_two.fifth(), 3, small.sent, HEAVY, (sum_one.got, got_grad)
+        sent, sent_two = sums(small.fourth() + sum_two.fifth())
+        small.fourth_sent(sent)
+        sum_two.fifth_sent(sent_two)
+        sent, sum_one.got, got_grad, got_result = sums(
+            small.fifth(), 1, sum_two.sent, LIGHT, (sum_one.got, got_grad, got_result)
         )
-        sum_two.fifth_sent(sent_two)
-        small.fifth_sent(*sums(small.fifth(), 1, sum_two.sent))
+        small.fifth_sent(sent)
         one, two = small.total()
         bias = one[2 * cut + 16 : 2 * cut + 18].astype(f32)
         bias_qk = lax.dynamic_slice_in_dim(bias[0], wires.core * qk_own, qk_own)

time: 444 us -> 439 us (0.989)
  waiting for transfers between devices: 69.2 us -> 79.1 us
  local copies, waits for them, and re-layouts: 17.6 us -> 10.2 us
  Pallas kernels: 260 us -> 254 us
    ppermute x18, waiting for transfers between devices: 26.5 us -> 35.4 us  [other_half(): return lax.ppermute(values_in, 'seq', [(0, 1), (1, 0)])]
    unnamed x49 -> x19, local copies, waits for them, and re-layouts: 7.37 us -> 0.05 us
    pallas_call x11 -> x9, Pallas kernels: 35.8 us -> 29.3 us  [sums(): pl.pallas_call(dropping(functools.partial(sums_kernel, plan=plan), len(ar...]
    ppermute x18, starting transfers between devices: 19.1 us -> 24.8 us  [other_half(): return lax.ppermute(values_in, 'seq', [(0, 1), (1, 0)])]
    ppermute x25, waiting for transfers between devices: 36.6 us -> 41.7 us  [flip(): lax.ppermute(values_in, 'fsdp', [(i, i ^ bit) for i in range(self.shards)])]
    ppermute x25, starting transfers between devices: 26 us -> 21.5 us  [flip(): lax.ppermute(values_in, 'fsdp', [(i, i ^ bit) for i in range(self.shards)])]
  transfers between devices with their start and end apart: 45 -> 45, of which waited for: 19 -> 19; matrix products, arithmetic and copies ran while one was open for 8% -> 7% of each run, Pallas kernels for 56% -> 55%
where the time goes in v1:
time: 439 us; the launch traced here: 433 us
  Pallas kernels  254 us (58%)
  waiting for transfers between devices  79.1 us (18%)
  starting transfers between devices  46.4 us (11%)
  other arithmetic  25.7 us (6%)
  between operations  17.5 us (4%)
  local copies, waits for them, and re-layouts  10.2 us (2%)
    pallas_call x2, Pallas kernels, mlp_call(): pl.pallas_call(functools.partial(mlp_kernel, counts=counts, tiles=tiles,...  101 us
    ppermute x25, waiting for transfers between devices, flip(): lax.ppermute(values_in, 'fsdp', [(i, i ^ bit) for i in range(self.shards)])  41.7 us
    ppermute x18, waiting for transfers between devices, other_half(): return lax.ppermute(values_in, 'seq', [(0, 1), (1, 0)])  35.4 us
    pallas_call x9, Pallas kernels, sums(): pl.pallas_call(dropping(functools.partial(sums_kernel, plan=plan), len(ar...  29.3 us
    pallas_call x1, Pallas kernels, near_backward(): pl.pallas_call(functools.partial(dropping(near_backward_kernel, 10, len(o...  25.5 us
    ppermute x18, starting transfers between devices, other_half(): return lax.ppermute(values_in, 'seq', [(0, 1), (1, 0)])  24.8 us
    ppermute x25, starting transfers between devices, flip(): lax.ppermute(values_in, 'fsdp', [(i, i ^ bit) for i in range(self.shards)])  21.5 us
    pallas_call x1, Pallas kernels, far_backward(): pl.pallas_call(functools.partial(dropping(dropping(far_backward_kernel, 1...  17.1 us
  transfers between devices with their start and end apart: 45, of which 19 were waited for; matrix products, arithmetic and copies ran while one was open for 7% of the time, Pallas kernels for 55%

profile of v1, /device:TPU:0, one launch (start us, length us, event | category | flops | bytes accessed | tf_op | source)
XLA Modules:
  0.0 432.5 jit_solution(18424008810287426464)
XLA Ops:
  8.9 4.4 %pack.1 = (bf16[4432,128]{1,0:T(8,128)(2,1)}, bf16[1680,128]{1,0:T(8,128)(2,1)}) custom-call(s32[1]{0:T(128)} %bitcast.half_ref.refs_0_, bf16[56,4864]{1,0:T(8,128)(2,1)} %refs_8_, bf16[56,4864]{1,0:T(8,128)(2,1)} %refs_9_, bf16[304,896]{1,0:T(8,128)(2,1)} %down_ref, bf16[56,896]{1,0:T(8,128)(2,1)} %out_ref), custom_call_target="tpu_custom_call" | custom-call | flops 1 | bytes 1 | tf_op jit(solution)/shard_map/pack/pallas_call | solution.py:885
  13.5 4.1 collective-permute-start.1
  18.5 1.5 collective-permute-start
  22.3 7.4 %collective-permute-done.2 = bf16[2,1,32,1152]{3,2,1,0:T(8,128)(2,1)S(1)} collective-permute-done((bf16[2,1,32,1152]{3,2,1,0:T(8,128)(2,1)S(1)}, bf16[2,1,32,1152]{3,2,1,0:T(8,128)(2,1)S(1)}, u32[]{:S(2)}, u32[]{:S(2)}) %collective-permute-start.2) | collective-permute-done | bytes 147488 | tf_op jit(solution)/shard_map/ppermute | solution.py:1047
  29.8 1.6 collective-permute-start.3
  31.4 4.3 collective-permute-done.4
  39.0 1.4 fusion.6
  46.7 1.6 collective-permute-start.5
  48.3 12.5 %collective-permute-done.5 = bf16[4,2,32,1152]{3,2,0,1:T(8,128)(2,1)S(1)} collective-permute-done((bf16[4,2,32,1152]{3,2,0,1:T(8,128)(2,1)S(1)}, bf16[4,2,32,1152]{3,2,0,1:T(8,128)(2,1)S(1)}, u32[]{:S(2)}, u32[]{:S(2)}) %collective-permute-start.5) | collective-permute-done | bytes 589856 | tf_op jit(solution)/shard_map/ppermute | solution.py:1050
  61.2 3.1 collective-permute-done.6
  65.3 1.5 slice.87
  68.2 6.8 %project.1 = (bf16[768,896]{1,0:T(8,128)(2,1)}, bf16[768,896]{1,0:T(8,128)(2,1)}, bf16[768,256]{1,0:T(8,128)(2,1)}) custom-call(bf16[768,896]{1,0:T(8,128)(2,1)} %pad_maximum_fusion.2.x_ref.refs_1_, f32[1,896]{1,0:T(1,128)} %reshape.163.gain_ref.refs_2_, bf16[896,1152]{1,0:T(8,128)(2,1)} %bitcast.63, f32[1,1152]{1,0:T(1,128)} %reshape.164.bias_ref, ...), custom_call_target="tpu_custom_call" | custom-call | flops 1 | bytes 1 | tf_op jit(solution)/shard_map/project/pallas_call | solution.py:76
  75.0 1.6 collective-permute-start.7
  78.0 16.8 %attention_near.1 = (f32[768,896]{1,0:T(8,128)}, f32[768,128]{1,0:T(8,128)}) custom-call(bf16[768,896]{1,0:T(8,128)(2,1)} %get-tuple-element.105.q_ref.refs_1_.refs_0_, bf16[768,128]{1,0:T(8,128)(2,1)} %select_convert_fusion.qx_ref.refs_2_.refs_1_, bf16[768,256]{1,0:T(8,128)(2,1)} %get-tuple-element.106.kv_ref.refs_7_, bf16[768,128]{1,0:T(8,128)(2,1)} %fusion.1.kx_ref.refs_8_), custom_call_target="tpu_custom_call" | custom-call | flops 60000002048 | bytes 16777216 | tf_op jit(solution)/shard_map/attention_near/pallas_call | solution.py:217
  94.8 6.4 %collective-permute-done.8 = bf16[384,896]{1,0:T(8,128)(2,1)} collective-permute-done((bf16[384,896]{1,0:T(8,128)(2,1)}, bf16[384,896]{1,0:T(8,128)(2,1)}, u32[]{:S(2)}, u32[]{:S(2)}) %collective-permute-start.8) | collective-permute-done | bytes 688160 | tf_op jit(solution)/shard_map/ppermute | solution.py:1050
  103.5 12.8 %attention_far.1 = (bf16[768,896]{1,0:T(8,128)(2,1)}, f32[128,768]{1,0:T(8,128)}) custom-call(s32[1]{0:T(128)} %bitcast.half_ref.refs_0_, bf16[768,896]{1,0:T(8,128)(2,1)} %get-tuple-element.105.q_ref.refs_1_.refs_0_, bf16[768,128]{1,0:T(8,128)(2,1)} %select_convert_fusion.qx_ref.refs_2_.refs_1_, bf16[768,256]{1,0:T(8,128)(2,1)} %copy-done.1, ...), custom_call_target="tpu_custom_call" | custom-call | flops 1 | bytes 1 | tf_op jit(solution)/shard_map/attention_far/pallas_call | solution.py:238
  116.3 1.7 all-gather.5.cloned.1.call-done
  117.9 7.7 %out_project.1 = (f32[768,896]{1,0:T(8,128)}, bf16[768,896]{1,0:T(8,128)(2,1)}, bf16[896,896]{1,0:T(8,128)(2,1)}) custom-call(bf16[768,896]{1,0:T(8,128)(2,1)} %pad_maximum_fusion.2.x_ref.refs_1_, bf16[768,896]{1,0:T(8,128)(2,1)} %get-tuple-element.113.att_ref.refs_4_.refs_3_.refs_8_, f32[1,896]{1,0:T(1,128)} %reshape.165.gain_ref.refs_11_, ...), custom_call_target="tpu_custom_call" | custom-call | flops 1 | bytes 1 | tf_op jit(solution)/shard_map/out_project/pallas_call | solution.py:602
  126.6 2.5 constant_dynamic-slice_fusion.2
  129.1 4.0 collective-permute-start.11
  133.1 50.3 %feed_forward.2 = (bf16[1536,896]{1,0:T(8,128)(2,1)}, bf16[1536,896]{1,0:T(8,128)(2,1)}, bf16[2,4,672,128]{3,2,1,0:T(8,128)(2,1)}, bf16[2,4,672,128]{3,2,1,0:T(8...) custom-call(s32[4]{0:T(128)} %pad_add_fusion.2.at_ref.refs_0_, ...), custom_call_target="tpu_custom_call" | custom-call | flops 60000002048 | bytes 16777216 | tf_op jit(solution)/shard_map/feed_forward/pallas_call | solution.py:785
  183.5 1.3 collective-permute-start.14
  185.0 2.3 broadcast_select_fusion.1
  187.3 1.7 pad_maximum_fusion.rest_0_
  189.3 50.3 %feed_forward.3 = (bf16[1536,896]{1,0:T(8,128)(2,1)}, bf16[1536,896]{1,0:T(8,128)(2,1)}, bf16[2,4,672,128]{3,2,1,0:T(8,128)(2,1)}, bf16[2,4,672,128]{3,2,1,0:T(8...) custom-call(s32[4]{0:T(128)} %pad_add_fusion.2.at_ref.refs_0_, ...), custom_call_target="tpu_custom_call" | custom-call | flops 60000002048 | bytes 16777216 | tf_op jit(solution)/shard_map/feed_forward/pallas_call | solution.py:785
  239.7 3.3 sums.9
  243.9 1.4 collective-permute-start.16
  245.3 10.0 %middle_back.1 = (bf16[384,896]{1,0:T(8,128)(2,1)}, bf16[384,896]{1,0:T(8,128)(2,1)}, f32[768,896]{1,0:T(8,128)}, bf16[768,896]{1,0:T(8,128)(2,1)}, bf16[768,896...) custom-call(s32[1]{0:T(128)} %bitcast.half_ref.refs_0_, ...), custom_call_target="tpu_custom_call", output_to_operand_aliasing={{5}: (15, {}), {6}: (16, {}), {7}: (17, {}), {8}: (18, {})} | custom-call | flops 1 | bytes 1 | tf_op jit(solution)/shard_map/middle_back/pallas_call | solution.py:651
  255.4 1.5 collective-permute-start.20
  256.8 17.1 %attention_far_back.1 = (f32[896,768]{1,0:T(8,128)}, bf16[768,256]{1,0:T(8,128)(2,1)}) custom-call(s32[1]{0:T(128)} %bitcast.half_ref.refs_0_, bf16[768,896]{1,0:T(8,128)(2,1)} %get-tuple-element.105.q_ref.refs_1_.refs_0_, bf16[768,128]{1,0:T(8,128)(2,1)} %select_convert_fusion.qx_ref.refs_2_.refs_1_, bf16[768,896]{1,0:T(8,128)(2,1)} %get-tuple-element.143.refs_3_.refs_2_, ...), custom_call_target="tpu_custom_call" | custom-call | flops 1 | bytes 1 | tf_op jit(solution)/shard_map/attention_far_back/pallas_call | solution.py:396
  274.7 4.7 %sums.10 = (bf16[2,1680,128]{2,1,0:T(8,128)(2,1)}, bf16[2,1680,128]{2,1,0:T(8,128)(2,1)}) custom-call(bf16[2,4,672,128]{3,2,1,0:T(8,128)(2,1)} %get-tuple-element.131.refs_0_.refs_6_, bf16[2,4,672,128]{3,2,1,0:T(8,128)(2,1)} %collective-permute-done.14.refs_1_.refs_7_, bf16[4,672,128]{2,1,0:T(8,128)(2,1)} %collective-permute-done.16.refs_2_.refs_8_, ...), custom_call_target="tpu_custom_call" | custom-call | flops 8000000000 | bytes 1048576 | tf_op jit(solution)/shard_map/sums/pallas_call | solution.py:1109
  280.6 1.7 collective-permute-start.18
  282.4 25.5 %attention_near_back.1 = (bf16[768,896]{1,0:T(8,128)(2,1)}, f32[768,256]{1,0:T(8,128)}) custom-call(bf16[768,896]{1,0:T(8,128)(2,1)} %get-tuple-element.105.q_ref.refs_1_.refs_0_, bf16[768,128]{1,0:T(8,128)(2,1)} %select_convert_fusion.qx_ref.refs_2_.refs_1_, bf16[768,896]{1,0:T(8,128)(2,1)} %get-tuple-element.143.refs_3_.refs_2_, ...), custom_call_target="tpu_custom_call" | custom-call | flops 1 | bytes 1 | tf_op jit(solution)/shard_map/attention_near_back/pallas_call | solution.py:431
  307.9 6.5 %collective-permute-done.18.refs_7_.refs_4_ = bf16[768,256]{1,0:T(8,128)(2,1)} collective-permute-done((bf16[768,256]{1,0:T(8,128)(2,1)}, bf16[768,256]{1,0:T(8,128)(2,1)}, u32[]{:S(2)}, u32[]{:S(2)}) %collective-permute-start.18) | collective-permute-done | bytes 393248 | tf_op jit(solution)/shard_map/ppermute | solution.py:1050
  314.4 3.7 sums.11
  319.3 1.5 collective-permute-start.23
  320.9 9.4 %weight_grads.1 = (bf16[768,1152]{1,0:T(8,128)(2,1)}, bf16[2,2,4,480,128]{4,3,2,1,0:T(8,128)(2,1)}, bf16[2,2,4,480,128]{4,3,2,1,0:T(8,128)(2,1)}, f32[1,1152]{1,0:T(1,128)}) custom-call(s32[4]{0:T(128)} %pad_add_fusion.2.at_ref.refs_0_, bf16[768,896]{1,0:T(8,128)(2,1)} %get-tuple-element.142.refs_1_, bf16[768,896]{1,0:T(8,128)(2,1)} %get-tuple-element.146.refs_6_.refs_2_, ...), custom_call_target="tpu_custom_call" | custom-call | flops 1 | bytes 1 | tf_op jit(solution)/shard_map/weight_grads/pallas_call | solution.py:518
  330.8 7.1 %input_grad.1 = (bf16[384,896]{1,0:T(8,128)(2,1)}, bf16[384,896]{1,0:T(8,128)(2,1)}) custom-call(s32[1]{0:T(128)} %bitcast.half_ref.refs_0_, bf16[768,896]{1,0:T(8,128)(2,1)} %pad_maximum_fusion.2.x_ref.refs_1_, f32[1,896]{1,0:T(1,128)} %reshape.163.gain_ref.refs_2_, bf16[768,1152]{1,0:T(8,128)(2,1)} %get-tuple-element.161.refs_3_, ...), custom_call_target="tpu_custom_call" | custom-call | flops 1 | bytes 1 | tf_op jit(solution)/shard_map/input_grad/pallas_call | solution.py:556
  337.9 4.0 collective-permute-done.25.refs_14_
  342.6 5.2 %sums.12 = (bf16[2,1680,128]{2,1,0:T(8,128)(2,1)}, bf16[2,1680,128]{2,1,0:T(8,128)(2,1)}, bf16[1680,128]{1,0:T(8,128)(2,1)}) custom-call(bf16[2,4,672,128]{3,2,1,0:T(8,128)(2,1)} %get-tuple-element.150.refs_0_.refs_6_, bf16[2,4,672,128]{3,2,1,0:T(8,128)(2,1)} %collective-permute-done.19.refs_1_.refs_7_, ...), custom_call_target="tpu_custom_call" | custom-call | flops 60000002048 | bytes 16777216 | tf_op jit(solution)/shard_map/sums/pallas_call | solution.py:1109
  347.7 1.4 collective-permute-start.29
  349.1 1.7 collective-permute-done.26.refs_9_.refs_6_
  350.8 3.5 sums.13
  355.2 1.4 collective-permute-start.28
  356.6 11.1 %collective-permute-done.29.refs_5_.refs_3_ = bf16[2,1680,128]{2,1,0:T(8,128)(2,1)} collective-permute-done((bf16[2,1680,128]{2,1,0:T(8,128)(2,1)}, bf16[2,1680,128]{2,1,0:T(8,128)(2,1)}, u32[]{:S(2)}, u32[]{:S(2)}) %collective-permute-start.29) | collective-permute-done | bytes 860192 | tf_op jit(solution)/shard_map/ppermute | solution.py:1047
  367.7 2.6 sums.14
  370.2 1.3 collective-permute-start.30
  371.6 1.3 collective-permute-start.31
  373.3 1.8 collective-permute-start.33
  375.1 1.5 collective-permute-start.36
  376.7 2.8 collective-permute-done.30.refs_2_.refs_8_
  379.5 2.3 sums.15
  381.8 1.6 collective-permute-start.32
  383.4 9.0 %collective-permute-done.33.refs_4_ = bf16[1680,128]{1,0:T(8,128)(2,1)} collective-permute-done((bf16[1680,128]{1,0:T(8,128)(2,1)}, bf16[1680,128]{1,0:T(8,128)(2,1)}, u32[]{:S(2)}, u32[]{:S(2)}) %collective-permute-start.33) | collective-permute-done | bytes 430112 | tf_op jit(solution)/shard_map/ppermute | solution.py:1047
  393.5 2.3 sums.16
  395.8 2.0 collective-permute-start.34
  397.8 1.6 collective-permute-start.40
  399.7 3.6 collective-permute-done.34.refs_2_
  403.2 1.7 sums.17
  405.0 2.6 maximum_bitcast_fusion.1
  407.5 1.9 collective-permute-start.37
  409.4 2.3 maximum_bitcast_fusion
  411.7 1.3 collective-permute-done.37
  417.1 6.1 %unpack.1 = (f32[56,4864]{1,0:T(8,128)}, f32[56,4864]{1,0:T(8,128)}, f32[304,896]{1,0:T(8,128)}, f32[56,128]{1,0:T(8,128)}) custom-call(s32[4]{0:T(128)} %pad_add_fusion.2.at_ref.refs_0_, bf16[1680,128]{1,0:T(8,128)(2,1)} %get-tuple-element.179.refs_0_, bf16[1680,128]{1,0:T(8,128)(2,1)} %get-tuple-element.184.refs_1_, ...), custom_call_target="tpu_custom_call" | custom-call | flops 1 | bytes 1 | tf_op jit(solution)/shard_map/unpack/pallas_call | solution.py:978
  (127 shorter events, 34.1 us)
Async XLA Ops:
  7.2 110.8 %all-gather.5.cloned.1.call-start = ((), (), s32[]{:S(2)}) async-start(), calls=%async_computation | async-start | bytes 19288064 | tf_op jit(solution)/shard_map/all_gather | solution.py:1222
  8.9 8.6 %copy-start.2 = (bf16[1,768,896]{2,1,0:T(8,128)(2,1)S(1)}, bf16[1,768,896]{2,1,0:T(8,128)(2,1)}, u32[]{:S(2)}) copy-start(bf16[1,768,896]{2,1,0:T(8,128)(2,1)} %param.11) | copy-start | bytes 4128772
  13.4 6.6 %copy-start.7 = (s32[1,768]{1,0:T(1,128)S(1)}, s32[1,768]{1,0:T(1,128)}, u32[]{:S(2)}) copy-start(s32[1,768]{1,0:T(1,128)} %param.12) | copy-start | bytes 9220
  13.4 175.9 %all-gather.7.cloned.1.call-start = ((), (), s32[]{:S(2)}) async-start(), calls=%async_computation.1 | async-start | bytes 7311360 | tf_op jit(solution)/shard_map/all_gather | solution.py:1224
  13.5 8.0 %collective-permute-start.1 = (bf16[1,32,1152]{2,1,0:T(8,128)(2,1)S(1)}, bf16[1,32,1152]{2,1,0:T(8,128)(2,1)S(1)}, u32[]{:S(2)}, u32[]{:S(2)}) collective-permute-start(bf16[1,32,1152]{2,1,0:T(8,128)(2,1)S(1)} %dynamic-slice_bitcast_fusion), channel_id=1, source_target_pairs={{0,8},{1,9},{2,10},{3,11},{4,12},{5,13},{6,14},{7,15},{8,0},{9,1},... | collective-permute-start | bytes 221192 | tf_op jit(solution)/shard_map/ppermute | solution.py:1047
  18.5 26.8 %collective-permute-start = (bf16[384,896]{1,0:T(8,128)(2,1)}, bf16[384,896]{1,0:T(8,128)(2,1)S(1)}, u32[]{:S(2)}, u32[]{:S(2)}) collective-permute-start(bf16[384,896]{1,0:T(8,128)(2,1)} %slice_bitcast_fusion), channel_id=1, source_target_pairs={{0,16},{16,0},{1,17},{17,1},{2,18},{18,2},{3,19},{19,3},{4,20},{20... | collective-permute-start | bytes 2064392 | tf_op jit(solution)/shard_map/ppermute | solution.py:1050
  20.0 15.7 %collective-permute-start.4 = (s32[1,768]{1,0:T(1,128)S(1)}, s32[1,768]{1,0:T(1,128)S(1)}, u32[]{:S(2)}, u32[]{:S(2)}) collective-permute-start(s32[1,768]{1,0:T(1,128)S(1)} %copy-done.7), channel_id=1, source_target_pairs={{0,16},{16,0},{1,17},{17,1},{2,18},{18,2},{3,19},{19,3},{4,20},{20... | collective-permute-start | bytes 9224 | tf_op jit(solution)/shard_map/ppermute | solution.py:1050
  21.5 8.2 %collective-permute-start.2 = (bf16[2,1,32,1152]{3,2,1,0:T(8,128)(2,1)S(1)}, bf16[2,1,32,1152]{3,2,1,0:T(8,128)(2,1)S(1)}, u32[]{:S(2)}, u32[]{:S(2)}) collective-permute-start(bf16[2,1,32,1152]{3,2,1,0:T(8,128)(2,1)S(1)} %pad_maximum_fusion.10), channel_id=1, source_target_pairs={{0,4},{1,5},{2,6},{3,7},{4,0},{5,1},{6,2},{7,3},{8,12},{9,13},{10,... | collective-permute-start | bytes 442376 | tf_op jit(solution)/shard_map/ppermute | solution.py:1047
  29.8 16.8 %collective-permute-start.3 = (bf16[4,32,1152]{2,1,0:T(8,128)(2,1)S(1)}, bf16[4,32,1152]{2,1,0:T(8,128)(2,1)S(1)}, u32[]{:S(2)}, u32[]{:S(2)}) collective-permute-start(bf16[4,32,1152]{2,1,0:T(8,128)(2,1)S(1)} %bitcast.72), channel_id=1, source_target_pairs={{0,2},{1,3},{2,0},{3,1},{4,6},{5,7},{6,4},{7,5},{8,10},{9,11},{10,... | collective-permute-start | bytes 884744 | tf_op jit(solution)/shard_map/ppermute | solution.py:1047
  46.7 14.0 %collective-permute-start.5 = (bf16[4,2,32,1152]{3,2,0,1:T(8,128)(2,1)S(1)}, bf16[4,2,32,1152]{3,2,0,1:T(8,128)(2,1)S(1)}, u32[]{:S(2)}, u32[]{:S(2)}) collective-permute-start(bf16[4,2,32,1152]{3,2,0,1:T(8,128)(2,1)S(1)} %pad_maximum_fusion.5), channel_id=1, source_target_pairs={{0,16},{16,0},{1,17},{17,1},{2,18},{18,2},{3,19},{19,3},{4,20},{20... | collective-permute-start | bytes 1769480 | tf_op jit(solution)/shard_map/ppermute | solution.py:1050
  61.0 3.2 collective-permute-start.6
  68.2 8.4 %copy-start.3 = (bf16[1,768,896]{2,1,0:T(8,128)(2,1)S(1)}, bf16[1,768,896]{2,1,0:T(8,128)(2,1)}, u32[]{:S(2)}) copy-start(bf16[1,768,896]{2,1,0:T(8,128)(2,1)} %param.21) | copy-start | bytes 4128772
  75.0 19.7 %collective-permute-start.7 = (bf16[768,256]{1,0:T(8,128)(2,1)}, bf16[768,256]{1,0:T(8,128)(2,1)S(1)}, u32[]{:S(2)}, u32[]{:S(2)}) collective-permute-start(bf16[768,256]{1,0:T(8,128)(2,1)} %get-tuple-element.106.kv_ref.refs_7_), channel_id=1, source_target_pairs={{0,16},{16,0},{1,17},{17,1},{2,18},{18,2},{3,19},{19,3},{4,20},{20... | collective-permute-start | bytes 1179656 | tf_op jit(solution)/shard_map/ppermute | solution.py:1050
  77.5 23.6 %collective-permute-start.8 = (bf16[384,896]{1,0:T(8,128)(2,1)}, bf16[384,896]{1,0:T(8,128)(2,1)}, u32[]{:S(2)}, u32[]{:S(2)}) collective-permute-start(bf16[384,896]{1,0:T(8,128)(2,1)} %slice.76), channel_id=1, source_target_pairs={{0,16},{16,0},{1,17},{17,1},{2,18},{18,2},{3,19},{19,3},{4,20},{20... | collective-permute-start | bytes 2064392 | tf_op jit(solution)/shard_map/ppermute | solution.py:1050
  94.8 7.6 %copy-start.1 = (bf16[768,256]{1,0:T(8,128)(2,1)}, bf16[768,256]{1,0:T(8,128)(2,1)S(1)}, u32[]{:S(2)}) copy-start(bf16[768,256]{1,0:T(8,128)(2,1)S(1)} %collective-permute-done.7.kv_ref.refs_6_) | copy-start | bytes 1179652
  102.5 13.7 %copy-start = (bf16[768,896]{1,0:T(8,128)(2,1)}, bf16[768,896]{1,0:T(8,128)(2,1)S(1)}, u32[]{:S(2)}) copy-start(bf16[768,896]{1,0:T(8,128)(2,1)S(1)} %pad_maximum_fusion.3.gnear_ref.refs_10_) | copy-start | bytes 4128772
  102.5 24.0 %collective-permute-start.10 = (bf16[768,896]{1,0:T(8,128)(2,1)S(1)}, bf16[768,896]{1,0:T(8,128)(2,1)}, u32[]{:S(2)}, u32[]{:S(2)}) collective-permute-start(bf16[768,896]{1,0:T(8,128)(2,1)S(1)} %pad_maximum_fusion.3.gnear_ref.refs_10_), channel_id=1, source_target_pairs={{0,1},{1,0},{2,3},{3,2},{4,5},{5,4},{6,7},{7,6},{8,9},{9,8},{10,11... | collective-permute-start | bytes 4128776 | tf_op jit(solution)/shard_map/ppermute | solution.py:1047
  125.7 7.4 %collective-permute-start.9 = (bf16[768,896]{1,0:T(8,128)(2,1)}, bf16[768,896]{1,0:T(8,128)(2,1)}, u32[]{:S(2)}, u32[]{:S(2)}) collective-permute-start(bf16[768,896]{1,0:T(8,128)(2,1)} %get-tuple-element.119.near_ref), channel_id=1, source_target_pairs={{0,1},{1,0},{2,3},{3,2},{4,5},{5,4},{6,7},{7,6},{8,9},{9,8},{10,11... | collective-permute-start | bytes 4128776 | tf_op jit(solution)/shard_map/ppermute | solution.py:1047
  129.1 54.3 %collective-permute-start.11 = (bf16[16,336,128]{2,1,0:T(8,128)(2,1)}, bf16[16,336,128]{2,1,0:T(8,128)(2,1)}, u32[]{:S(2)}, u32[]{:S(2)}) collective-permute-start(bf16[16,336,128]{2,1,0:T(8,128)(2,1)} %constant_dynamic-slice_fusion.2), channel_id=1, source_target_pairs={{0,16},{16,0},{1,17},{17,1},{2,18},{18,2},{3,19},{19,3},{4,20},{20... | collective-permute-start | bytes 4128776 | tf_op jit(solution)/shard_map/ppermute | solution.py:1050
  183.4 61.9 %collective-permute-start.12 = (bf16[1536,896]{1,0:T(8,128)(2,1)}, bf16[1536,896]{1,0:T(8,128)(2,1)}, u32[]{:S(2)}, u32[]{:S(2)}) collective-permute-start(bf16[1536,896]{1,0:T(8,128)(2,1)} %get-tuple-element.127), channel_id=1, source_target_pairs={{0,1},{1,0},{2,3},{3,2},{4,5},{5,4},{6,7},{7,6},{8,9},{9,8},{10,11... | collective-permute-start | bytes 8257544 | tf_op jit(solution)/shard_map/ppermute | solution.py:1047
  183.5 56.2 %collective-permute-start.14 = (bf16[2,4,672,128]{3,2,1,0:T(8,128)(2,1)}, bf16[2,4,672,128]{3,2,1,0:T(8,128)(2,1)}, u32[]{:S(2)}, u32[]{:S(2)}) collective-permute-start(bf16[2,4,672,128]{3,2,1,0:T(8,128)(2,1)} %get-tuple-element.132), channel_id=1, source_target_pairs={{0,2},{1,3},{2,0},{3,1},{4,6},{5,7},{6,4},{7,5},{8,10},{9,11},{10,... | collective-permute-start | bytes 4128776 | tf_op jit(solution)/shard_map/ppermute | solution.py:1047
  184.8 54.9 %collective-permute-start.15 = (bf16[2,4,1008,128]{3,2,1,0:T(8,128)(2,1)}, bf16[2,4,1008,128]{3,2,1,0:T(8,128)(2,1)}, u32[]{:S(2)}, u32[]{:S(2)}) collective-permute-start(bf16[2,4,1008,128]{3,2,1,0:T(8,128)(2,1)} %get-tuple-element.134), channel_id=1, source_target_pairs={{0,16},{16,0},{1,17},{17,1},{2,18},{18,2},{3,19},{19,3},{4,20},{20... | collective-permute-start | bytes 6193160 | tf_op jit(solution)/shard_map/ppermute | solution.py:1050
  239.6 5.7 %collective-permute-start.13 = (bf16[1536,896]{1,0:T(8,128)(2,1)}, bf16[1536,896]{1,0:T(8,128)(2,1)}, u32[]{:S(2)}, u32[]{:S(2)}) collective-permute-start(bf16[1536,896]{1,0:T(8,128)(2,1)} %get-tuple-element.128), channel_id=1, source_target_pairs={{0,1},{1,0},{2,3},{3,2},{4,5},{5,4},{6,7},{7,6},{8,9},{9,8},{10,11... | collective-permute-start | bytes 8257544 | tf_op jit(solution)/shard_map/ppermute | solution.py:1047
  243.0 31.7 %collective-permute-start.17 = (bf16[4,1008,128]{2,1,0:T(8,128)(2,1)}, bf16[4,1008,128]{2,1,0:T(8,128)(2,1)}, u32[]{:S(2)}, u32[]{:S(2)}) collective-permute-start(bf16[4,1008,128]{2,1,0:T(8,128)(2,1)} %get-tuple-element.136.refs_14_), channel_id=1, source_target_pairs={{0,2},{1,3},{2,0},{3,1},{4,6},{5,7},{6,4},{7,5},{8,10},{9,11},{10,... | collective-permute-start | bytes 3096584 | tf_op jit(solution)/shard_map/ppermute | solution.py:1047
  243.9 30.8 %collective-permute-start.16 = (bf16[4,672,128]{2,1,0:T(8,128)(2,1)}, bf16[4,672,128]{2,1,0:T(8,128)(2,1)}, u32[]{:S(2)}, u32[]{:S(2)}) collective-permute-start(bf16[4,672,128]{2,1,0:T(8,128)(2,1)} %get-tuple-element.135.refs_13_), channel_id=1, source_target_pairs={{0,16},{16,0},{1,17},{17,1},{2,18},{18,2},{3,19},{19,3},{4,20},{20... | collective-permute-start | bytes 2064392 | tf_op jit(solution)/shard_map/ppermute | solution.py:1050
  255.4 59.0 %collective-permute-start.20 = (bf16[2,4,1008,128]{3,2,1,0:T(8,128)(2,1)}, bf16[2,4,1008,128]{3,2,1,0:T(8,128)(2,1)}, u32[]{:S(2)}, u32[]{:S(2)}) collective-permute-start(bf16[2,4,1008,128]{3,2,1,0:T(8,128)(2,1)} %get-tuple-element.153), channel_id=1, source_target_pairs={{0,16},{16,0},{1,17},{17,1},{2,18},{18,2},{3,19},{19,3},{4,20},{20... | collective-permute-start | bytes 6193160 | tf_op jit(solution)/shard_map/ppermute | solution.py:1050
  274.0 40.5 %collective-permute-start.19 = (bf16[2,4,672,128]{3,2,1,0:T(8,128)(2,1)}, bf16[2,4,672,128]{3,2,1,0:T(8,128)(2,1)}, u32[]{:S(2)}, u32[]{:S(2)}) collective-permute-start(bf16[2,4,672,128]{3,2,1,0:T(8,128)(2,1)} %get-tuple-element.151), channel_id=1, source_target_pairs={{0,2},{1,3},{2,0},{3,1},{4,6},{5,7},{6,4},{7,5},{8,10},{9,11},{10,... | collective-permute-start | bytes 4128776 | tf_op jit(solution)/shard_map/ppermute | solution.py:1047
  279.4 35.0 %collective-permute-start.21 = (bf16[2,1680,128]{2,1,0:T(8,128)(2,1)}, bf16[2,1680,128]{2,1,0:T(8,128)(2,1)}, u32[]{:S(2)}, u32[]{:S(2)}) collective-permute-start(bf16[2,1680,128]{2,1,0:T(8,128)(2,1)} %get-tuple-element.145.refs_10_), channel_id=1, source_target_pairs={{0,4},{1,5},{2,6},{3,7},{4,0},{5,1},{6,2},{7,3},{8,12},{9,13},{10,... | collective-permute-start | bytes 2580488 | tf_op jit(solution)/shard_map/ppermute | solution.py:1047
  280.6 33.8 %collective-permute-start.18 = (bf16[768,256]{1,0:T(8,128)(2,1)}, bf16[768,256]{1,0:T(8,128)(2,1)}, u32[]{:S(2)}, u32[]{:S(2)}) collective-permute-start(bf16[768,256]{1,0:T(8,128)(2,1)} %get-tuple-element.148), channel_id=1, source_target_pairs={{0,16},{16,0},{1,17},{17,1},{2,18},{18,2},{3,19},{19,3},{4,20},{20... | collective-permute-start | bytes 1179656 | tf_op jit(solution)/shard_map/ppermute | solution.py:1050
  318.2 24.4 %collective-permute-start.24 = (bf16[4,1008,128]{2,1,0:T(8,128)(2,1)}, bf16[4,1008,128]{2,1,0:T(8,128)(2,1)}, u32[]{:S(2)}, u32[]{:S(2)}) collective-permute-start(bf16[4,1008,128]{2,1,0:T(8,128)(2,1)} %get-tuple-element.157.refs_10_), channel_id=1, source_target_pairs={{0,2},{1,3},{2,0},{3,1},{4,6},{5,7},{6,4},{7,5},{8,10},{9,11},{10,... | collective-permute-start | bytes 3096584 | tf_op jit(solution)/shard_map/ppermute | solution.py:1047
  319.3 22.6 %collective-permute-start.23 = (bf16[4,672,128]{2,1,0:T(8,128)(2,1)}, bf16[4,672,128]{2,1,0:T(8,128)(2,1)}, u32[]{:S(2)}, u32[]{:S(2)}) collective-permute-start(bf16[4,672,128]{2,1,0:T(8,128)(2,1)} %get-tuple-element.156.refs_9_), channel_id=1, source_target_pairs={{0,16},{16,0},{1,17},{17,1},{2,18},{18,2},{3,19},{19,3},{4,20},{20... | collective-permute-start | bytes 2064392 | tf_op jit(solution)/shard_map/ppermute | solution.py:1050
  320.8 21.1 %collective-permute-start.25 = (bf16[1680,128]{1,0:T(8,128)(2,1)}, bf16[1680,128]{1,0:T(8,128)(2,1)}, u32[]{:S(2)}, u32[]{:S(2)}) collective-permute-start(bf16[1680,128]{1,0:T(8,128)(2,1)} %get-tuple-element.158.refs_11_), channel_id=1, source_target_pairs={{0,8},{1,9},{2,10},{3,11},{4,12},{5,13},{6,14},{7,15},{8,0},{9,1},... | collective-permute-start | bytes 1290248 | tf_op jit(solution)/shard_map/ppermute | solution.py:1047
  330.4 20.4 %collective-permute-start.22 = (bf16[2,2,4,480,128]{4,3,2,1,0:T(8,128)(2,1)}, bf16[2,2,4,480,128]{4,3,2,1,0:T(8,128)(2,1)}, u32[]{:S(2)}, u32[]{:S(2)}) collective-permute-start(bf16[2,2,4,480,128]{4,3,2,1,0:T(8,128)(2,1)} %get-tuple-element.160), channel_id=1, source_target_pairs={{0,1},{1,0},{2,3},{3,2},{4,5},{5,4},{6,7},{7,6},{8,9},{9,8},{10,11... | collective-permute-start | bytes 5898248 | tf_op jit(solution)/shard_map/ppermute | solution.py:1047
  330.4 20.4 %collective-permute-start.26 = (bf16[384,896]{1,0:T(8,128)(2,1)}, bf16[384,896]{1,0:T(8,128)(2,1)}, u32[]{:S(2)}, u32[]{:S(2)}) collective-permute-start(bf16[384,896]{1,0:T(8,128)(2,1)} %get-tuple-element.165), channel_id=1, source_target_pairs={{0,16},{16,0},{1,17},{17,1},{2,18},{18,2},{3,19},{19,3},{4,20},{20... | collective-permute-start | bytes 2064392 | tf_op jit(solution)/shard_map/ppermute | solution.py:1050
  347.7 19.9 %collective-permute-start.29 = (bf16[2,1680,128]{2,1,0:T(8,128)(2,1)}, bf16[2,1680,128]{2,1,0:T(8,128)(2,1)}, u32[]{:S(2)}, u32[]{:S(2)}) collective-permute-start(bf16[2,1680,128]{2,1,0:T(8,128)(2,1)} %get-tuple-element.164.refs_8_), channel_id=1, source_target_pairs={{0,4},{1,5},{2,6},{3,7},{4,0},{5,1},{6,2},{7,3},{8,12},{9,13},{10,... | collective-permute-start | bytes 2580488 | tf_op jit(solution)/shard_map/ppermute | solution.py:1047
  354.3 13.4 %collective-permute-start.27 = (bf16[2,4,240,128]{3,2,1,0:T(8,128)(2,1)}, bf16[2,4,240,128]{3,2,1,0:T(8,128)(2,1)}, u32[]{:S(2)}, u32[]{:S(2)}) collective-permute-start(bf16[2,4,240,128]{3,2,1,0:T(8,128)(2,1)} %get-tuple-element.167), channel_id=1, source_target_pairs={{0,2},{1,3},{2,0},{3,1},{4,6},{5,7},{6,4},{7,5},{8,10},{9,11},{10,... | collective-permute-start | bytes 1474568 | tf_op jit(solution)/shard_map/ppermute | solution.py:1047
  355.2 12.5 %collective-permute-start.28 = (bf16[2,4,240,128]{3,2,1,0:T(8,128)(2,1)}, bf16[2,4,240,128]{3,2,1,0:T(8,128)(2,1)}, u32[]{:S(2)}, u32[]{:S(2)}) collective-permute-start(bf16[2,4,240,128]{3,2,1,0:T(8,128)(2,1)} %get-tuple-element.169), channel_id=1, source_target_pairs={{0,16},{16,0},{1,17},{17,1},{2,18},{18,2},{3,19},{19,3},{4,20},{20... | collective-permute-start | bytes 1474568 | tf_op jit(solution)/shard_map/ppermute | solution.py:1050
  370.2 9.2 %collective-permute-start.30 = (bf16[4,240,128]{2,1,0:T(8,128)(2,1)}, bf16[4,240,128]{2,1,0:T(8,128)(2,1)}, u32[]{:S(2)}, u32[]{:S(2)}) collective-permute-start(bf16[4,240,128]{2,1,0:T(8,128)(2,1)} %get-tuple-element.172), channel_id=1, source_target_pairs={{0,16},{16,0},{1,17},{17,1},{2,18},{18,2},{3,19},{19,3},{4,20},{20... | collective-permute-start | bytes 737288 | tf_op jit(solution)/shard_map/ppermute | solution.py:1050
  371.6 7.9 %collective-permute-start.31 = (bf16[4,240,128]{2,1,0:T(8,128)(2,1)}, bf16[4,240,128]{2,1,0:T(8,128)(2,1)}, u32[]{:S(2)}, u32[]{:S(2)}) collective-permute-start(bf16[4,240,128]{2,1,0:T(8,128)(2,1)} %get-tuple-element.173), channel_id=1, source_target_pairs={{0,2},{1,3},{2,0},{3,1},{4,6},{5,7},{6,4},{7,5},{8,10},{9,11},{10,... | collective-permute-start | bytes 737288 | tf_op jit(solution)/shard_map/ppermute | solution.py:1047
  372.8 26.6 %collective-permute-start.35 = (bf16[1680,128]{1,0:T(8,128)(2,1)}, bf16[1680,128]{1,0:T(8,128)(2,1)}, u32[]{:S(2)}, u32[]{:S(2)}) collective-permute-start(bf16[1680,128]{1,0:T(8,128)(2,1)} %get-tuple-element.179.refs_0_), channel_id=1, source_target_pairs={{0,16},{16,0},{1,17},{17,1},{2,18},{18,2},{3,19},{19,3},{4,20},{20... | collective-permute-start | bytes 1290248 | tf_op jit(solution)/shard_map/ppermute | solution.py:1050
  373.3 19.0 %collective-permute-start.33 = (bf16[1680,128]{1,0:T(8,128)(2,1)}, bf16[1680,128]{1,0:T(8,128)(2,1)}, u32[]{:S(2)}, u32[]{:S(2)}) collective-permute-start(bf16[1680,128]{1,0:T(8,128)(2,1)} %get-tuple-element.174.refs_12_), channel_id=1, source_target_pairs={{0,8},{1,9},{2,10},{3,11},{4,12},{5,13},{6,14},{7,15},{8,0},{9,1},... | collective-permute-start | bytes 1290248 | tf_op jit(solution)/shard_map/ppermute | solution.py:1047
  375.1 28.1 %collective-permute-start.36 = (bf16[384,896]{1,0:T(8,128)(2,1)}, bf16[384,896]{1,0:T(8,128)(2,1)}, u32[]{:S(2)}, u32[]{:S(2)}) collective-permute-start(bf16[384,896]{1,0:T(8,128)(2,1)} %get-tuple-element.180), channel_id=1, source_target_pairs={{0,16},{16,0},{1,17},{17,1},{2,18},{18,2},{3,19},{19,3},{4,20},{20... | collective-permute-start | bytes 2064392 | tf_op jit(solution)/shard_map/ppermute | solution.py:1050
  381.8 11.7 %collective-permute-start.32 = (bf16[2,480,128]{2,1,0:T(8,128)(2,1)}, bf16[2,480,128]{2,1,0:T(8,128)(2,1)}, u32[]{:S(2)}, u32[]{:S(2)}) collective-permute-start(bf16[2,480,128]{2,1,0:T(8,128)(2,1)} %get-tuple-element.176), channel_id=1, source_target_pairs={{0,4},{1,5},{2,6},{3,7},{4,0},{5,1},{6,2},{7,3},{8,12},{9,13},{10,... | collective-permute-start | bytes 737288 | tf_op jit(solution)/shard_map/ppermute | solution.py:1047
  395.8 7.4 %collective-permute-start.34 = (bf16[480,128]{1,0:T(8,128)(2,1)}, bf16[480,128]{1,0:T(8,128)(2,1)}, u32[]{:S(2)}, u32[]{:S(2)}) collective-permute-start(bf16[480,128]{1,0:T(8,128)(2,1)} %get-tuple-element.177), channel_id=1, source_target_pairs={{0,8},{1,9},{2,10},{3,11},{4,12},{5,13},{6,14},{7,15},{8,0},{9,1},... | collective-permute-start | bytes 368648 | tf_op jit(solution)/shard_map/ppermute | solution.py:1047
  397.8 18.5 %collective-permute-start.38 = (bf16[1680,128]{1,0:T(8,128)(2,1)}, bf16[1680,128]{1,0:T(8,128)(2,1)}, u32[]{:S(2)}, u32[]{:S(2)}) collective-permute-start(bf16[1680,128]{1,0:T(8,128)(2,1)} %get-tuple-element.179.refs_0_), channel_id=1, source_target_pairs={{0,1},{1,0},{2,3},{3,2},{4,5},{5,4},{6,7},{7,6},{8,9},{9,8},{10,11... | collective-permute-start | bytes 1290248 | tf_op jit(solution)/shard_map/ppermute | solution.py:1047
  397.8 17.2 %collective-permute-start.40 = (bf16[1680,128]{1,0:T(8,128)(2,1)}, bf16[1680,128]{1,0:T(8,128)(2,1)}, u32[]{:S(2)}, u32[]{:S(2)}) collective-permute-start(bf16[1680,128]{1,0:T(8,128)(2,1)} %get-tuple-element.178.refs_3_.refs_4_), channel_id=1, source_target_pairs={{0,16},{16,0},{1,17},{17,1},{2,18},{18,2},{3,19},{19,3},{4,20},{20... | collective-permute-start | bytes 1290248 | tf_op jit(solution)/shard_map/ppermute | solution.py:1050
  399.4 16.9 %collective-permute-start.41 = (bf16[1680,128]{1,0:T(8,128)(2,1)}, bf16[1680,128]{1,0:T(8,128)(2,1)}, u32[]{:S(2)}, u32[]{:S(2)}) collective-permute-start(bf16[1680,128]{1,0:T(8,128)(2,1)} %get-tuple-element.178.refs_3_.refs_4_), channel_id=1, source_target_pairs={{0,1},{1,0},{2,3},{3,2},{4,5},{5,4},{6,7},{7,6},{8,9},{9,8},{10,11... | collective-permute-start | bytes 1290248 | tf_op jit(solution)/shard_map/ppermute | solution.py:1047
  405.0 2.6 copy-start.6
  405.0 4.5 %copy-start.4 = (bf16[384,896]{1,0:T(8,128)(2,1)S(1)}, bf16[384,896]{1,0:T(8,128)(2,1)}, u32[]{:S(2)}) copy-start(bf16[384,896]{1,0:T(8,128)(2,1)} %get-tuple-element.141) | copy-start | bytes 2064388
  407.5 5.5 %collective-permute-start.37 = (bf16[480,128]{1,0:T(8,128)(2,1)S(1)}, bf16[480,128]{1,0:T(8,128)(2,1)S(1)}, u32[]{:S(2)}, u32[]{:S(2)}) collective-permute-start(bf16[480,128]{1,0:T(8,128)(2,1)S(1)} %copy-done.6), channel_id=1, source_target_pairs={{0,16},{16,0},{1,17},{17,1},{2,18},{18,2},{3,19},{19,3},{4,20},{20... | collective-permute-start | bytes 368648 | tf_op jit(solution)/shard_map/ppermute | solution.py:1050
  409.4 6.9 %collective-permute-start.39 = (bf16[1680,128]{1,0:T(8,128)(2,1)}, bf16[1680,128]{1,0:T(8,128)(2,1)}, u32[]{:S(2)}, u32[]{:S(2)}) collective-permute-start(bf16[1680,128]{1,0:T(8,128)(2,1)} %get-tuple-element.184.refs_1_), channel_id=1, source_target_pairs={{0,1},{1,0},{2,3},{3,2},{4,5},{5,4},{6,7},{7,6},{8,9},{9,8},{10,11... | collective-permute-start | bytes 1290248 | tf_op jit(solution)/shard_map/ppermute | solution.py:1047
  411.7 3.3 copy-start.5
  413.0 2.8 copy-start.8
  415.0 2.1 collective-permute-start.42
Sparse Core Ops, SparseCore 0:
  13.5 104.3 all-gather.4
  120.7 68.5 all-gather.6

commit v2 on v1

--- a/solution.py
+++ b/solution.py
@@ -19,6 +19,7 @@
 
 LIGHT = pl.CostEstimate(flops=1, bytes_accessed=1, transcendentals=0)
 MIDDLE = pl.CostEstimate(flops=8 * 10**9, bytes_accessed=MIB, transcendentals=0)
+SHORT = pl.CostEstimate(flops=69 * 10**8, bytes_accessed=MIB, transcendentals=0)
 HEAVY = pl.CostEstimate(flops=6 * 10**10, bytes_accessed=16 * MIB, transcendentals=0)
 
 bf16 = jnp.bfloat16
@@ -564,7 +565,7 @@
         ),
         out_shape=[jax.ShapeDtypeStruct((rows, width), bf16)] * 2,
         compiler_params=pltpu.CompilerParams(vmem_limit_bytes=64 * MIB - 65536),
-        cost_estimate=LIGHT,
+        cost_estimate=SHORT,
         name="input_grad",
     )(half, x, gain, project, weight, grad_middle, *others)
 
@@ -1329,11 +1330,10 @@
     )
     others = ()
     if small_mesh:
-        *sent_two, sent_one, sent_result = sums(
-            sum_two.second(1) + sum_one.fourth(1), 1, (query_grad, got_kv), through=(sent_result,)
-        )
+        (sent_one,) = sums(sum_one.fourth(), 1, (query_grad,))
+        sum_one.fourth_sent(sent_one)
+        *sent_two, sent_result = sums(sum_two.second(), 1, (sent_one, got_kv), through=(sent_result,))
         sum_two.second_sent(*sent_two)
-        sum_one.fourth_sent(sent_one)
         others = (*sum_two.sent, *sum_one.sent)
     got_result = wires.other_half(sent_result)
     project, mine, theirs, bias_grad = weight_grads(
@@ -1345,19 +1345,22 @@
     cut = blocks // 4 * full_depth
     if small_mesh:
         theirs = wires.flip(theirs, 1)
-        kept_grad, sent_grad = input_grad(half, tokens, gain_one, project, qkv_full, grad_middle, ())
-        sent_two, kept_two, sent_one = sums(sum_two.third() + sum_one.fifth(3), 3, (kept_grad,), HEAVY)
+        (sent_one,) = sums(sum_one.fifth(), 1, (project,))
+        sum_one.fifth_sent(sent_one)
+        kept_grad, sent_grad = input_grad(half, tokens, gain_one, project, qkv_full, grad_middle, (sent_one,))
+        first, later = sum_two.third()
+        (sent_two,) = sums([first], 3, (kept_grad,), HEAVY)
+
+        def small_groups(part, grid):
+            for axis in range(2):
+                block, place = [2, 2, 4, (cut + 16) // grid, LANES], [0, 0, 0, axis, 0]
+                block[axis], place[axis] = None, part
+                yield [[(array, tuple(block), tuple(place)) for array in (mine, theirs)]]
+
+        send_x, send_y = sums(list(small_groups(1, 1)), 1, (sent_two, got_result))
+        keep_x, keep_y, kept_two = sums([*small_groups(0, 3), later], 3, (send_x, send_y))
+        small = ChipSum(wires, keep_x, send_x, keep_y, send_y, 1)
         sum_two.third_sent(sent_two, kept_two)
-        sum_one.fifth_sent(sent_one)
-        groups_of = []
-        for axis in range(2):
-            block = [2, 2, 4, cut + 16, LANES]
-            block[axis] = None
-            for part in (0, 1):
-                place = [0, 0, 0, axis, 0]
-                place[axis] = part
-                groups_of.append([[(array, tuple(block), tuple(place)) for array in (mine, theirs)]])
-        small = ChipSum(wires, *sums(groups_of, 1, (*sum_two.sent, got_result)), 1)
         *sent, sent_two, sent_grad = sums(small.second() + sum_two.fourth(), 1, (), LIGHT, (sent_grad,))
         small.second_sent(*sent)
         sum_two.fourth_sent(sent_two)

time: 439 us -> 437 us (level)
  waiting for transfers between devices: 79.1 us -> 71.5 us
  Pallas kernels: 254 us -> 259 us
    pallas_call x9 -> x12, Pallas kernels: 29.3 us -> 35 us  [sums(): pl.pallas_call(dropping(functools.partial(sums_kernel, plan=plan), len(ar...]
    ppermute x25, waiting for transfers between devices: 41.7 us -> 36.6 us  [flip(): lax.ppermute(values_in, 'fsdp', [(i, i ^ bit) for i in range(self.shards)])]
  transfers between devices with their start and end apart: 45 -> 45, of which waited for: 19 -> 19; matrix products, arithmetic and copies ran while one was open for 7% -> 7% of each run, Pallas kernels for 55% -> 57%
where the time goes in v2:
time: 437 us; the launch traced here: 431 us
  Pallas kernels  259 us (59%)
  waiting for transfers between devices  71.5 us (16%)
  starting transfers between devices  46.5 us (11%)
  other arithmetic  25.7 us (6%)
  between operations  17.5 us (4%)
  local copies, waits for them, and re-layouts  10.2 us (2%)
    pallas_call x2, Pallas kernels, mlp_call(): pl.pallas_call(functools.partial(mlp_kernel, counts=counts, tiles=tiles,...  101 us
    ppermute x25, waiting for transfers between devices, flip(): lax.ppermute(values_in, 'fsdp', [(i, i ^ bit) for i in range(self.shards)])  36.6 us
    pallas_call x12, Pallas kernels, sums(): pl.pallas_call(dropping(functools.partial(sums_kernel, plan=plan), len(ar...  35 us
    ppermute x18, waiting for transfers between devices, other_half(): return lax.ppermute(values_in, 'seq', [(0, 1), (1, 0)])  33 us
    pallas_call x1, Pallas kernels, near_backward(): pl.pallas_call(functools.partial(dropping(near_backward_kernel, 10, len(o...  25.5 us
    ppermute x18, starting transfers between devices, other_half(): return lax.ppermute(values_in, 'seq', [(0, 1), (1, 0)])  24 us
    ppermute x25, starting transfers between devices, flip(): lax.ppermute(values_in, 'fsdp', [(i, i ^ bit) for i in range(self.shards)])  22.3 us
    pallas_call x1, Pallas kernels, far_backward(): pl.pallas_call(functools.partial(dropping(dropping(far_backward_kernel, 1...  17.1 us
  transfers between devices with their start and end apart: 45, of which 19 were waited for; matrix products, arithmetic and copies ran while one was open for 7% of the time, Pallas kernels for 57%

profile of v2, /device:TPU:0, one launch (start us, length us, event | category | flops | bytes accessed | tf_op | source)
XLA Modules:
  0.0 430.6 jit_solution(9799920498849662030)
XLA Ops:
  8.9 4.4 %pack.1 = (bf16[4432,128]{1,0:T(8,128)(2,1)}, bf16[1680,128]{1,0:T(8,128)(2,1)}) custom-call(s32[1]{0:T(128)} %bitcast.half_ref.refs_0_, bf16[56,4864]{1,0:T(8,128)(2,1)} %refs_8_, bf16[56,4864]{1,0:T(8,128)(2,1)} %refs_9_, bf16[304,896]{1,0:T(8,128)(2,1)} %down_ref, bf16[56,896]{1,0:T(8,128)(2,1)} %out_ref), custom_call_target="tpu_custom_call" | custom-call | flops 1 | bytes 1 | tf_op jit(solution)/shard_map/pack/pallas_call | solution.py:886
  13.5 4.1 collective-permute-start.1
  18.5 1.5 collective-permute-start
  22.3 7.4 %collective-permute-done.2 = bf16[2,1,32,1152]{3,2,1,0:T(8,128)(2,1)S(1)} collective-permute-done((bf16[2,1,32,1152]{3,2,1,0:T(8,128)(2,1)S(1)}, bf16[2,1,32,1152]{3,2,1,0:T(8,128)(2,1)S(1)}, u32[]{:S(2)}, u32[]{:S(2)}) %collective-permute-start.2) | collective-permute-done | bytes 147488 | tf_op jit(solution)/shard_map/ppermute | solution.py:1048
  29.8 1.6 collective-permute-start.3
  31.4 4.3 collective-permute-done.4
  39.0 1.4 fusion.6
  46.7 1.6 collective-permute-start.5
  48.3 12.5 %collective-permute-done.5 = bf16[4,2,32,1152]{3,2,0,1:T(8,128)(2,1)S(1)} collective-permute-done((bf16[4,2,32,1152]{3,2,0,1:T(8,128)(2,1)S(1)}, bf16[4,2,32,1152]{3,2,0,1:T(8,128)(2,1)S(1)}, u32[]{:S(2)}, u32[]{:S(2)}) %collective-permute-start.5) | collective-permute-done | bytes 589856 | tf_op jit(solution)/shard_map/ppermute | solution.py:1051
  61.2 3.1 collective-permute-done.6
  65.3 1.5 slice.87
  68.2 6.8 %project.1 = (bf16[768,896]{1,0:T(8,128)(2,1)}, bf16[768,896]{1,0:T(8,128)(2,1)}, bf16[768,256]{1,0:T(8,128)(2,1)}) custom-call(bf16[768,896]{1,0:T(8,128)(2,1)} %pad_maximum_fusion.2.x_ref.refs_1_, f32[1,896]{1,0:T(1,128)} %reshape.163.gain_ref.refs_2_, bf16[896,1152]{1,0:T(8,128)(2,1)} %bitcast.65, f32[1,1152]{1,0:T(1,128)} %reshape.164.bias_ref, ...), custom_call_target="tpu_custom_call" | custom-call | flops 1 | bytes 1 | tf_op jit(solution)/shard_map/project/pallas_call | solution.py:77
  75.0 1.6 collective-permute-start.7
  78.0 16.8 %attention_near.1 = (f32[768,896]{1,0:T(8,128)}, f32[768,128]{1,0:T(8,128)}) custom-call(bf16[768,896]{1,0:T(8,128)(2,1)} %get-tuple-element.102.q_ref.refs_1_.refs_0_, bf16[768,128]{1,0:T(8,128)(2,1)} %select_convert_fusion.qx_ref.refs_2_.refs_1_, bf16[768,256]{1,0:T(8,128)(2,1)} %get-tuple-element.103.kv_ref.refs_7_, bf16[768,128]{1,0:T(8,128)(2,1)} %fusion.1.kx_ref.refs_8_), custom_call_target="tpu_custom_call" | custom-call | flops 60000002048 | bytes 16777216 | tf_op jit(solution)/shard_map/attention_near/pallas_call | solution.py:218
  94.8 6.4 %collective-permute-done.8 = bf16[384,896]{1,0:T(8,128)(2,1)} collective-permute-done((bf16[384,896]{1,0:T(8,128)(2,1)}, bf16[384,896]{1,0:T(8,128)(2,1)}, u32[]{:S(2)}, u32[]{:S(2)}) %collective-permute-start.8) | collective-permute-done | bytes 688160 | tf_op jit(solution)/shard_map/ppermute | solution.py:1051
  103.5 12.8 %attention_far.1 = (bf16[768,896]{1,0:T(8,128)(2,1)}, f32[128,768]{1,0:T(8,128)}) custom-call(s32[1]{0:T(128)} %bitcast.half_ref.refs_0_, bf16[768,896]{1,0:T(8,128)(2,1)} %get-tuple-element.102.q_ref.refs_1_.refs_0_, bf16[768,128]{1,0:T(8,128)(2,1)} %select_convert_fusion.qx_ref.refs_2_.refs_1_, bf16[768,256]{1,0:T(8,128)(2,1)} %copy-done.1, ...), custom_call_target="tpu_custom_call" | custom-call | flops 1 | bytes 1 | tf_op jit(solution)/shard_map/attention_far/pallas_call | solution.py:239
  116.3 1.7 all-gather.5.cloned.1.call-done
  117.9 7.7 %out_project.1 = (f32[768,896]{1,0:T(8,128)}, bf16[768,896]{1,0:T(8,128)(2,1)}, bf16[896,896]{1,0:T(8,128)(2,1)}) custom-call(bf16[768,896]{1,0:T(8,128)(2,1)} %pad_maximum_fusion.2.x_ref.refs_1_, bf16[768,896]{1,0:T(8,128)(2,1)} %get-tuple-element.110.att_ref.refs_4_.refs_3_.refs_8_, f32[1,896]{1,0:T(1,128)} %reshape.165.gain_ref.refs_11_, ...), custom_call_target="tpu_custom_call" | custom-call | flops 1 | bytes 1 | tf_op jit(solution)/shard_map/out_project/pallas_call | solution.py:603
  126.6 2.5 constant_dynamic-slice_fusion.2
  129.1 4.0 collective-permute-start.11
  133.1 50.3 %feed_forward.2 = (bf16[1536,896]{1,0:T(8,128)(2,1)}, bf16[1536,896]{1,0:T(8,128)(2,1)}, bf16[2,4,672,128]{3,2,1,0:T(8,128)(2,1)}, bf16[2,4,672,128]{3,2,1,0:T(8...) custom-call(s32[4]{0:T(128)} %pad_add_fusion.2.at_ref.refs_0_, ...), custom_call_target="tpu_custom_call" | custom-call | flops 60000002048 | bytes 16777216 | tf_op jit(solution)/shard_map/feed_forward/pallas_call | solution.py:786
  183.5 1.3 collective-permute-start.14
  185.0 2.3 broadcast_select_fusion.1
  187.3 1.7 pad_maximum_fusion.rest_0_
  189.3 50.3 %feed_forward.3 = (bf16[1536,896]{1,0:T(8,128)(2,1)}, bf16[1536,896]{1,0:T(8,128)(2,1)}, bf16[2,4,672,128]{3,2,1,0:T(8,128)(2,1)}, bf16[2,4,672,128]{3,2,1,0:T(8...) custom-call(s32[4]{0:T(128)} %pad_add_fusion.2.at_ref.refs_0_, ...), custom_call_target="tpu_custom_call" | custom-call | flops 60000002048 | bytes 16777216 | tf_op jit(solution)/shard_map/feed_forward/pallas_call | solution.py:786
  239.7 3.3 sums.12
  243.9 1.4 collective-permute-start.16
  245.3 10.1 %middle_back.1 = (bf16[384,896]{1,0:T(8,128)(2,1)}, bf16[384,896]{1,0:T(8,128)(2,1)}, f32[768,896]{1,0:T(8,128)}, bf16[768,896]{1,0:T(8,128)(2,1)}, bf16[768,896...) custom-call(s32[1]{0:T(128)} %bitcast.half_ref.refs_0_, ...), custom_call_target="tpu_custom_call", output_to_operand_aliasing={{5}: (15, {}), {6}: (16, {}), {7}: (17, {}), {8}: (18, {})} | custom-call | flops 1 | bytes 1 | tf_op jit(solution)/shard_map/middle_back/pallas_call | solution.py:652
  255.4 1.5 collective-permute-start.20
  256.8 17.1 %attention_far_back.1 = (f32[896,768]{1,0:T(8,128)}, bf16[768,256]{1,0:T(8,128)(2,1)}) custom-call(s32[1]{0:T(128)} %bitcast.half_ref.refs_0_, bf16[768,896]{1,0:T(8,128)(2,1)} %get-tuple-element.102.q_ref.refs_1_.refs_0_, bf16[768,128]{1,0:T(8,128)(2,1)} %select_convert_fusion.qx_ref.refs_2_.refs_1_, bf16[768,896]{1,0:T(8,128)(2,1)} %get-tuple-element.140.refs_3_.refs_2_, ...), custom_call_target="tpu_custom_call" | custom-call | flops 1 | bytes 1 | tf_op jit(solution)/shard_map/attention_far_back/pallas_call | solution.py:397
  274.7 4.7 %sums.13 = (bf16[2,1680,128]{2,1,0:T(8,128)(2,1)}, bf16[2,1680,128]{2,1,0:T(8,128)(2,1)}) custom-call(bf16[2,4,672,128]{3,2,1,0:T(8,128)(2,1)} %get-tuple-element.128.refs_0_.refs_6_, bf16[2,4,672,128]{3,2,1,0:T(8,128)(2,1)} %collective-permute-done.14.refs_1_.refs_7_, bf16[4,672,128]{2,1,0:T(8,128)(2,1)} %collective-permute-done.16.refs_2_.refs_8_, ...), custom_call_target="tpu_custom_call" | custom-call | flops 8000000000 | bytes 1048576 | tf_op jit(solution)/shard_map/sums/pallas_call | solution.py:1110
  280.6 1.8 collective-permute-start.18
  282.3 25.5 %attention_near_back.1 = (bf16[768,896]{1,0:T(8,128)(2,1)}, f32[768,256]{1,0:T(8,128)}) custom-call(bf16[768,896]{1,0:T(8,128)(2,1)} %get-tuple-element.102.q_ref.refs_1_.refs_0_, bf16[768,128]{1,0:T(8,128)(2,1)} %select_convert_fusion.qx_ref.refs_2_.refs_1_, bf16[768,896]{1,0:T(8,128)(2,1)} %get-tuple-element.140.refs_3_.refs_2_, ...), custom_call_target="tpu_custom_call" | custom-call | flops 1 | bytes 1 | tf_op jit(solution)/shard_map/attention_near_back/pallas_call | solution.py:432
  307.9 2.0 sums.14.refs_4_.refs_11_
  309.9 2.2 collective-permute-start.25
  312.1 2.3 collective-permute-done.18.refs_5_.refs_4_
  314.4 3.3 sums.15
  318.8 1.5 collective-permute-start.23
  320.4 9.3 %weight_grads.1 = (bf16[768,1152]{1,0:T(8,128)(2,1)}, bf16[2,2,4,480,128]{4,3,2,1,0:T(8,128)(2,1)}, bf16[2,2,4,480,128]{4,3,2,1,0:T(8,128)(2,1)}, f32[1,1152]{1,0:T(1,128)}) custom-call(s32[4]{0:T(128)} %pad_add_fusion.2.at_ref.refs_0_, bf16[768,896]{1,0:T(8,128)(2,1)} %get-tuple-element.139.refs_1_, bf16[768,896]{1,0:T(8,128)(2,1)} %get-tuple-element.143.refs_2_, ...), custom_call_target="tpu_custom_call" | custom-call | flops 1 | bytes 1 | tf_op jit(solution)/shard_map/weight_grads/pallas_call | solution.py:519
  330.9 2.2 sums.16.refs_6_.refs_0_
  333.1 7.0 %input_grad.1 = (bf16[384,896]{1,0:T(8,128)(2,1)}, bf16[384,896]{1,0:T(8,128)(2,1)}) custom-call(s32[1]{0:T(128)} %bitcast.half_ref.refs_0_, bf16[768,896]{1,0:T(8,128)(2,1)} %pad_maximum_fusion.2.x_ref.refs_1_, f32[1,896]{1,0:T(1,128)} %reshape.163.gain_ref.refs_2_, bf16[768,1152]{1,0:T(8,128)(2,1)} %get-tuple-element.157.refs_3_, ...), custom_call_target="tpu_custom_call" | custom-call | flops 6899999744 | bytes 1048576 | tf_op jit(solution)/shard_map/input_grad/pallas_call | solution.py:557
  340.1 2.0 collective-permute-done.24.refs_5_.refs_9_
  342.1 3.6 sums.17.refs_4_
  347.0 3.3 collective-permute-done.26.refs_5_.refs_6_
  350.3 2.5 sums.18
  353.8 1.4 collective-permute-start.28
  355.2 4.5 %sums.19 = (bf16[2,4,240,128]{3,2,1,0:T(8,128)(2,1)}, bf16[2,4,240,128]{3,2,1,0:T(8,128)(2,1)}, bf16[2,1680,128]{2,1,0:T(8,128)(2,1)}) custom-call(bf16[2,2,4,480,128]{4,3,2,1,0:T(8,128)(2,1)} %get-tuple-element.155.refs_0_.refs_2_, bf16[2,2,4,480,128]{4,3,2,1,0:T(8,128)(2,1)} %collective-permute-done.22.refs_1_.refs_3_, ...), custom_call_target="tpu_custom_call" | custom-call | flops 1 | bytes 1 | tf_op jit(solution)/shard_map/sums/pallas_call | solution.py:1110
  359.7 5.8 %collective-permute-done.29.refs_5_.refs_3_ = bf16[2,1680,128]{2,1,0:T(8,128)(2,1)} collective-permute-done((bf16[2,1680,128]{2,1,0:T(8,128)(2,1)}, bf16[2,1680,128]{2,1,0:T(8,128)(2,1)}, u32[]{:S(2)}, u32[]{:S(2)}) %collective-permute-start.29) | collective-permute-done | bytes 860192 | tf_op jit(solution)/shard_map/ppermute | solution.py:1048
  365.5 2.6 sums.20
  368.1 1.4 collective-permute-start.30
  371.2 1.8 collective-permute-start.33
  373.0 1.5 collective-permute-start.36
  374.6 2.7 collective-permute-done.30.refs_2_.refs_8_
  377.3 2.3 sums.21
  380.9 9.4 %collective-permute-done.33.refs_4_ = bf16[1680,128]{1,0:T(8,128)(2,1)} collective-permute-done((bf16[1680,128]{1,0:T(8,128)(2,1)}, bf16[1680,128]{1,0:T(8,128)(2,1)}, u32[]{:S(2)}, u32[]{:S(2)}) %collective-permute-start.33) | collective-permute-done | bytes 430112 | tf_op jit(solution)/shard_map/ppermute | solution.py:1048
  390.3 1.9 collective-permute-done.32.refs_1_
  392.2 2.3 sums.22
  395.6 1.5 collective-permute-start.40
  397.4 4.6 %collective-permute-done.34.refs_2_ = bf16[480,128]{1,0:T(8,128)(2,1)} collective-permute-done((bf16[480,128]{1,0:T(8,128)(2,1)}, bf16[480,128]{1,0:T(8,128)(2,1)}, u32[]{:S(2)}, u32[]{:S(2)}) %collective-permute-start.34) | collective-permute-done | bytes 122912 | tf_op jit(solution)/shard_map/ppermute | solution.py:1048
  401.9 1.7 sums.23
  403.7 2.6 maximum_bitcast_fusion.1
  407.3 2.3 maximum_bitcast_fusion
  409.6 1.5 collective-permute-done.37
  415.2 6.1 %unpack.1 = (f32[56,4864]{1,0:T(8,128)}, f32[56,4864]{1,0:T(8,128)}, f32[304,896]{1,0:T(8,128)}, f32[56,128]{1,0:T(8,128)}) custom-call(s32[4]{0:T(128)} %pad_add_fusion.2.at_ref.refs_0_, bf16[1680,128]{1,0:T(8,128)(2,1)} %sums.16.refs_6_.refs_0_, bf16[1680,128]{1,0:T(8,128)(2,1)} %get-tuple-element.178.refs_1_, ...), custom_call_target="tpu_custom_call" | custom-call | flops 1 | bytes 1 | tf_op jit(solution)/shard_map/unpack/pallas_call | solution.py:979
  (130 shorter events, 39.0 us)
Async XLA Ops:
  7.2 110.8 %all-gather.5.cloned.1.call-start = ((), (), s32[]{:S(2)}) async-start(), calls=%async_computation | async-start | bytes 19288064 | tf_op jit(solution)/shard_map/all_gather | solution.py:1223
  8.9 8.6 %copy-start.2 = (bf16[1,768,896]{2,1,0:T(8,128)(2,1)S(1)}, bf16[1,768,896]{2,1,0:T(8,128)(2,1)}, u32[]{:S(2)}) copy-start(bf16[1,768,896]{2,1,0:T(8,128)(2,1)} %param.11) | copy-start | bytes 4128772
  13.4 6.6 %copy-start.7 = (s32[1,768]{1,0:T(1,128)S(1)}, s32[1,768]{1,0:T(1,128)}, u32[]{:S(2)}) copy-start(s32[1,768]{1,0:T(1,128)} %param.12) | copy-start | bytes 9220
  13.4 175.9 %all-gather.7.cloned.1.call-start = ((), (), s32[]{:S(2)}) async-start(), calls=%async_computation.1 | async-start | bytes 7311360 | tf_op jit(solution)/shard_map/all_gather | solution.py:1225
  13.5 8.0 %collective-permute-start.1 = (bf16[1,32,1152]{2,1,0:T(8,128)(2,1)S(1)}, bf16[1,32,1152]{2,1,0:T(8,128)(2,1)S(1)}, u32[]{:S(2)}, u32[]{:S(2)}) collective-permute-start(bf16[1,32,1152]{2,1,0:T(8,128)(2,1)S(1)} %dynamic-slice_bitcast_fusion), channel_id=1, source_target_pairs={{0,8},{1,9},{2,10},{3,11},{4,12},{5,13},{6,14},{7,15},{8,0},{9,1},... | collective-permute-start | bytes 221192 | tf_op jit(solution)/shard_map/ppermute | solution.py:1048
  18.5 26.8 %collective-permute-start = (bf16[384,896]{1,0:T(8,128)(2,1)}, bf16[384,896]{1,0:T(8,128)(2,1)S(1)}, u32[]{:S(2)}, u32[]{:S(2)}) collective-permute-start(bf16[384,896]{1,0:T(8,128)(2,1)} %slice_bitcast_fusion), channel_id=1, source_target_pairs={{0,16},{16,0},{1,17},{17,1},{2,18},{18,2},{3,19},{19,3},{4,20},{20... | collective-permute-start | bytes 2064392 | tf_op jit(solution)/shard_map/ppermute | solution.py:1051
  20.0 15.7 %collective-permute-start.4 = (s32[1,768]{1,0:T(1,128)S(1)}, s32[1,768]{1,0:T(1,128)S(1)}, u32[]{:S(2)}, u32[]{:S(2)}) collective-permute-start(s32[1,768]{1,0:T(1,128)S(1)} %copy-done.7), channel_id=1, source_target_pairs={{0,16},{16,0},{1,17},{17,1},{2,18},{18,2},{3,19},{19,3},{4,20},{20... | collective-permute-start | bytes 9224 | tf_op jit(solution)/shard_map/ppermute | solution.py:1051
  21.5 8.2 %collective-permute-start.2 = (bf16[2,1,32,1152]{3,2,1,0:T(8,128)(2,1)S(1)}, bf16[2,1,32,1152]{3,2,1,0:T(8,128)(2,1)S(1)}, u32[]{:S(2)}, u32[]{:S(2)}) collective-permute-start(bf16[2,1,32,1152]{3,2,1,0:T(8,128)(2,1)S(1)} %pad_maximum_fusion.10), channel_id=1, source_target_pairs={{0,4},{1,5},{2,6},{3,7},{4,0},{5,1},{6,2},{7,3},{8,12},{9,13},{10,... | collective-permute-start | bytes 442376 | tf_op jit(solution)/shard_map/ppermute | solution.py:1048
  29.8 16.8 %collective-permute-start.3 = (bf16[4,32,1152]{2,1,0:T(8,128)(2,1)S(1)}, bf16[4,32,1152]{2,1,0:T(8,128)(2,1)S(1)}, u32[]{:S(2)}, u32[]{:S(2)}) collective-permute-start(bf16[4,32,1152]{2,1,0:T(8,128)(2,1)S(1)} %bitcast.72), channel_id=1, source_target_pairs={{0,2},{1,3},{2,0},{3,1},{4,6},{5,7},{6,4},{7,5},{8,10},{9,11},{10,... | collective-permute-start | bytes 884744 | tf_op jit(solution)/shard_map/ppermute | solution.py:1048
  46.7 14.0 %collective-permute-start.5 = (bf16[4,2,32,1152]{3,2,0,1:T(8,128)(2,1)S(1)}, bf16[4,2,32,1152]{3,2,0,1:T(8,128)(2,1)S(1)}, u32[]{:S(2)}, u32[]{:S(2)}) collective-permute-start(bf16[4,2,32,1152]{3,2,0,1:T(8,128)(2,1)S(1)} %pad_maximum_fusion.5), channel_id=1, source_target_pairs={{0,16},{16,0},{1,17},{17,1},{2,18},{18,2},{3,19},{19,3},{4,20},{20... | collective-permute-start | bytes 1769480 | tf_op jit(solution)/shard_map/ppermute | solution.py:1051
  61.0 3.2 collective-permute-start.6
  68.2 8.4 %copy-start.3 = (bf16[1,768,896]{2,1,0:T(8,128)(2,1)S(1)}, bf16[1,768,896]{2,1,0:T(8,128)(2,1)}, u32[]{:S(2)}) copy-start(bf16[1,768,896]{2,1,0:T(8,128)(2,1)} %param.21) | copy-start | bytes 4128772
  75.0 19.7 %collective-permute-start.7 = (bf16[768,256]{1,0:T(8,128)(2,1)}, bf16[768,256]{1,0:T(8,128)(2,1)S(1)}, u32[]{:S(2)}, u32[]{:S(2)}) collective-permute-start(bf16[768,256]{1,0:T(8,128)(2,1)} %get-tuple-element.103.kv_ref.refs_7_), channel_id=1, source_target_pairs={{0,16},{16,0},{1,17},{17,1},{2,18},{18,2},{3,19},{19,3},{4,20},{20... | collective-permute-start | bytes 1179656 | tf_op jit(solution)/shard_map/ppermute | solution.py:1051
  77.5 23.6 %collective-permute-start.8 = (bf16[384,896]{1,0:T(8,128)(2,1)}, bf16[384,896]{1,0:T(8,128)(2,1)}, u32[]{:S(2)}, u32[]{:S(2)}) collective-permute-start(bf16[384,896]{1,0:T(8,128)(2,1)} %slice.76), channel_id=1, source_target_pairs={{0,16},{16,0},{1,17},{17,1},{2,18},{18,2},{3,19},{19,3},{4,20},{20... | collective-permute-start | bytes 2064392 | tf_op jit(solution)/shard_map/ppermute | solution.py:1051
  94.8 7.6 %copy-start.1 = (bf16[768,256]{1,0:T(8,128)(2,1)}, bf16[768,256]{1,0:T(8,128)(2,1)S(1)}, u32[]{:S(2)}) copy-start(bf16[768,256]{1,0:T(8,128)(2,1)S(1)} %collective-permute-done.7.kv_ref.refs_6_) | copy-start | bytes 1179652
  102.5 13.7 %copy-start = (bf16[768,896]{1,0:T(8,128)(2,1)}, bf16[768,896]{1,0:T(8,128)(2,1)S(1)}, u32[]{:S(2)}) copy-start(bf16[768,896]{1,0:T(8,128)(2,1)S(1)} %pad_maximum_fusion.3.gnear_ref.refs_10_) | copy-start | bytes 4128772
  102.5 24.0 %collective-permute-start.10 = (bf16[768,896]{1,0:T(8,128)(2,1)S(1)}, bf16[768,896]{1,0:T(8,128)(2,1)}, u32[]{:S(2)}, u32[]{:S(2)}) collective-permute-start(bf16[768,896]{1,0:T(8,128)(2,1)S(1)} %pad_maximum_fusion.3.gnear_ref.refs_10_), channel_id=1, source_target_pairs={{0,1},{1,0},{2,3},{3,2},{4,5},{5,4},{6,7},{7,6},{8,9},{9,8},{10,11... | collective-permute-start | bytes 4128776 | tf_op jit(solution)/shard_map/ppermute | solution.py:1048
  125.7 7.4 %collective-permute-start.9 = (bf16[768,896]{1,0:T(8,128)(2,1)}, bf16[768,896]{1,0:T(8,128)(2,1)}, u32[]{:S(2)}, u32[]{:S(2)}) collective-permute-start(bf16[768,896]{1,0:T(8,128)(2,1)} %get-tuple-element.116.near_ref), channel_id=1, source_target_pairs={{0,1},{1,0},{2,3},{3,2},{4,5},{5,4},{6,7},{7,6},{8,9},{9,8},{10,11... | collective-permute-start | bytes 4128776 | tf_op jit(solution)/shard_map/ppermute | solution.py:1048
  129.1 54.3 %collective-permute-start.11 = (bf16[16,336,128]{2,1,0:T(8,128)(2,1)}, bf16[16,336,128]{2,1,0:T(8,128)(2,1)}, u32[]{:S(2)}, u32[]{:S(2)}) collective-permute-start(bf16[16,336,128]{2,1,0:T(8,128)(2,1)} %constant_dynamic-slice_fusion.2), channel_id=1, source_target_pairs={{0,16},{16,0},{1,17},{17,1},{2,18},{18,2},{3,19},{19,3},{4,20},{20... | collective-permute-start | bytes 4128776 | tf_op jit(solution)/shard_map/ppermute | solution.py:1051
  183.4 61.9 %collective-permute-start.12 = (bf16[1536,896]{1,0:T(8,128)(2,1)}, bf16[1536,896]{1,0:T(8,128)(2,1)}, u32[]{:S(2)}, u32[]{:S(2)}) collective-permute-start(bf16[1536,896]{1,0:T(8,128)(2,1)} %get-tuple-element.124), channel_id=1, source_target_pairs={{0,1},{1,0},{2,3},{3,2},{4,5},{5,4},{6,7},{7,6},{8,9},{9,8},{10,11... | collective-permute-start | bytes 8257544 | tf_op jit(solution)/shard_map/ppermute | solution.py:1048
  183.5 56.2 %collective-permute-start.14 = (bf16[2,4,672,128]{3,2,1,0:T(8,128)(2,1)}, bf16[2,4,672,128]{3,2,1,0:T(8,128)(2,1)}, u32[]{:S(2)}, u32[]{:S(2)}) collective-permute-start(bf16[2,4,672,128]{3,2,1,0:T(8,128)(2,1)} %get-tuple-element.129), channel_id=1, source_target_pairs={{0,2},{1,3},{2,0},{3,1},{4,6},{5,7},{6,4},{7,5},{8,10},{9,11},{10,... | collective-permute-start | bytes 4128776 | tf_op jit(solution)/shard_map/ppermute | solution.py:1048
  184.8 54.9 %collective-permute-start.15 = (bf16[2,4,1008,128]{3,2,1,0:T(8,128)(2,1)}, bf16[2,4,1008,128]{3,2,1,0:T(8,128)(2,1)}, u32[]{:S(2)}, u32[]{:S(2)}) collective-permute-start(bf16[2,4,1008,128]{3,2,1,0:T(8,128)(2,1)} %get-tuple-element.131), channel_id=1, source_target_pairs={{0,16},{16,0},{1,17},{17,1},{2,18},{18,2},{3,19},{19,3},{4,20},{20... | collective-permute-start | bytes 6193160 | tf_op jit(solution)/shard_map/ppermute | solution.py:1051
  239.6 5.7 %collective-permute-start.13 = (bf16[1536,896]{1,0:T(8,128)(2,1)}, bf16[1536,896]{1,0:T(8,128)(2,1)}, u32[]{:S(2)}, u32[]{:S(2)}) collective-permute-start(bf16[1536,896]{1,0:T(8,128)(2,1)} %get-tuple-element.125), channel_id=1, source_target_pairs={{0,1},{1,0},{2,3},{3,2},{4,5},{5,4},{6,7},{7,6},{8,9},{9,8},{10,11... | collective-permute-start | bytes 8257544 | tf_op jit(solution)/shard_map/ppermute | solution.py:1048
  243.0 31.7 %collective-permute-start.17 = (bf16[4,1008,128]{2,1,0:T(8,128)(2,1)}, bf16[4,1008,128]{2,1,0:T(8,128)(2,1)}, u32[]{:S(2)}, u32[]{:S(2)}) collective-permute-start(bf16[4,1008,128]{2,1,0:T(8,128)(2,1)} %get-tuple-element.133.refs_14_), channel_id=1, source_target_pairs={{0,2},{1,3},{2,0},{3,1},{4,6},{5,7},{6,4},{7,5},{8,10},{9,11},{10,... | collective-permute-start | bytes 3096584 | tf_op jit(solution)/shard_map/ppermute | solution.py:1048
  243.9 30.8 %collective-permute-start.16 = (bf16[4,672,128]{2,1,0:T(8,128)(2,1)}, bf16[4,672,128]{2,1,0:T(8,128)(2,1)}, u32[]{:S(2)}, u32[]{:S(2)}) collective-permute-start(bf16[4,672,128]{2,1,0:T(8,128)(2,1)} %get-tuple-element.132.refs_13_), channel_id=1, source_target_pairs={{0,16},{16,0},{1,17},{17,1},{2,18},{18,2},{3,19},{19,3},{4,20},{20... | collective-permute-start | bytes 2064392 | tf_op jit(solution)/shard_map/ppermute | solution.py:1051
  255.4 59.0 %collective-permute-start.20 = (bf16[2,4,1008,128]{3,2,1,0:T(8,128)(2,1)}, bf16[2,4,1008,128]{3,2,1,0:T(8,128)(2,1)}, u32[]{:S(2)}, u32[]{:S(2)}) collective-permute-start(bf16[2,4,1008,128]{3,2,1,0:T(8,128)(2,1)} %get-tuple-element.150), channel_id=1, source_target_pairs={{0,16},{16,0},{1,17},{17,1},{2,18},{18,2},{3,19},{19,3},{4,20},{20... | collective-permute-start | bytes 6193160 | tf_op jit(solution)/shard_map/ppermute | solution.py:1051
  273.9 40.5 %collective-permute-start.19 = (bf16[2,4,672,128]{3,2,1,0:T(8,128)(2,1)}, bf16[2,4,672,128]{3,2,1,0:T(8,128)(2,1)}, u32[]{:S(2)}, u32[]{:S(2)}) collective-permute-start(bf16[2,4,672,128]{3,2,1,0:T(8,128)(2,1)} %get-tuple-element.148), channel_id=1, source_target_pairs={{0,2},{1,3},{2,0},{3,1},{4,6},{5,7},{6,4},{7,5},{8,10},{9,11},{10,... | collective-permute-start | bytes 4128776 | tf_op jit(solution)/shard_map/ppermute | solution.py:1048
  279.4 28.5 %collective-permute-start.21 = (bf16[2,1680,128]{2,1,0:T(8,128)(2,1)}, bf16[2,1680,128]{2,1,0:T(8,128)(2,1)}, u32[]{:S(2)}, u32[]{:S(2)}) collective-permute-start(bf16[2,1680,128]{2,1,0:T(8,128)(2,1)} %get-tuple-element.142.refs_10_), channel_id=1, source_target_pairs={{0,4},{1,5},{2,6},{3,7},{4,0},{5,1},{6,2},{7,3},{8,12},{9,13},{10,... | collective-permute-start | bytes 2580488 | tf_op jit(solution)/shard_map/ppermute | solution.py:1048
  280.6 33.8 %collective-permute-start.18 = (bf16[768,256]{1,0:T(8,128)(2,1)}, bf16[768,256]{1,0:T(8,128)(2,1)}, u32[]{:S(2)}, u32[]{:S(2)}) collective-permute-start(bf16[768,256]{1,0:T(8,128)(2,1)} %get-tuple-element.145), channel_id=1, source_target_pairs={{0,16},{16,0},{1,17},{17,1},{2,18},{18,2},{3,19},{19,3},{4,20},{20... | collective-permute-start | bytes 1179656 | tf_op jit(solution)/shard_map/ppermute | solution.py:1051
  309.9 21.0 %collective-permute-start.25 = (bf16[1680,128]{1,0:T(8,128)(2,1)}, bf16[1680,128]{1,0:T(8,128)(2,1)}, u32[]{:S(2)}, u32[]{:S(2)}) collective-permute-start(bf16[1680,128]{1,0:T(8,128)(2,1)} %sums.14.refs_4_.refs_11_), channel_id=1, source_target_pairs={{0,8},{1,9},{2,10},{3,11},{4,12},{5,13},{6,14},{7,15},{8,0},{9,1},... | collective-permute-start | bytes 1290248 | tf_op jit(solution)/shard_map/ppermute | solution.py:1048
  317.7 24.4 %collective-permute-start.24 = (bf16[4,1008,128]{2,1,0:T(8,128)(2,1)}, bf16[4,1008,128]{2,1,0:T(8,128)(2,1)}, u32[]{:S(2)}, u32[]{:S(2)}) collective-permute-start(bf16[4,1008,128]{2,1,0:T(8,128)(2,1)} %get-tuple-element.154.refs_10_), channel_id=1, source_target_pairs={{0,2},{1,3},{2,0},{3,1},{4,6},{5,7},{6,4},{7,5},{8,10},{9,11},{10,... | collective-permute-start | bytes 3096584 | tf_op jit(solution)/shard_map/ppermute | solution.py:1048
  318.8 21.3 %collective-permute-start.23 = (bf16[4,672,128]{2,1,0:T(8,128)(2,1)}, bf16[4,672,128]{2,1,0:T(8,128)(2,1)}, u32[]{:S(2)}, u32[]{:S(2)}) collective-permute-start(bf16[4,672,128]{2,1,0:T(8,128)(2,1)} %get-tuple-element.153.refs_9_), channel_id=1, source_target_pairs={{0,16},{16,0},{1,17},{17,1},{2,18},{18,2},{3,19},{19,3},{4,20},{20... | collective-permute-start | bytes 2064392 | tf_op jit(solution)/shard_map/ppermute | solution.py:1051
  329.7 20.6 %collective-permute-start.22 = (bf16[2,2,4,480,128]{4,3,2,1,0:T(8,128)(2,1)}, bf16[2,2,4,480,128]{4,3,2,1,0:T(8,128)(2,1)}, u32[]{:S(2)}, u32[]{:S(2)}) collective-permute-start(bf16[2,2,4,480,128]{4,3,2,1,0:T(8,128)(2,1)} %get-tuple-element.156), channel_id=1, source_target_pairs={{0,1},{1,0},{2,3},{3,2},{4,5},{5,4},{6,7},{7,6},{8,9},{9,8},{10,11... | collective-permute-start | bytes 5898248 | tf_op jit(solution)/shard_map/ppermute | solution.py:1048
  329.7 20.6 %collective-permute-start.26 = (bf16[384,896]{1,0:T(8,128)(2,1)}, bf16[384,896]{1,0:T(8,128)(2,1)}, u32[]{:S(2)}, u32[]{:S(2)}) collective-permute-start(bf16[384,896]{1,0:T(8,128)(2,1)} %get-tuple-element.160), channel_id=1, source_target_pairs={{0,16},{16,0},{1,17},{17,1},{2,18},{18,2},{3,19},{19,3},{4,20},{20... | collective-permute-start | bytes 2064392 | tf_op jit(solution)/shard_map/ppermute | solution.py:1051
  345.7 19.8 %collective-permute-start.29 = (bf16[2,1680,128]{2,1,0:T(8,128)(2,1)}, bf16[2,1680,128]{2,1,0:T(8,128)(2,1)}, u32[]{:S(2)}, u32[]{:S(2)}) collective-permute-start(bf16[2,1680,128]{2,1,0:T(8,128)(2,1)} %sums.17.refs_4_), channel_id=1, source_target_pairs={{0,4},{1,5},{2,6},{3,7},{4,0},{5,1},{6,2},{7,3},{8,12},{9,13},{10,... | collective-permute-start | bytes 2580488 | tf_op jit(solution)/shard_map/ppermute | solution.py:1048
  352.9 12.6 %collective-permute-start.27 = (bf16[2,4,240,128]{3,2,1,0:T(8,128)(2,1)}, bf16[2,4,240,128]{3,2,1,0:T(8,128)(2,1)}, u32[]{:S(2)}, u32[]{:S(2)}) collective-permute-start(bf16[2,4,240,128]{3,2,1,0:T(8,128)(2,1)} %get-tuple-element.161.refs_10_), channel_id=1, source_target_pairs={{0,2},{1,3},{2,0},{3,1},{4,6},{5,7},{6,4},{7,5},{8,10},{9,11},{10,... | collective-permute-start | bytes 1474568 | tf_op jit(solution)/shard_map/ppermute | solution.py:1048
  353.8 11.7 %collective-permute-start.28 = (bf16[2,4,240,128]{3,2,1,0:T(8,128)(2,1)}, bf16[2,4,240,128]{3,2,1,0:T(8,128)(2,1)}, u32[]{:S(2)}, u32[]{:S(2)}) collective-permute-start(bf16[2,4,240,128]{3,2,1,0:T(8,128)(2,1)} %get-tuple-element.162.refs_11_), channel_id=1, source_target_pairs={{0,16},{16,0},{1,17},{17,1},{2,18},{18,2},{3,19},{19,3},{4,20},{20... | collective-permute-start | bytes 1474568 | tf_op jit(solution)/shard_map/ppermute | solution.py:1051
  368.1 9.2 %collective-permute-start.30 = (bf16[4,240,128]{2,1,0:T(8,128)(2,1)}, bf16[4,240,128]{2,1,0:T(8,128)(2,1)}, u32[]{:S(2)}, u32[]{:S(2)}) collective-permute-start(bf16[4,240,128]{2,1,0:T(8,128)(2,1)} %get-tuple-element.167), channel_id=1, source_target_pairs={{0,16},{16,0},{1,17},{17,1},{2,18},{18,2},{3,19},{19,3},{4,20},{20... | collective-permute-start | bytes 737288 | tf_op jit(solution)/shard_map/ppermute | solution.py:1051
  369.5 7.8 %collective-permute-start.31 = (bf16[4,240,128]{2,1,0:T(8,128)(2,1)}, bf16[4,240,128]{2,1,0:T(8,128)(2,1)}, u32[]{:S(2)}, u32[]{:S(2)}) collective-permute-start(bf16[4,240,128]{2,1,0:T(8,128)(2,1)} %get-tuple-element.168), channel_id=1, source_target_pairs={{0,2},{1,3},{2,0},{3,1},{4,6},{5,7},{6,4},{7,5},{8,10},{9,11},{10,... | collective-permute-start | bytes 737288 | tf_op jit(solution)/shard_map/ppermute | solution.py:1048
  370.7 26.4 %collective-permute-start.35 = (bf16[1680,128]{1,0:T(8,128)(2,1)}, bf16[1680,128]{1,0:T(8,128)(2,1)}, u32[]{:S(2)}, u32[]{:S(2)}) collective-permute-start(bf16[1680,128]{1,0:T(8,128)(2,1)} %sums.16.refs_6_.refs_0_), channel_id=1, source_target_pairs={{0,16},{16,0},{1,17},{17,1},{2,18},{18,2},{3,19},{19,3},{4,20},{20... | collective-permute-start | bytes 1290248 | tf_op jit(solution)/shard_map/ppermute | solution.py:1051
  371.2 19.0 %collective-permute-start.33 = (bf16[1680,128]{1,0:T(8,128)(2,1)}, bf16[1680,128]{1,0:T(8,128)(2,1)}, u32[]{:S(2)}, u32[]{:S(2)}) collective-permute-start(bf16[1680,128]{1,0:T(8,128)(2,1)} %get-tuple-element.169.refs_12_), channel_id=1, source_target_pairs={{0,8},{1,9},{2,10},{3,11},{4,12},{5,13},{6,14},{7,15},{8,0},{9,1},... | collective-permute-start | bytes 1290248 | tf_op jit(solution)/shard_map/ppermute | solution.py:1048
  373.0 28.9 %collective-permute-start.36 = (bf16[384,896]{1,0:T(8,128)(2,1)}, bf16[384,896]{1,0:T(8,128)(2,1)}, u32[]{:S(2)}, u32[]{:S(2)}) collective-permute-start(bf16[384,896]{1,0:T(8,128)(2,1)} %get-tuple-element.174), channel_id=1, source_target_pairs={{0,16},{16,0},{1,17},{17,1},{2,18},{18,2},{3,19},{19,3},{4,20},{20... | collective-permute-start | bytes 2064392 | tf_op jit(solution)/shard_map/ppermute | solution.py:1051
  379.6 12.6 %collective-permute-start.32 = (bf16[2,480,128]{2,1,0:T(8,128)(2,1)}, bf16[2,480,128]{2,1,0:T(8,128)(2,1)}, u32[]{:S(2)}, u32[]{:S(2)}) collective-permute-start(bf16[2,480,128]{2,1,0:T(8,128)(2,1)} %get-tuple-element.171), channel_id=1, source_target_pairs={{0,4},{1,5},{2,6},{3,7},{4,0},{5,1},{6,2},{7,3},{8,12},{9,13},{10,... | collective-permute-start | bytes 737288 | tf_op jit(solution)/shard_map/ppermute | solution.py:1048
  394.5 7.4 %collective-permute-start.34 = (bf16[480,128]{1,0:T(8,128)(2,1)}, bf16[480,128]{1,0:T(8,128)(2,1)}, u32[]{:S(2)}, u32[]{:S(2)}) collective-permute-start(bf16[480,128]{1,0:T(8,128)(2,1)} %get-tuple-element.172), channel_id=1, source_target_pairs={{0,8},{1,9},{2,10},{3,11},{4,12},{5,13},{6,14},{7,15},{8,0},{9,1},... | collective-permute-start | bytes 368648 | tf_op jit(solution)/shard_map/ppermute | solution.py:1048
  395.6 18.9 %collective-permute-start.38 = (bf16[1680,128]{1,0:T(8,128)(2,1)}, bf16[1680,128]{1,0:T(8,128)(2,1)}, u32[]{:S(2)}, u32[]{:S(2)}) collective-permute-start(bf16[1680,128]{1,0:T(8,128)(2,1)} %sums.16.refs_6_.refs_0_), channel_id=1, source_target_pairs={{0,1},{1,0},{2,3},{3,2},{4,5},{5,4},{6,7},{7,6},{8,9},{9,8},{10,11... | collective-permute-start | bytes 1290248 | tf_op jit(solution)/shard_map/ppermute | solution.py:1048
  395.6 17.5 %collective-permute-start.40 = (bf16[1680,128]{1,0:T(8,128)(2,1)}, bf16[1680,128]{1,0:T(8,128)(2,1)}, u32[]{:S(2)}, u32[]{:S(2)}) collective-permute-start(bf16[1680,128]{1,0:T(8,128)(2,1)} %get-tuple-element.173.refs_3_.refs_4_), channel_id=1, source_target_pairs={{0,16},{16,0},{1,17},{17,1},{2,18},{18,2},{3,19},{19,3},{4,20},{20... | collective-permute-start | bytes 1290248 | tf_op jit(solution)/shard_map/ppermute | solution.py:1051
  397.1 17.3 %collective-permute-start.41 = (bf16[1680,128]{1,0:T(8,128)(2,1)}, bf16[1680,128]{1,0:T(8,128)(2,1)}, u32[]{:S(2)}, u32[]{:S(2)}) collective-permute-start(bf16[1680,128]{1,0:T(8,128)(2,1)} %get-tuple-element.173.refs_3_.refs_4_), channel_id=1, source_target_pairs={{0,1},{1,0},{2,3},{3,2},{4,5},{5,4},{6,7},{7,6},{8,9},{9,8},{10,11... | collective-permute-start | bytes 1290248 | tf_op jit(solution)/shard_map/ppermute | solution.py:1048
  403.7 2.6 copy-start.6
  403.7 3.7 copy-start.4
  406.2 4.9 %collective-permute-start.37 = (bf16[480,128]{1,0:T(8,128)(2,1)S(1)}, bf16[480,128]{1,0:T(8,128)(2,1)S(1)}, u32[]{:S(2)}, u32[]{:S(2)}) collective-permute-start(bf16[480,128]{1,0:T(8,128)(2,1)S(1)} %copy-done.6), channel_id=1, source_target_pairs={{0,16},{16,0},{1,17},{17,1},{2,18},{18,2},{3,19},{19,3},{4,20},{20... | collective-permute-start | bytes 368648 | tf_op jit(solution)/shard_map/ppermute | solution.py:1051
  407.3 7.2 %collective-permute-start.39 = (bf16[1680,128]{1,0:T(8,128)(2,1)}, bf16[1680,128]{1,0:T(8,128)(2,1)}, u32[]{:S(2)}, u32[]{:S(2)}) collective-permute-start(bf16[1680,128]{1,0:T(8,128)(2,1)} %get-tuple-element.178.refs_1_), channel_id=1, source_target_pairs={{0,1},{1,0},{2,3},{3,2},{4,5},{5,4},{6,7},{7,6},{8,9},{9,8},{10,11... | collective-permute-start | bytes 1290248 | tf_op jit(solution)/shard_map/ppermute | solution.py:1048
  409.6 3.5 copy-start.5
  411.1 2.8 copy-start.8
  413.1 2.1 collective-permute-start.42
Sparse Core Ops, SparseCore 0:
  13.5 104.3 all-gather.4
  120.7 68.5 all-gather.6
